TPU v7x, 32 devices: a whole 2x2x4 slice. The times are simulated.
32 devices in a mesh: lead: 2 (over x), gy: 4 (over y, core), gx: 4 (over z).
Axes of the slice: x: 2, y: 2, z: 4, core: 2. Of those that a mesh axis runs over, the one named last changes fastest.
Arguments:
- inputs: bfloat16 [2, 256, 32, 256], P('lead', 'gy', 'gx'), may hold values from -6 to 6
- lead_ids: int32 [2], P('lead'), may hold values from 0 to 359
- film: float32 [360, 4, 256], replicated, may hold values from -3 to 3
- flat_weights: bfloat16 [2, 589824], P(None, ('lead', 'gy', 'gx')), may hold values from -0.25 to 0.25
- cotangent: bfloat16 [2, 256, 32, 256], P('lead', 'gy', 'gx'), may hold values from -6 to 6
Outputs:
- outputs: bfloat16 [2, 256, 32, 256], P('lead', 'gy', 'gx')
- weight_grad: float32 [589824], P(('lead', 'gy', 'gx'))
All inputs are finite; a program needn't handle non-finite values.
Results may differ from a plain program's by a relative error of at most 0.0047.
Values may be sent and summed in bfloat16 or wider, within the bound.
No kernel may reach another device: no remote copies, remote signals or barrier semaphores. Data moves between devices by JAX's collectives and lax.ppermute only.
A program may use at most 64 MiB of HBM per device.

v0:
```python
import math

import jax
import jax.numpy as jnp
from jax import lax
from jax.sharding import PartitionSpec as P

FIRST_DILATION = 64
SECOND_DILATION = 128


def passed_along(value, axis, steps):
    count = lax.axis_size(axis)
    leading, last = (max(0, -steps), min(count, count - steps))
    return lax.ppermute(value, axis, [(source, source + steps) for source in range(leading, last)])


def shortened(array):
    return jax.tree.map(lambda a: a.astype(jnp.bfloat16) if a.dtype == jnp.float32 else a, array)


def adjacent_cells(weather_field, row_step, col_step):
    row_list = [-1, 0, 1]
    col_list = [-1, 0, 1] if col_step < lax.axis_size("gx") else [0]
    taps = []
    stacked = jnp.stack(
        [
            (
                weather_field
                if row_off == 0
                else passed_along(weather_field, "gy", -row_off * row_step)
            )
            for row_off in row_list
        ]
    )
    columns = [
        (
            stacked
            if col_off == 0
            else passed_along(shortened(stacked), "gx", -col_off * col_step).astype(stacked.dtype)
        )
        for col_off in col_list
    ]
    for col_off in col_list:
        for row_off in row_list:
            taps.append(
                (row_off, col_off, columns[col_list.index(col_off)][row_list.index(row_off)])
            )
    return taps


def lower(taps, weight_four, flipped):
    patch_width = weight_four.shape[-1]
    cols = jnp.concatenate(
        [piece.reshape(-1, patch_width) for row_off, col_off, piece in taps], axis=1
    )
    blocks = []
    for row_off, col_off, piece in taps:
        if flipped:
            blocks.append(weight_four[1 - row_off, 1 - col_off].T)
        else:
            blocks.append(weight_four[row_off + 1, col_off + 1])
    return (cols, jnp.concatenate(blocks, axis=0))


def shards(inputs, lead_ids, film, flat_weights, cotangent):
    tile_row_count, tile_column_count, patch_width = (
        inputs.shape[1],
        inputs.shape[2],
        inputs.shape[3],
    )
    gathered = lax.all_gather(flat_weights, ("lead", "gy", "gx"), axis=1, tiled=True)
    weight_a = gathered[0].reshape(3, 3, patch_width, patch_width)
    weight_b = gathered[1].reshape(3, 3, patch_width, patch_width)
    table_rows = film.shape[0]
    picker = (jnp.arange(table_rows, dtype=jnp.int32) == lead_ids[0]).astype(jnp.float32)
    film_row = jnp.dot(
        picker, film.reshape(table_rows, -1), precision=lax.Precision.HIGHEST
    ).reshape(4, patch_width)
    mult_a = 1.0 + film_row[0]
    shift_a = film_row[1]
    mult_b = 1.0 + film_row[2]
    shift_b = film_row[3]
    weather_field = inputs[0]
    input_kernel_taps = adjacent_cells(
        weather_field, FIRST_DILATION // tile_row_count, FIRST_DILATION // tile_column_count
    )
    input_columns, matrix_a = lower(input_kernel_taps, weight_a, False)
    pre_a = jnp.dot(input_columns, matrix_a, preferred_element_type=jnp.float32) * mult_a + shift_a
    sig_a = jax.nn.sigmoid(pre_a)
    hidden_state = (
        weather_field.reshape(-1, patch_width).astype(jnp.float32) + pre_a * sig_a
    ).astype(jnp.bfloat16)
    taps_hidden = adjacent_cells(
        hidden_state.reshape(tile_row_count, tile_column_count, patch_width),
        SECOND_DILATION // tile_row_count,
        SECOND_DILATION // tile_column_count,
    )
    hidden_columns, matrix_b = lower(taps_hidden, weight_b, False)
    pre_b = jnp.dot(hidden_columns, matrix_b, preferred_element_type=jnp.float32) * mult_b + shift_b
    sig_b = jax.nn.sigmoid(pre_b)
    outputs = (hidden_state.astype(jnp.float32) + pre_b * sig_b).astype(jnp.bfloat16)
    upstream = cotangent[0].reshape(-1, patch_width).astype(jnp.float32)
    second_gradient = (upstream * mult_b * sig_b * (1.0 + pre_b * (1.0 - sig_b))).astype(
        jnp.bfloat16
    )
    taps_grad = adjacent_cells(
        second_gradient.reshape(tile_row_count, tile_column_count, patch_width),
        SECOND_DILATION // tile_row_count,
        SECOND_DILATION // tile_column_count,
    )
    column_gradient, matrix_t = lower(taps_grad, weight_b, True)
    back = upstream + jnp.dot(column_gradient, matrix_t, preferred_element_type=jnp.float32)
    grad_a = (back * mult_a * sig_a * (1.0 + pre_a * (1.0 - sig_a))).astype(jnp.bfloat16)
    scale = 1.0 / math.sqrt(
        lax.axis_size(("lead", "gy", "gx")) * tile_row_count * tile_column_count
    )
    products = (
        lax.dot_general(
            input_columns, grad_a, (((0,), (0,)), ((), ())), preferred_element_type=jnp.float32
        )
        * scale
    )
    term = jnp.zeros((3, 3, patch_width, patch_width), jnp.float32)
    for number, (row_off, col_off, piece) in enumerate(input_kernel_taps):
        term = term.at[row_off + 1, col_off + 1].set(
            products[number * patch_width : (number + 1) * patch_width]
        )
    flat_term = term.reshape(lax.axis_size(("lead", "gy")), lax.axis_size("gx"), -1)
    partial_sum = lax.psum_scatter(flat_term, "gx", scatter_dimension=1, tiled=True)
    total = lax.psum_scatter(partial_sum, ("lead", "gy"), scatter_dimension=0, tiled=True)
    return (outputs.reshape(inputs.shape), total.reshape(-1))


def solution(mesh):
    return jax.shard_map(
        shards,
        mesh=mesh,
        in_specs=(
            P("lead", "gy", "gx", None),
            P("lead"),
            P(),
            P(None, ("lead", "gy", "gx")),
            P("lead", "gy", "gx", None),
        ),
        out_specs=(P("lead", "gy", "gx", None), P(("lead", "gy", "gx"))),
        check_vma=False,
    )
```

profile of v0, /device:TPU:0, one launch (start us, length us, event | category | flops | bytes accessed | tf_op | source)
XLA Modules:
  0.0 250.9 jit_solution(15108442992412897639)
XLA Ops:
  7.2 0.0 all-gather.2.cloned.1.call-start
  7.2 0.7 all-gather.2.cloned.1.call-update
  7.9 0.0 reduce-scatter.2.cloned.1.call-start
  7.9 1.3 collective-permute-start.1
  9.2 3.8 %collective-permute-start = (bf16[64,8,256]{2,1,0:T(8,128)(2,1)}, bf16[64,8,256]{2,1,0:T(8,128)(2,1)}, u32[]{:S(2)}, u32[]{:S(2)}) collective-permute-start(bf16[64,8,256]{2,1,0:T(8,128)(2,1)} %bitcast.71), channel_id=1, source_target_pairs={{0,4},{4,8},{8,12},{1,5},{5,9},{9,13},{2,6},{6,10},{10,14},{3,7},{... | collective-permute-start | bytes 786440 | tf_op jit(solution)/shard_map/ppermute | solution.py:15
  13.7 1.7 copy.10
  15.4 0.6 fusion.65
  16.0 55.0 %all-gather.2.cloned.1.call-done = bf16[2,589824]{1,0:T(2,128)(2,1)} async-done(((bf16[2,18432]{1,0:T(2,128)(2,1)}), bf16[2,589824]{1,0:T(2,128)(2,1)}) %all-gather.2.cloned.1.call-update) | async-done | bytes 2359312 | tf_op jit(solution)/shard_map/all_gather | solution.py:72
  71.0 26.3 %slice_reduce_fusion = (bf16[589824]{0:T(1024)(128)(2,1)S(1)}, bf16[589824]{0:T(1024)(128)(2,1)S(1)}) fusion(bf16[2,589824]{1,0:T(2,128)(2,1)} %all-gather.2.cloned.1.call-done), kind=kLoop, calls=%fused_computation | loop fusion | bytes 4718592 | tf_op jit(solution)/shard_map/slice | solution.py:74
  97.2 0.4 reshape_squeeze.11
  97.7 0.0 collective-permute-done.1
  97.7 0.0 collective-permute-done
  97.7 2.4 add_convert_fusion.1
  100.1 1.3 collective-permute-start.3
  101.4 4.6 %collective-permute-start.2 = (bf16[64,8,256]{2,1,0:T(8,128)(2,1)S(1)}, bf16[64,8,256]{2,1,0:T(8,128)(2,1)S(1)}, u32[]{:S(2)}, u32[]{:S(2)}) collective-permute-start(bf16[64,8,256]{2,1,0:T(8,128)(2,1)S(1)} %bitcast.77), channel_id=1, source_target_pairs={{0,8},{4,12},{1,9},{5,13},{2,10},{6,14},{3,11},{7,15},{16,24},{20,... | collective-permute-start | bytes 786440 | tf_op jit(solution)/shard_map/ppermute | solution.py:15
  106.0 0.0 copy-start
  106.0 0.4 reshape_squeeze.12
  106.5 0.1 slice_bitcast_fusion.6
  106.5 4.0 %collective-permute-done.3 = bf16[64,8,256]{2,1,0:T(8,128)(2,1)S(1)} collective-permute-done((bf16[64,8,256]{2,1,0:T(8,128)(2,1)S(1)}, bf16[64,8,256]{2,1,0:T(8,128)(2,1)S(1)}, u32[]{:S(2)}, u32[]{:S(2)}) %collective-permute-start.3) | collective-permute-done | bytes 262176 | tf_op jit(solution)/shard_map/ppermute | solution.py:15
  110.5 0.0 copy-start.2
  110.5 1.2 collective-permute-done.2
  111.7 0.0 copy-start.3
  111.7 0.0 copy-done.2
  111.7 0.7 copy-done.3
  112.4 0.0 copy-done
  112.4 0.0 copy-start.1
  112.4 0.0 copy-start.5
  112.4 2.4 fusion.24
  114.7 1.3 collective-permute-start.5
  116.0 4.8 %collective-permute-start.4 = (bf16[64,8,256]{2,1,0:T(8,128)(2,1)S(1)}, bf16[64,8,256]{2,1,0:T(8,128)(2,1)S(1)}, u32[]{:S(2)}, u32[]{:S(2)}) collective-permute-start(bf16[64,8,256]{2,1,0:T(8,128)(2,1)S(1)} %bitcast.75), channel_id=1, source_target_pairs={{0,8},{4,12},{1,9},{5,13},{2,10},{6,14},{3,11},{7,15},{16,24},{20,... | collective-permute-start | bytes 786440 | tf_op jit(solution)/shard_map/ppermute | solution.py:15
  120.8 0.6 fusion.60
  121.4 2.7 %collective-permute-done.5 = bf16[64,8,256]{2,1,0:T(8,128)(2,1)S(1)} collective-permute-done((bf16[64,8,256]{2,1,0:T(8,128)(2,1)S(1)}, bf16[64,8,256]{2,1,0:T(8,128)(2,1)S(1)}, u32[]{:S(2)}, u32[]{:S(2)}) %collective-permute-start.5) | collective-permute-done | bytes 262176 | tf_op jit(solution)/shard_map/ppermute | solution.py:15
  124.1 1.2 collective-permute-done.4
  125.3 0.0 copy-done.1
  125.3 0.0 copy-done.5
  125.3 2.1 convolution_multiply_fusion
  127.4 0.2 broadcast_in_dim.2
  127.6 1.2 fusion.50
  128.9 2.2 reshape.167
  131.1 4.5 %copy.8 = f32[8,4,18432]{2,0,1:T(8,128)} copy(f32[8,4,18432]{2,1,0:T(4,128)} %reshape.167) | data formatting | bytes 4718592 | tf_op jit(solution)/shard_map/reshape | solution.py:129
  135.6 0.0 copy-start.4
  135.6 0.0 reduce-scatter.2.cloned.1.call-update
  135.6 0.0 all-reduce.3.cloned.1.call-start
  135.6 48.9 %reduce-scatter.2.cloned.1.call-done = f32[8,1,18432]{2,0,1:T(8,128)} async-done(((f32[8,4,18432]{2,0,1:T(8,128)}), f32[8,1,18432]{2,0,1:T(8,128)}) %reduce-scatter.2.cloned.1.call-update) | async-done | bytes 589840 | tf_op jit(solution)/shard_map/reduce_scatter | solution.py:130
  184.5 2.5 copy.9
  187.0 0.0 all-reduce.3.cloned.1.call-update
  187.1 0.0 copy-done.4
  187.1 0.7 dynamic-slice.24
  187.7 54.5 %all-reduce.3.cloned.1.call-done = f32[8,1,18432]{2,1,0:T(1,128)} async-done(((f32[8,1,18432]{2,1,0:T(1,128)}), f32[8,1,18432]{2,1,0:T(1,128)}) %all-reduce.3.cloned.1.call-update) | async-done | bytes 589840
  242.2 2.2 constant_dynamic-slice_fusion
  (7 shorter events, 0.1 us)
Async XLA Ops:
  7.2 63.8 %all-gather.2.cloned.1.call-start = ((), (), s32[]{:S(2)}) async-start(), calls=%async_computation.1 | async-start | bytes 2433024 | tf_op jit(solution)/shard_map/all_gather | solution.py:72
  7.9 176.6 %reduce-scatter.2.cloned.1.call-start = ((), (), s32[]{:S(2)}) async-start(), calls=%async_computation.2 | async-start | bytes 2949120 | tf_op jit(solution)/shard_map/reduce_scatter | solution.py:130
  7.9 89.8 %collective-permute-start.1 = (bf16[64,8,256]{2,1,0:T(8,128)(2,1)}, bf16[64,8,256]{2,1,0:T(8,128)(2,1)}, u32[]{:S(2)}, u32[]{:S(2)}) collective-permute-start(bf16[64,8,256]{2,1,0:T(8,128)(2,1)} %bitcast.70), channel_id=1, source_target_pairs={{4,0},{8,4},{12,8},{5,1},{9,5},{13,9},{6,2},{10,6},{14,10},{7,3},{... | collective-permute-start | bytes 786440 | tf_op jit(solution)/shard_map/ppermute | solution.py:15
  9.2 88.5 %collective-permute-start = (bf16[64,8,256]{2,1,0:T(8,128)(2,1)}, bf16[64,8,256]{2,1,0:T(8,128)(2,1)}, u32[]{:S(2)}, u32[]{:S(2)}) collective-permute-start(bf16[64,8,256]{2,1,0:T(8,128)(2,1)} %bitcast.71), channel_id=1, source_target_pairs={{0,4},{4,8},{8,12},{1,5},{5,9},{9,13},{2,6},{6,10},{10,14},{3,7},{... | collective-permute-start | bytes 786440 | tf_op jit(solution)/shard_map/ppermute | solution.py:15
  100.1 10.4 %collective-permute-start.3 = (bf16[64,8,256]{2,1,0:T(8,128)(2,1)S(1)}, bf16[64,8,256]{2,1,0:T(8,128)(2,1)S(1)}, u32[]{:S(2)}, u32[]{:S(2)}) collective-permute-start(bf16[64,8,256]{2,1,0:T(8,128)(2,1)S(1)} %bitcast.76), channel_id=1, source_target_pairs={{8,0},{12,4},{9,1},{13,5},{10,2},{14,6},{11,3},{15,7},{24,16},{28,... | collective-permute-start | bytes 786440 | tf_op jit(solution)/shard_map/ppermute | solution.py:15
  101.4 10.3 %collective-permute-start.2 = (bf16[64,8,256]{2,1,0:T(8,128)(2,1)S(1)}, bf16[64,8,256]{2,1,0:T(8,128)(2,1)S(1)}, u32[]{:S(2)}, u32[]{:S(2)}) collective-permute-start(bf16[64,8,256]{2,1,0:T(8,128)(2,1)S(1)} %bitcast.77), channel_id=1, source_target_pairs={{0,8},{4,12},{1,9},{5,13},{2,10},{6,14},{3,11},{7,15},{16,24},{20,... | collective-permute-start | bytes 786440 | tf_op jit(solution)/shard_map/ppermute | solution.py:15
  106.0 6.4 %copy-start = (bf16[1,64,8,256]{3,2,1,0:T(8,128)(2,1)S(1)}, bf16[1,64,8,256]{3,2,1,0:T(8,128)(2,1)}, u32[]{:S(2)}) copy-start(bf16[1,64,8,256]{3,2,1,0:T(8,128)(2,1)} %param.15) | copy-start | bytes 786436
  110.5 1.2 copy-start.2
  111.7 0.7 copy-start.3
  112.4 12.9 %copy-start.1 = (bf16[1,64,8,256]{3,2,1,0:T(8,128)(2,1)S(1)}, bf16[1,64,8,256]{3,2,1,0:T(8,128)(2,1)}, u32[]{:S(2)}) copy-start(bf16[1,64,8,256]{3,2,1,0:T(8,128)(2,1)} %param.11) | copy-start | bytes 786436
  112.4 12.9 %copy-start.5 = (f32[512,256]{1,0:T(8,128)S(1)}, f32[512,256]{1,0:T(8,128)}, u32[]{:S(2)}) copy-start(f32[512,256]{1,0:T(8,128)} %get-tuple-element.58) | copy-start | bytes 1572868
  114.7 9.3 %collective-permute-start.5 = (bf16[64,8,256]{2,1,0:T(8,128)(2,1)S(1)}, bf16[64,8,256]{2,1,0:T(8,128)(2,1)S(1)}, u32[]{:S(2)}, u32[]{:S(2)}) collective-permute-start(bf16[64,8,256]{2,1,0:T(8,128)(2,1)S(1)} %bitcast.74), channel_id=1, source_target_pairs={{8,0},{12,4},{9,1},{13,5},{10,2},{14,6},{11,3},{15,7},{24,16},{28,... | collective-permute-start | bytes 786440 | tf_op jit(solution)/shard_map/ppermute | solution.py:15
  116.0 9.2 %collective-permute-start.4 = (bf16[64,8,256]{2,1,0:T(8,128)(2,1)S(1)}, bf16[64,8,256]{2,1,0:T(8,128)(2,1)S(1)}, u32[]{:S(2)}, u32[]{:S(2)}) collective-permute-start(bf16[64,8,256]{2,1,0:T(8,128)(2,1)S(1)} %bitcast.75), channel_id=1, source_target_pairs={{0,8},{4,12},{1,9},{5,13},{2,10},{6,14},{3,11},{7,15},{16,24},{20,... | collective-permute-start | bytes 786440 | tf_op jit(solution)/shard_map/ppermute | solution.py:15
  135.6 51.5 %copy-start.4 = (u32[32]{0:T(128)S(1)}, u32[32]{0:T(128)}, u32[]{:S(2)}) copy-start(u32[32]{0:T(128)} %constant.101) | copy-start | bytes 388
  135.6 106.6 %all-reduce.3.cloned.1.call-start = ((), (), s32[]{:S(2)}) async-start(), calls=%async_computation.3 | async-start | bytes 1179648
Sparse Core Ops, SparseCore 0:
  10.9 60.0 all-gather.1
  135.7 48.7 reduce-scatter.1
  187.7 54.4 all-reduce.2
where the time goes:
time: 251 us
  waiting for transfers between devices  168 us (67%)
  local copies, waits for them, and re-layouts  43.7 us (17%)
  starting transfers between devices  17.1 us (7%)
  between operations  14.6 us (6%)
  matrix products  7.43 us (3%)
    unnamed x4, waiting for transfers between devices  55.2 us
    all_gather x1, waiting for transfers between devices, shards(): lax.all_gather(flat_weights, ('lead', 'gy', 'gx'), axis=1, tiled=True)  55 us
    reduce_scatter x1, waiting for transfers between devices, shards(): lax.psum_scatter(flat_term, 'gx', scatter_dimension=1, tiled=True)  48.9 us
    slice x1, local copies, waits for them, and re-layouts, shards(): weight_b = gathered[1].reshape(3, 3, patch_width, patch_width)  26.3 us
    ppermute x6, starting transfers between devices, passed_along(): lax.ppermute(value, axis, [(source, source + steps) for source in range(l...  17 us
    ppermute x6, waiting for transfers between devices, passed_along(): lax.ppermute(value, axis, [(source, source + steps) for source in range(l...  9.05 us
    reshape x2, local copies, waits for them, and re-layouts, shards(): term.reshape(lax.axis_size(('lead', 'gy')), lax.axis_size('gx'), -1)  6.7 us
    unnamed x15, local copies, waits for them, and re-layouts  5.21 us
  transfers between devices with their start and end apart: 9, of which 7 were waited for; matrix products, arithmetic and copies ran while one was open for 12% of the time, Pallas kernels for 0%

commit v1 on v0

--- a/solution.py
+++ b/solution.py
@@ -2,11 +2,15 @@
 
 import jax
 import jax.numpy as jnp
+import numpy as np
 from jax import lax
+from jax.experimental import pallas as pl
+from jax.experimental.pallas import tpu as pltpu
 from jax.sharding import PartitionSpec as P
 
 FIRST_DILATION = 64
 SECOND_DILATION = 128
+AXES = ("lead", "gy", "gx")
 
 
 def passed_along(value, axis, steps):
@@ -63,20 +67,16 @@
     return (cols, jnp.concatenate(blocks, axis=0))
 
 
-def shards(inputs, lead_ids, film, flat_weights, cotangent):
+def general_shards(inputs, lead_ids, film, flat_weights, cotangent):
     tile_row_count, tile_column_count, patch_width = (
         inputs.shape[1],
         inputs.shape[2],
         inputs.shape[3],
     )
-    gathered = lax.all_gather(flat_weights, ("lead", "gy", "gx"), axis=1, tiled=True)
+    gathered = lax.all_gather(flat_weights, AXES, axis=1, tiled=True)
     weight_a = gathered[0].reshape(3, 3, patch_width, patch_width)
     weight_b = gathered[1].reshape(3, 3, patch_width, patch_width)
-    table_rows = film.shape[0]
-    picker = (jnp.arange(table_rows, dtype=jnp.int32) == lead_ids[0]).astype(jnp.float32)
-    film_row = jnp.dot(
-        picker, film.reshape(table_rows, -1), precision=lax.Precision.HIGHEST
-    ).reshape(4, patch_width)
+    film_row = lax.dynamic_index_in_dim(film, lead_ids[0], 0, keepdims=False)
     mult_a = 1.0 + film_row[0]
     shift_a = film_row[1]
     mult_b = 1.0 + film_row[2]
@@ -112,9 +112,7 @@
     column_gradient, matrix_t = lower(taps_grad, weight_b, True)
     back = upstream + jnp.dot(column_gradient, matrix_t, preferred_element_type=jnp.float32)
     grad_a = (back * mult_a * sig_a * (1.0 + pre_a * (1.0 - sig_a))).astype(jnp.bfloat16)
-    scale = 1.0 / math.sqrt(
-        lax.axis_size(("lead", "gy", "gx")) * tile_row_count * tile_column_count
-    )
+    scale = 1.0 / math.sqrt(lax.axis_size(AXES) * tile_row_count * tile_column_count)
     products = (
         lax.dot_general(
             input_columns, grad_a, (((0,), (0,)), ((), ())), preferred_element_type=jnp.float32
@@ -132,17 +130,251 @@
     return (outputs.reshape(inputs.shape), total.reshape(-1))
 
 
+def fits(mesh, rows, columns):
+    size = mesh.shape
+    return (
+        tuple(mesh.axis_names) == AXES
+        and (size["lead"], size["gy"], size["gx"]) == (2, 4, 4)
+        and FIRST_DILATION == rows
+        and SECOND_DILATION == 2 * rows
+        and FIRST_DILATION // columns >= size["gx"]
+    )
+
+
+def pairs(move):
+    number = lambda x, y, c, z: x * 16 + (2 * y + c) * 4 + z
+    return [
+        (number(x, y, c, z), number(*move(x, y, c, z)))
+        for x in range(2)
+        for y in range(2)
+        for c in range(2)
+        for z in range(4)
+    ]
+
+
+def moved(value, dx=0, dy=0, dc=0, dz=0):
+    return lax.ppermute(
+        value, AXES, pairs(lambda x, y, c, z: (x ^ dx, y ^ dy, c ^ dc, z ^ dz))
+    )
+
+
+CORE_GROUPS = [
+    [x * 16 + (2 * y + c) * 4 + z for x in range(2) for y in range(2) for z in range(4)]
+    for c in range(2)
+]
+
+
+def used_rows(width, shard_rows):
+    found = []
+    for block in range(3):
+        start = (3 * block + 1) * width
+        row = start
+        while row < start + width:
+            shard = row // shard_rows
+            stop = min((shard + 1) * shard_rows, start + width)
+            place = (shard // 16, shard // 8 % 2, shard // 4 % 2, shard % 4)
+            found.append((*place, row - shard * shard_rows, stop - row, block * width + row - start))
+            row = stop
+    return found
+
+
+def main_kernel(
+    pieces,
+    scale,
+    where_ref,
+    mine_x,
+    other_x,
+    mine_ct,
+    other_ct,
+    near_x0,
+    near_x1,
+    lane_own,
+    lane_other,
+    film_ref,
+    out_keep,
+    out_send,
+    grad_keep,
+    grad_send,
+    weights,
+    around,
+    total,
+):
+    x, y, c, z = (where_ref[i] for i in range(4))
+    width = film_ref.shape[1]
+    half = mine_x.shape[0]
+    f32, bf16 = jnp.float32, jnp.bfloat16
+
+    for cx, cy, cc, cz, first, count, row in pieces:
+        place = (cx ^ x) + 2 * (cy ^ y)
+        for k in range(2):
+            own = lane_own[place, cz ^ z, k].astype(f32)
+            weights[k, c, row : row + count, :] = own[first : first + count]
+            oth = lane_other[place, cz ^ z, k].astype(f32)
+            weights[k, 1 - c, row : row + count, :] = oth[first : first + count]
+
+    def block(k, number):
+        rows = slice(number * width, (number + 1) * width)
+        return jnp.concatenate([weights[k, 0, rows, :], weights[k, 1, rows, :]], axis=1).astype(
+            bf16
+        )
+
+    first_half = y == 0
+    lo = jnp.where(first_half, mine_x[...], other_x[...])
+    hi = jnp.where(first_half, other_x[...], mine_x[...])
+    mid = jnp.concatenate([lo, hi], axis=0)
+    around[0] = jnp.zeros_like(lo)
+    around[3] = jnp.zeros_like(lo)
+    around[1] = jnp.where(first_half, near_x0[...], near_x1[...])
+    around[2] = jnp.where(first_half, near_x1[...], near_x0[...])
+    above = jnp.concatenate([around[c], around[c + 1]], axis=0)
+    below = jnp.concatenate([around[c + 1], around[c + 2]], axis=0)
+    dot = lambda a, b: jnp.dot(a, b, preferred_element_type=f32)
+    dot_t = lambda a, b: lax.dot_general(a, b, (((1,), (1,)), ((), ())), preferred_element_type=f32)
+    t_dot = lambda a, b: lax.dot_general(a, b, (((0,), (0,)), ((), ())), preferred_element_type=f32)
+
+    mult_a = 1.0 + film_ref[0:1, :]
+    shift_a = film_ref[1:2, :]
+    mult_b = 1.0 + film_ref[2:3, :]
+    shift_b = film_ref[3:4, :]
+    conv_a = dot(above, block(0, 0)) + dot(mid, block(0, 1)) + dot(below, block(0, 2))
+    pre_a = conv_a * mult_a + shift_a
+    sig_a = jax.nn.sigmoid(pre_a)
+    hidden = (mid.astype(f32) + pre_a * sig_a).astype(bf16)
+
+    up, centre, down = block(1, 0), block(1, 1), block(1, 2)
+    straight = dot(hidden, centre)
+    across = jnp.concatenate([dot(hidden[half:], down), dot(hidden[:half], up)], axis=0)
+    pre_b = (straight + across) * mult_b + shift_b
+    sig_b = jax.nn.sigmoid(pre_b)
+    result = (hidden.astype(f32) + pre_b * sig_b).astype(bf16)
+    out_keep[...] = jnp.where(first_half, result[:half], result[half:])
+    out_send[...] = jnp.where(first_half, result[half:], result[:half])
+
+    ct_lo = jnp.where(first_half, mine_ct[...], other_ct[...])
+    ct_hi = jnp.where(first_half, other_ct[...], mine_ct[...])
+    upstream = jnp.concatenate([ct_lo, ct_hi], axis=0).astype(f32)
+    grad_b = (upstream * mult_b * sig_b * (1.0 + pre_b * (1.0 - sig_b))).astype(bf16)
+    back = upstream + dot_t(grad_b, centre)
+    back = back + jnp.concatenate([dot_t(grad_b[half:], up), dot_t(grad_b[:half], down)], axis=0)
+    grad_a = (back * mult_a * sig_a * (1.0 + pre_a * (1.0 - sig_a))).astype(bf16)
+
+    lane = width // 2
+    for number, rows in enumerate((above, mid, below)):
+        product = t_dot(rows, grad_a) * scale
+        total[0, number * width : (number + 1) * width, :] = product[:, :lane]
+        total[1, number * width : (number + 1) * width, :] = product[:, lane:]
+    grad_keep[...] = jnp.zeros_like(grad_keep)
+    grad_send[...] = jnp.zeros_like(grad_send)
+    for cx, cy, cc, cz, first, count, row in pieces:
+        chip = cx * 8 + cy * 4 + cz
+        grad_keep[chip, first : first + count, :] = total[c, row : row + count, :]
+        grad_send[chip, first : first + count, :] = total[1 - c, row : row + count, :]
+
+
+def last_kernel(where_ref, own_ref, other_ref, out_ref):
+    c, low = where_ref[2], where_ref[4]
+    rows = own_ref.shape[0]
+    row = lax.broadcasted_iota(jnp.int32, own_ref.shape, 0)
+    held = jnp.logical_xor(row < low, c == 0)
+    own = jnp.where(held, own_ref[...], 0.0)
+    other = jnp.where(held, other_ref[...], 0.0)
+    out_ref[pl.ds(0, rows, stride=2), :] = jnp.where(c == 0, own, other)
+    out_ref[pl.ds(1, rows, stride=2), :] = jnp.where(c == 0, other, own)
+
+
+def row_shards(inputs, lead_ids, film, flat_weights, cotangent):
+    rows, columns, width = inputs.shape[1:]
+    half = rows // 2 * columns
+    lane = width // 2
+    shard_rows = flat_weights.shape[1] // width
+    x, gy, z = (lax.axis_index(axis) for axis in AXES)
+    y, c = gy // 2, gy % 2
+    pieces = used_rows(width, shard_rows)
+
+    low = jnp.where(
+        x == 0,
+        jnp.where((y == 0) & (z == 3), 40, shard_rows),
+        jnp.where((y == 1) & (z == 0), 40, 0),
+    )
+    where = jnp.stack([x, y, c, z, low]).astype(jnp.int32)
+
+    shard = flat_weights.reshape(2, shard_rows, width)
+    left, right = shard[:, :, :lane], shard[:, :, lane:]
+    near = moved(jnp.where(c == 0, right, left), dc=1)
+    row = lax.broadcasted_iota(jnp.int32, near.shape, 1)
+    piece = jnp.where((row < low) == (c == 1), jnp.where(c == 0, left, right), near)
+    line = jnp.stack([piece, moved(piece, dz=1), moved(piece, dz=2), moved(piece, dz=3)])
+    plane = jnp.stack([line, moved(line, dx=1), moved(line, dy=1), moved(line, dx=1, dy=1)])
+    plane_near = moved(plane, dc=1)
+
+    halves_x = inputs.reshape(2, half, width)
+    halves_ct = cotangent.reshape(2, half, width)
+    pick = lambda halves, number: lax.dynamic_index_in_dim(halves, number, 0, keepdims=False)
+    mine_x, mine_ct = pick(halves_x, y), pick(halves_ct, y)
+    other_x = moved(pick(halves_x, 1 - y), dy=1)
+    other_ct = moved(pick(halves_ct, 1 - y), dy=1)
+    near_x0 = moved(mine_x, dc=1)
+    near_x1 = moved(other_x, dc=1)
+    film_row = lax.dynamic_index_in_dim(film, lead_ids[0], 0, keepdims=False)
+
+    scale = 1.0 / math.sqrt(lax.axis_size(AXES) * rows * columns)
+    vmem = pl.BlockSpec(memory_space=pltpu.VMEM)
+    smem = pl.BlockSpec(memory_space=pltpu.SMEM)
+    chips = 16
+    out_keep, out_send, grad_keep, grad_send = pl.pallas_call(
+        lambda *refs: main_kernel(pieces, scale, *refs),
+        out_shape=(
+            jax.ShapeDtypeStruct((half, width), jnp.bfloat16),
+            jax.ShapeDtypeStruct((half, width), jnp.bfloat16),
+            jax.ShapeDtypeStruct((chips, shard_rows, lane), jnp.float32),
+            jax.ShapeDtypeStruct((chips, shard_rows, lane), jnp.float32),
+        ),
+        in_specs=[smem] + [vmem] * 9,
+        out_specs=(vmem,) * 4,
+        scratch_shapes=[
+            pltpu.VMEM((2, 2, 3 * width, lane), jnp.float32),
+            pltpu.VMEM((4, half, width), jnp.bfloat16),
+            pltpu.VMEM((2, 3 * width, lane), jnp.float32),
+        ],
+        compiler_params=pltpu.CompilerParams(vmem_limit_bytes=40 * 1024 * 1024),
+        name="blocks",
+    )(where, mine_x, other_x, mine_ct, other_ct, near_x0, near_x1, plane, plane_near, film_row)
+
+    other_out = moved(out_send, dy=1)
+    first = jnp.where(y == 0, out_keep, other_out)
+    second = jnp.where(y == 0, other_out, out_keep)
+    outputs = jnp.stack([first, second]).reshape(inputs.shape)
+
+    chip_term = (grad_keep + moved(grad_send, dc=1)).astype(jnp.bfloat16)
+    terms = lax.all_to_all(chip_term, AXES, 0, 0, axis_index_groups=CORE_GROUPS)
+    lane_sum = jnp.sum(terms.astype(jnp.float32), axis=0)
+    total = pl.pallas_call(
+        last_kernel,
+        out_shape=jax.ShapeDtypeStruct((2 * shard_rows, lane), jnp.float32),
+        in_specs=[smem, vmem, vmem],
+        out_specs=vmem,
+        name="total",
+    )(where, lane_sum, moved(lane_sum, dc=1))
+    return (outputs, total.reshape(-1))
+
+
 def solution(mesh):
-    return jax.shard_map(
-        shards,
-        mesh=mesh,
-        in_specs=(
-            P("lead", "gy", "gx", None),
-            P("lead"),
-            P(),
-            P(None, ("lead", "gy", "gx")),
-            P("lead", "gy", "gx", None),
-        ),
-        out_specs=(P("lead", "gy", "gx", None), P(("lead", "gy", "gx"))),
-        check_vma=False,
-    )
+    def whole(inputs, lead_ids, film, flat_weights, cotangent):
+        size = mesh.shape
+        rows, columns = inputs.shape[1] // size["gy"], inputs.shape[2] // size["gx"]
+        plan = row_shards if fits(mesh, rows, columns) else general_shards
+        return jax.shard_map(
+            plan,
+            mesh=mesh,
+            in_specs=(
+                P("lead", "gy", "gx", None),
+                P("lead"),
+                P(),
+                P(None, AXES),
+                P("lead", "gy", "gx", None),
+            ),
+            out_specs=(P("lead", "gy", "gx", None), P(AXES)),
+            check_vma=False,
+        )(inputs, lead_ids, film, flat_weights, cotangent)
+
+    return whole

time: 251 us -> 58.2 us (0.23)
  waiting for transfers between devices: 168 us -> 28.4 us
  local copies, waits for them, and re-layouts: 43.7 us -> 3.76 us
  between operations: 14.6 us -> 1.47 us
  matrix products: 7.43 us -> 0 us
  Pallas kernels: 0 us -> 3.92 us
    unnamed x4 -> x0, waiting for transfers between devices: 55.2 us -> none
    all_gather x1 -> x0, waiting for transfers between devices: 55 us -> none  [shards(): lax.all_gather(flat_weights, ('lead', 'gy', 'gx'), axis=1, tiled=True)]
    reduce_scatter x1 -> x0, waiting for transfers between devices: 48.9 us -> none  [shards(): lax.psum_scatter(flat_term, 'gx', scatter_dimension=1, tiled=True)]
    slice x1 -> x0, local copies, waits for them, and re-layouts: 26.3 us -> none  [shards(): weight_b = gathered[1].reshape(3, 3, patch_width, patch_width)]
    ppermute x6 -> x15, waiting for transfers between devices: 9.05 us -> 24.4 us  [moved(): lax.ppermute(value, AXES, pairs(lambda x, y, c, z: (x ^ dx, y ^ dy, c ^ d...]
    dot_general x4 -> x0, matrix products: 7.43 us -> none  [the longest x1 2.4 us: shards(): jnp.dot(input_columns, matrix_a, preferred_element_type=jnp.float32)]
    reshape x2 -> x0, local copies, waits for them, and re-layouts: 6.7 us -> none  [shards(): term.reshape(lax.axis_size(('lead', 'gy')), lax.axis_size('gx'), -1)]
    all_to_all x0 -> x1, starting transfers between devices: none -> 4.41 us  [row_shards(): terms = lax.all_to_all(chip_term, AXES, 0, 0, axis_index_groups=CORE_GROUPS)]
  transfers between devices with their start and end apart: 9 -> 16, of which waited for: 7 -> 12; matrix products, arithmetic and copies ran while one was open for 12% -> 3% of each run, Pallas kernels for 0% -> 0%
where the time goes in v1:
time: 58.2 us; the launch traced here: 57.9 us
  waiting for transfers between devices  28.4 us (49%)
  starting transfers between devices  18.5 us (32%)
  Pallas kernels  3.92 us (7%)
  local copies, waits for them, and re-layouts  3.76 us (6%)
  other arithmetic  1.78 us (3%)
  between operations  1.47 us (3%)
    ppermute x15, waiting for transfers between devices, moved(): lax.ppermute(value, AXES, pairs(lambda x, y, c, z: (x ^ dx, y ^ dy, c ^ d...  24.4 us
    ppermute x15, starting transfers between devices, moved(): lax.ppermute(value, AXES, pairs(lambda x, y, c, z: (x ^ dx, y ^ dy, c ^ d...  14.1 us
    all_to_all x1, starting transfers between devices, row_shards(): terms = lax.all_to_all(chip_term, AXES, 0, 0, axis_index_groups=CORE_GROUPS)  4.41 us
    all_to_all x1, waiting for transfers between devices, row_shards(): terms = lax.all_to_all(chip_term, AXES, 0, 0, axis_index_groups=CORE_GROUPS)  3.99 us
    unnamed x21, local copies, waits for them, and re-layouts  2.97 us
    pallas_call x1, Pallas kernels, row_shards(): pl.pallas_call(lambda *refs: main_kernel(pieces, scale, *refs), out_shape...  2.48 us
    pallas_call x1, Pallas kernels, row_shards(): pl.pallas_call(last_kernel, out_shape=jax.ShapeDtypeStruct((2 * shard_row...  1.44 us
  transfers between devices with their start and end apart: 16, of which 12 were waited for; matrix products, arithmetic and copies ran while one was open for 3% of the time, Pallas kernels for 0%

profile of v1, /device:TPU:0, one launch (start us, length us, event | category | flops | bytes accessed | tf_op | source)
XLA Modules:
  0.0 57.9 jit_solution(6727406122602262949)
XLA Ops:
  0.6 0.0 copy-start
  0.6 0.0 copy-start.6
  0.7 0.0 copy-start.7
  0.7 1.0 %copy.9 = bf16[1,2,72,256]{3,2,1,0:T(8,128)(2,1)S(1)} copy(bf16[1,2,72,256]{3,1,2,0:T(2,128)(2,1)} %bitcast.49) | data formatting | bytes 147456
  1.7 0.5 collective-permute-start.4
  2.3 0.9 %collective-permute-done.4 = bf16[2,72,128]{2,1,0:T(8,128)(2,1)S(1)} collective-permute-done((bf16[2,72,128]{2,1,0:T(8,128)(2,1)S(1)}, bf16[2,72,128]{2,1,0:T(8,128)(2,1)S(1)}, u32[]{:S(2)}, u32[]{:S(2)}) %collective-permute-start.4) | collective-permute-done | bytes 36896 | tf_op jit(solution)/shard_map/ppermute | solution.py:156
  3.1 0.1 select_select_fusion
  3.2 5.0 %collective-permute-start.7 = (bf16[2,72,128]{2,1,0:T(8,128)(2,1)S(1)}, bf16[2,72,128]{2,1,0:T(8,128)(2,1)S(1)}, u32[]{:S(2)}, u32[]{:S(2)}) collective-permute-start(bf16[2,72,128]{2,1,0:T(8,128)(2,1)S(1)} %select_select_fusion), channel_id=1, source_target_pairs={{0,3},{1,2},{2,1},{3,0},{4,7},{5,6},{6,5},{7,4},{8,11},{9,10},{10,... | collective-permute-start | bytes 110600 | tf_op jit(solution)/shard_map/ppermute | solution.py:156
  8.2 0.0 collective-permute-start.6
  8.2 0.6 %collective-permute-start.5 = (bf16[2,72,128]{2,1,0:T(8,128)(2,1)S(1)}, bf16[2,72,128]{2,1,0:T(8,128)(2,1)S(1)}, u32[]{:S(2)}, u32[]{:S(2)}) collective-permute-start(bf16[2,72,128]{2,1,0:T(8,128)(2,1)S(1)} %select_select_fusion), channel_id=1, source_target_pairs={{0,1},{1,0},{2,3},{3,2},{4,5},{5,4},{6,7},{7,6},{8,9},{9,8},{10,11... | collective-permute-start | bytes 110600 | tf_op jit(solution)/shard_map/ppermute | solution.py:156
  8.9 1.3 %collective-permute-done.7 = bf16[2,72,128]{2,1,0:T(8,128)(2,1)S(1)} collective-permute-done((bf16[2,72,128]{2,1,0:T(8,128)(2,1)S(1)}, bf16[2,72,128]{2,1,0:T(8,128)(2,1)S(1)}, u32[]{:S(2)}, u32[]{:S(2)}) %collective-permute-start.7) | collective-permute-done | bytes 36896 | tf_op jit(solution)/shard_map/ppermute | solution.py:156
  10.2 2.9 %collective-permute-done.6 = bf16[2,72,128]{2,1,0:T(8,128)(2,1)S(1)} collective-permute-done((bf16[2,72,128]{2,1,0:T(8,128)(2,1)S(1)}, bf16[2,72,128]{2,1,0:T(8,128)(2,1)S(1)}, u32[]{:S(2)}, u32[]{:S(2)}) %collective-permute-start.6) | collective-permute-done | bytes 36896 | tf_op jit(solution)/shard_map/ppermute | solution.py:156
  13.1 0.0 collective-permute-done.5
  13.1 1.6 %collective-permute-start.9 = (bf16[4,2,72,128]{3,2,1,0:T(8,128)(2,1)S(1)}, bf16[4,2,72,128]{3,2,1,0:T(8,128)(2,1)S(1)}, u32[]{:S(2)}, u32[]{:S(2)}) collective-permute-start(bf16[4,2,72,128]{3,2,1,0:T(8,128)(2,1)S(1)} %get-tuple-element.17), channel_id=1, source_target_pairs={{0,8},{1,9},{2,10},{3,11},{4,12},{5,13},{6,14},{7,15},{8,0},{9,1},... | collective-permute-start | bytes 442376 | tf_op jit(solution)/shard_map/ppermute | solution.py:156
  14.7 1.5 %collective-permute-start.8 = (bf16[4,2,72,128]{3,2,1,0:T(8,128)(2,1)S(1)}, bf16[4,2,72,128]{3,2,1,0:T(8,128)(2,1)S(1)}, u32[]{:S(2)}, u32[]{:S(2)}) collective-permute-start(bf16[4,2,72,128]{3,2,1,0:T(8,128)(2,1)S(1)} %get-tuple-element.17), channel_id=1, source_target_pairs={{0,16},{1,17},{2,18},{3,19},{4,20},{5,21},{6,22},{7,23},{8,24},{9,... | collective-permute-start | bytes 442376 | tf_op jit(solution)/shard_map/ppermute | solution.py:156
  16.2 0.5 collective-permute-start.10
  16.7 1.8 %collective-permute-done.9 = bf16[4,2,72,128]{3,2,1,0:T(8,128)(2,1)S(1)} collective-permute-done((bf16[4,2,72,128]{3,2,1,0:T(8,128)(2,1)S(1)}, bf16[4,2,72,128]{3,2,1,0:T(8,128)(2,1)S(1)}, u32[]{:S(2)}, u32[]{:S(2)}) %collective-permute-start.9) | collective-permute-done | bytes 147488 | tf_op jit(solution)/shard_map/ppermute | solution.py:156
  18.4 2.4 %collective-permute-done.8 = bf16[4,2,72,128]{3,2,1,0:T(8,128)(2,1)S(1)} collective-permute-done((bf16[4,2,72,128]{3,2,1,0:T(8,128)(2,1)S(1)}, bf16[4,2,72,128]{3,2,1,0:T(8,128)(2,1)S(1)}, u32[]{:S(2)}, u32[]{:S(2)}) %collective-permute-start.8) | collective-permute-done | bytes 147488 | tf_op jit(solution)/shard_map/ppermute | solution.py:156
  20.9 2.0 %collective-permute-done.10 = bf16[4,2,72,128]{3,2,1,0:T(8,128)(2,1)S(1)} collective-permute-done((bf16[4,2,72,128]{3,2,1,0:T(8,128)(2,1)S(1)}, bf16[4,2,72,128]{3,2,1,0:T(8,128)(2,1)S(1)}, u32[]{:S(2)}, u32[]{:S(2)}) %collective-permute-start.10) | collective-permute-done | bytes 147488 | tf_op jit(solution)/shard_map/ppermute | solution.py:156
  22.9 0.1 pad_maximum_fusion.refs_7_
  23.0 0.1 collective-permute-start.11
  23.1 0.0 copy-done.6
  23.1 1.1 %collective-permute-start = (bf16[256,256]{1,0:T(8,128)(2,1)S(1)}, bf16[256,256]{1,0:T(8,128)(2,1)S(1)}, u32[]{:S(2)}, u32[]{:S(2)}) collective-permute-start(bf16[256,256]{1,0:T(8,128)(2,1)S(1)} %get-tuple-element.14), channel_id=1, source_target_pairs={{0,8},{1,9},{2,10},{3,11},{4,12},{5,13},{6,14},{7,15},{8,0},{9,1},... | collective-permute-start | bytes 393224 | tf_op jit(solution)/shard_map/ppermute | solution.py:156
  24.2 0.2 collective-permute-start.2
  24.4 0.0 copy-done.7
  24.4 0.7 %dynamic-slice_bitcast_fusion = (bf16[256,256]{1,0:T(8,128)(2,1)}, bf16[256,256]{1,0:T(8,128)(2,1)S(1)}) fusion(bf16[2,256,256]{2,1,0:T(8,128)(2,1)S(1)} %bitcast.43, s32[]{:T(128)S(6)} %select_n.70, s32[]{:T(128)S(6)} %select_n.69), kind=kLoop, calls=%fused_computation.7 | loop fusion | bytes 524296 | tf_op jit(solution)/shard_map/jit(dynamic_index_in_dim)/squeeze | solution.py:312
  25.1 1.0 %collective-permute-start.1 = (bf16[256,256]{1,0:T(8,128)(2,1)}, bf16[256,256]{1,0:T(8,128)(2,1)S(1)}, u32[]{:S(2)}, u32[]{:S(2)}) collective-permute-start(bf16[256,256]{1,0:T(8,128)(2,1)} %get-tuple-element.12), channel_id=1, source_target_pairs={{0,8},{1,9},{2,10},{3,11},{4,12},{5,13},{6,14},{7,15},{8,0},{9,1},... | collective-permute-start | bytes 393224 | tf_op jit(solution)/shard_map/ppermute | solution.py:156
  26.1 3.4 %collective-permute-done.refs_2_ = bf16[256,256]{1,0:T(8,128)(2,1)S(1)} collective-permute-done((bf16[256,256]{1,0:T(8,128)(2,1)S(1)}, bf16[256,256]{1,0:T(8,128)(2,1)S(1)}, u32[]{:S(2)}, u32[]{:S(2)}) %collective-permute-start) | collective-permute-done | bytes 131104 | tf_op jit(solution)/shard_map/ppermute | solution.py:156
  29.5 0.0 collective-permute-start.3
  30.2 0.1 stack.62.refs_0_.where_ref
  30.3 0.0 copy-done
  30.3 0.0 copy-start.3
  30.3 0.0 collective-permute-done.2.refs_5_
  30.3 1.6 %collective-permute-done.1.refs_4_ = bf16[256,256]{1,0:T(8,128)(2,1)S(1)} collective-permute-done((bf16[256,256]{1,0:T(8,128)(2,1)}, bf16[256,256]{1,0:T(8,128)(2,1)S(1)}, u32[]{:S(2)}, u32[]{:S(2)}) %collective-permute-start.1) | collective-permute-done | bytes 131104 | tf_op jit(solution)/shard_map/ppermute | solution.py:156
  31.9 0.0 collective-permute-done.3.refs_6_
  31.9 0.0 collective-permute-done.11.refs_8_
  31.9 2.5 %blocks.1 = (bf16[256,256]{1,0:T(8,128)(2,1)S(1)}, bf16[256,256]{1,0:T(8,128)(2,1)S(1)}, f32[16,72,128]{2,1,0:T(8,128)S(1)}, f32[16,72,128]{2,1,0:T(8,128)S(1)}) custom-call(s32[5]{0:T(128)S(1)} %stack.62.refs_0_.where_ref, bf16[256,256]{1,0:T(8,128)(2,1)S(1)} %get-tuple-element.15.refs_1_, bf16[256,256]{1,0:T(8,128)(2,1)S(1)} %collective-permute-done.refs_2_, ...), custom_call_target="tpu_custom_call" | custom-call | tf_op jit(solution)/shard_map/blocks/pallas_call | solution.py:324
  34.4 0.0 copy-start.1
  34.4 0.6 %copy-done.1 = bf16[256,256]{1,0:T(8,128)(2,1)} copy-done((bf16[256,256]{1,0:T(8,128)(2,1)}, bf16[256,256]{1,0:T(8,128)(2,1)S(1)}, u32[]{:S(2)}) %copy-start.1) | copy-done | bytes 131096
  35.0 0.0 copy-start.4
  35.0 0.6 %copy-done.4 = bf16[256,256]{1,0:T(8,128)(2,1)} copy-done((bf16[256,256]{1,0:T(8,128)(2,1)}, bf16[256,256]{1,0:T(8,128)(2,1)S(1)}, u32[]{:S(2)}) %copy-start.4) | copy-done | bytes 131096
  35.7 0.0 copy-start.5
  35.7 0.0 copy-start.2
  35.7 0.0 collective-permute-start.13
  35.7 2.0 %collective-permute-done.13 = f32[16,72,128]{2,1,0:T(8,128)S(1)} collective-permute-done((f32[16,72,128]{2,1,0:T(8,128)S(1)}, f32[16,72,128]{2,1,0:T(8,128)S(1)}, u32[]{:S(2)}, u32[]{:S(2)}) %collective-permute-start.13) | collective-permute-done | bytes 589856 | tf_op jit(solution)/shard_map/ppermute | solution.py:156
  37.7 0.8 %add_convert_fusion = bf16[16,72,128]{2,1,0:T(8,128)(2,1)} fusion(f32[16,72,128]{2,1,0:T(8,128)S(1)} %get-tuple-element.8, f32[16,72,128]{2,1,0:T(8,128)S(1)} %collective-permute-done.13), kind=kLoop, calls=%fused_computation.2 | loop fusion | flops 294912 | bytes 1474560 | tf_op jit(solution)/shard_map/convert_element_type | solution.py:348
  38.5 0.0 copy-done.3
  38.5 4.4 %all-to-all-start = ((bf16[16,72,128]{2,1,0:T(8,128)(2,1)}), bf16[16,72,128]{2,1,0:T(8,128)(2,1)S(1)}, u32[]{:S(2)}, u32[]{:S(2)}) async-start(bf16[16,72,128]{2,1,0:T(8,128)(2,1)} %add_convert_fusion), calls=%async_computation | async-start | bytes 589824 | tf_op jit(solution)/shard_map/all_to_all | solution.py:349
  42.9 0.0 copy-done.5
  42.9 2.0 %collective-permute-start.12 = (bf16[256,256]{1,0:T(8,128)(2,1)S(1)}, bf16[256,256]{1,0:T(8,128)(2,1)S(1)}, u32[]{:S(2)}, u32[]{:S(2)}) collective-permute-start(bf16[256,256]{1,0:T(8,128)(2,1)S(1)} %copy-done.5), channel_id=1, source_target_pairs={{0,8},{1,9},{2,10},{3,11},{4,12},{5,13},{6,14},{7,15},{8,0},{9,1},... | collective-permute-start | bytes 393224 | tf_op jit(solution)/shard_map/ppermute | solution.py:156
  44.9 5.5 %collective-permute-done.12 = bf16[256,256]{1,0:T(8,128)(2,1)S(1)} collective-permute-done((bf16[256,256]{1,0:T(8,128)(2,1)S(1)}, bf16[256,256]{1,0:T(8,128)(2,1)S(1)}, u32[]{:S(2)}, u32[]{:S(2)}) %collective-permute-start.12) | collective-permute-done | bytes 131104 | tf_op jit(solution)/shard_map/ppermute | solution.py:156
  50.5 0.0 copy-done.2
  50.5 4.0 %all-to-all-done = bf16[16,72,128]{2,1,0:T(8,128)(2,1)S(1)} async-done(((bf16[16,72,128]{2,1,0:T(8,128)(2,1)}), bf16[16,72,128]{2,1,0:T(8,128)(2,1)S(1)}, u32[]{:S(2)}, u32[]{:S(2)}) %all-to-all-start) | async-done | bytes 294944 | tf_op jit(solution)/shard_map/all_to_all | solution.py:349
  54.5 0.0 copy-start.8
  54.5 0.1 collective-permute-start.14
  54.6 0.7 %pad_maximum_fusion.1 = bf16[2,256,256]{2,1,0:T(8,128)(2,1)} fusion(bf16[1,256,256]{2,1,0:T(8,128)(2,1)S(1)} %get-tuple-element.11, bf16[1,256,256]{2,1,0:T(8,128)(2,1)S(1)} %get-tuple-element.10), kind=kLoop, calls=%fused_computation.3 | loop fusion | flops 131072 | bytes 524288 | tf_op jit(solution)/shard_map/stack | solution.py:346
  55.3 0.5 collective-permute-done.14.other_ref
  55.8 0.0 copy-done.8
  55.8 0.0 copy-start.9
  55.8 0.6 %copy-done.9 = f32[72,128]{1,0:T(8,128)} copy-done((f32[72,128]{1,0:T(8,128)}, f32[72,128]{1,0:T(8,128)S(1)}, u32[]{:S(2)}) %copy-start.9) | copy-done | bytes 36888
  56.4 1.4 %total.1 = f32[144,128]{1,0:T(8,128)} custom-call(s32[5]{0:T(128)} %copy-done.3, f32[72,128]{1,0:T(8,128)} %copy-done.8, f32[72,128]{1,0:T(8,128)} %copy-done.9), custom_call_target="tpu_custom_call" | custom-call | tf_op jit(solution)/shard_map/total/pallas_call | solution.py:351
  (7 shorter events, 0.1 us)
Async XLA Ops:
  0.6 29.6 %copy-start = (f32[360,4,256]{2,1,0:T(4,128)S(1)}, f32[360,4,256]{2,1,0:T(4,128)}, u32[]{:S(2)}) copy-start(f32[360,4,256]{2,1,0:T(4,128)} %param.7) | copy-start | bytes 4423684
  0.6 22.5 %copy-start.6 = (bf16[1,64,8,256]{3,2,1,0:T(8,128)(2,1)S(1)}, bf16[1,64,8,256]{3,2,1,0:T(8,128)(2,1)}, u32[]{:S(2)}) copy-start(bf16[1,64,8,256]{3,2,1,0:T(8,128)(2,1)} %param.5) | copy-start | bytes 786436
  0.7 23.7 %copy-start.7 = (bf16[1,64,8,256]{3,2,1,0:T(8,128)(2,1)S(1)}, bf16[1,64,8,256]{3,2,1,0:T(8,128)(2,1)}, u32[]{:S(2)}) copy-start(bf16[1,64,8,256]{3,2,1,0:T(8,128)(2,1)} %param.9) | copy-start | bytes 786436
  1.7 1.4 %collective-permute-start.4 = (bf16[2,72,128]{2,1,0:T(8,128)(2,1)S(1)}, bf16[2,72,128]{2,1,0:T(8,128)(2,1)S(1)}, u32[]{:S(2)}, u32[]{:S(2)}) collective-permute-start(bf16[2,72,128]{2,1,0:T(8,128)(2,1)S(1)} %broadcast_select_fusion), channel_id=1, source_target_pairs={{0,4},{1,5},{2,6},{3,7},{4,0},{5,1},{6,2},{7,3},{8,12},{9,13},{10,... | collective-permute-start | bytes 110600 | tf_op jit(solution)/shard_map/ppermute | solution.py:156
  3.2 7.0 %collective-permute-start.7 = (bf16[2,72,128]{2,1,0:T(8,128)(2,1)S(1)}, bf16[2,72,128]{2,1,0:T(8,128)(2,1)S(1)}, u32[]{:S(2)}, u32[]{:S(2)}) collective-permute-start(bf16[2,72,128]{2,1,0:T(8,128)(2,1)S(1)} %select_select_fusion), channel_id=1, source_target_pairs={{0,3},{1,2},{2,1},{3,0},{4,7},{5,6},{6,5},{7,4},{8,11},{9,10},{10,... | collective-permute-start | bytes 110600 | tf_op jit(solution)/shard_map/ppermute | solution.py:156
  8.2 4.9 %collective-permute-start.6 = (bf16[2,72,128]{2,1,0:T(8,128)(2,1)S(1)}, bf16[2,72,128]{2,1,0:T(8,128)(2,1)S(1)}, u32[]{:S(2)}, u32[]{:S(2)}) collective-permute-start(bf16[2,72,128]{2,1,0:T(8,128)(2,1)S(1)} %select_select_fusion), channel_id=1, source_target_pairs={{0,2},{1,3},{2,0},{3,1},{4,6},{5,7},{6,4},{7,5},{8,10},{9,11},{10,... | collective-permute-start | bytes 110600 | tf_op jit(solution)/shard_map/ppermute | solution.py:156
  8.2 4.9 %collective-permute-start.5 = (bf16[2,72,128]{2,1,0:T(8,128)(2,1)S(1)}, bf16[2,72,128]{2,1,0:T(8,128)(2,1)S(1)}, u32[]{:S(2)}, u32[]{:S(2)}) collective-permute-start(bf16[2,72,128]{2,1,0:T(8,128)(2,1)S(1)} %select_select_fusion), channel_id=1, source_target_pairs={{0,1},{1,0},{2,3},{3,2},{4,5},{5,4},{6,7},{7,6},{8,9},{9,8},{10,11... | collective-permute-start | bytes 110600 | tf_op jit(solution)/shard_map/ppermute | solution.py:156
  13.1 5.3 %collective-permute-start.9 = (bf16[4,2,72,128]{3,2,1,0:T(8,128)(2,1)S(1)}, bf16[4,2,72,128]{3,2,1,0:T(8,128)(2,1)S(1)}, u32[]{:S(2)}, u32[]{:S(2)}) collective-permute-start(bf16[4,2,72,128]{3,2,1,0:T(8,128)(2,1)S(1)} %get-tuple-element.17), channel_id=1, source_target_pairs={{0,8},{1,9},{2,10},{3,11},{4,12},{5,13},{6,14},{7,15},{8,0},{9,1},... | collective-permute-start | bytes 442376 | tf_op jit(solution)/shard_map/ppermute | solution.py:156
  14.7 6.2 %collective-permute-start.8 = (bf16[4,2,72,128]{3,2,1,0:T(8,128)(2,1)S(1)}, bf16[4,2,72,128]{3,2,1,0:T(8,128)(2,1)S(1)}, u32[]{:S(2)}, u32[]{:S(2)}) collective-permute-start(bf16[4,2,72,128]{3,2,1,0:T(8,128)(2,1)S(1)} %get-tuple-element.17), channel_id=1, source_target_pairs={{0,16},{1,17},{2,18},{3,19},{4,20},{5,21},{6,22},{7,23},{8,24},{9,... | collective-permute-start | bytes 442376 | tf_op jit(solution)/shard_map/ppermute | solution.py:156
  16.2 6.8 %collective-permute-start.10 = (bf16[4,2,72,128]{3,2,1,0:T(8,128)(2,1)S(1)}, bf16[4,2,72,128]{3,2,1,0:T(8,128)(2,1)S(1)}, u32[]{:S(2)}, u32[]{:S(2)}) collective-permute-start(bf16[4,2,72,128]{3,2,1,0:T(8,128)(2,1)S(1)} %get-tuple-element.17), channel_id=1, source_target_pairs={{0,24},{1,25},{2,26},{3,27},{4,28},{5,29},{6,30},{7,31},{8,16},{9,... | collective-permute-start | bytes 442376 | tf_op jit(solution)/shard_map/ppermute | solution.py:156
  23.0 8.9 %collective-permute-start.11 = (bf16[4,4,2,72,128]{4,3,2,1,0:T(8,128)(2,1)S(1)}, bf16[4,4,2,72,128]{4,3,2,1,0:T(8,128)(2,1)S(1)}, u32[]{:S(2)}, u32[]{:S(2)}) collective-permute-start(bf16[4,4,2,72,128]{4,3,2,1,0:T(8,128)(2,1)S(1)} %pad_maximum_fusion.refs_7_), channel_id=1, source_target_pairs={{0,4},{1,5},{2,6},{3,7},{4,0},{5,1},{6,2},{7,3},{8,12},{9,13},{10,... | collective-permute-start | bytes 1769480 | tf_op jit(solution)/shard_map/ppermute | solution.py:156
  23.1 6.4 %collective-permute-start = (bf16[256,256]{1,0:T(8,128)(2,1)S(1)}, bf16[256,256]{1,0:T(8,128)(2,1)S(1)}, u32[]{:S(2)}, u32[]{:S(2)}) collective-permute-start(bf16[256,256]{1,0:T(8,128)(2,1)S(1)} %get-tuple-element.14), channel_id=1, source_target_pairs={{0,8},{1,9},{2,10},{3,11},{4,12},{5,13},{6,14},{7,15},{8,0},{9,1},... | collective-permute-start | bytes 393224 | tf_op jit(solution)/shard_map/ppermute | solution.py:156
  24.2 6.1 %collective-permute-start.2 = (bf16[256,256]{1,0:T(8,128)(2,1)S(1)}, bf16[256,256]{1,0:T(8,128)(2,1)S(1)}, u32[]{:S(2)}, u32[]{:S(2)}) collective-permute-start(bf16[256,256]{1,0:T(8,128)(2,1)S(1)} %get-tuple-element.15.refs_1_), channel_id=1, source_target_pairs={{0,4},{1,5},{2,6},{3,7},{4,0},{5,1},{6,2},{7,3},{8,12},{9,13},{10,... | collective-permute-start | bytes 393224 | tf_op jit(solution)/shard_map/ppermute | solution.py:156
  25.1 6.8 %collective-permute-start.1 = (bf16[256,256]{1,0:T(8,128)(2,1)}, bf16[256,256]{1,0:T(8,128)(2,1)S(1)}, u32[]{:S(2)}, u32[]{:S(2)}) collective-permute-start(bf16[256,256]{1,0:T(8,128)(2,1)} %get-tuple-element.12), channel_id=1, source_target_pairs={{0,8},{1,9},{2,10},{3,11},{4,12},{5,13},{6,14},{7,15},{8,0},{9,1},... | collective-permute-start | bytes 393224 | tf_op jit(solution)/shard_map/ppermute | solution.py:156
  29.5 2.4 %collective-permute-start.3 = (bf16[256,256]{1,0:T(8,128)(2,1)S(1)}, bf16[256,256]{1,0:T(8,128)(2,1)S(1)}, u32[]{:S(2)}, u32[]{:S(2)}) collective-permute-start(bf16[256,256]{1,0:T(8,128)(2,1)S(1)} %collective-permute-done.refs_2_), channel_id=1, source_target_pairs={{0,4},{1,5},{2,6},{3,7},{4,0},{5,1},{6,2},{7,3},{8,12},{9,13},{10,... | collective-permute-start | bytes 393224 | tf_op jit(solution)/shard_map/ppermute | solution.py:156
  30.3 8.2 %copy-start.3 = (s32[5]{0:T(128)}, s32[5]{0:T(128)S(1)}, u32[]{:S(2)}) copy-start(s32[5]{0:T(128)S(1)} %stack.62.refs_0_.where_ref) | copy-start | bytes 64
  34.4 0.7 %copy-start.1 = (bf16[256,256]{1,0:T(8,128)(2,1)}, bf16[256,256]{1,0:T(8,128)(2,1)S(1)}, u32[]{:S(2)}) copy-start(bf16[256,256]{1,0:T(8,128)(2,1)S(1)} %get-tuple-element.6) | copy-start | bytes 393220
  35.0 0.6 %copy-start.4 = (bf16[256,256]{1,0:T(8,128)(2,1)}, bf16[256,256]{1,0:T(8,128)(2,1)S(1)}, u32[]{:S(2)}) copy-start(bf16[256,256]{1,0:T(8,128)(2,1)S(1)} %get-tuple-element.7) | copy-start | bytes 393220
  35.7 7.2 %copy-start.5 = (bf16[256,256]{1,0:T(8,128)(2,1)S(1)}, bf16[256,256]{1,0:T(8,128)(2,1)}, u32[]{:S(2)}) copy-start(bf16[256,256]{1,0:T(8,128)(2,1)} %copy-done.4) | copy-start | bytes 393220
  35.7 14.8 %copy-start.2 = (bf16[256,256]{1,0:T(8,128)(2,1)S(1)}, bf16[256,256]{1,0:T(8,128)(2,1)}, u32[]{:S(2)}) copy-start(bf16[256,256]{1,0:T(8,128)(2,1)} %copy-done.1) | copy-start | bytes 393220
  35.7 2.0 %collective-permute-start.13 = (f32[16,72,128]{2,1,0:T(8,128)S(1)}, f32[16,72,128]{2,1,0:T(8,128)S(1)}, u32[]{:S(2)}, u32[]{:S(2)}) collective-permute-start(f32[16,72,128]{2,1,0:T(8,128)S(1)} %get-tuple-element.9), channel_id=1, source_target_pairs={{0,4},{1,5},{2,6},{3,7},{4,0},{5,1},{6,2},{7,3},{8,12},{9,13},{10,... | collective-permute-start | bytes 1769480 | tf_op jit(solution)/shard_map/ppermute | solution.py:156
  38.5 16.0 %all-to-all-start = ((bf16[16,72,128]{2,1,0:T(8,128)(2,1)}), bf16[16,72,128]{2,1,0:T(8,128)(2,1)S(1)}, u32[]{:S(2)}, u32[]{:S(2)}) async-start(bf16[16,72,128]{2,1,0:T(8,128)(2,1)} %add_convert_fusion), calls=%async_computation | async-start | bytes 589824 | tf_op jit(solution)/shard_map/all_to_all | solution.py:349
  42.9 7.5 %collective-permute-start.12 = (bf16[256,256]{1,0:T(8,128)(2,1)S(1)}, bf16[256,256]{1,0:T(8,128)(2,1)S(1)}, u32[]{:S(2)}, u32[]{:S(2)}) collective-permute-start(bf16[256,256]{1,0:T(8,128)(2,1)S(1)} %copy-done.5), channel_id=1, source_target_pairs={{0,8},{1,9},{2,10},{3,11},{4,12},{5,13},{6,14},{7,15},{8,0},{9,1},... | collective-permute-start | bytes 393224 | tf_op jit(solution)/shard_map/ppermute | solution.py:156
  54.5 1.3 %copy-start.8 = (f32[72,128]{1,0:T(8,128)}, f32[72,128]{1,0:T(8,128)S(1)}, u32[]{:S(2)}) copy-start(f32[72,128]{1,0:T(8,128)S(1)} %convert_reduce_fusion.own_ref) | copy-start | bytes 110596
  54.5 1.3 %collective-permute-start.14 = (f32[72,128]{1,0:T(8,128)S(1)}, f32[72,128]{1,0:T(8,128)S(1)}, u32[]{:S(2)}, u32[]{:S(2)}) collective-permute-start(f32[72,128]{1,0:T(8,128)S(1)} %convert_reduce_fusion.own_ref), channel_id=1, source_target_pairs={{0,4},{1,5},{2,6},{3,7},{4,0},{5,1},{6,2},{7,3},{8,12},{9,13},{10,... | collective-permute-start | bytes 110600 | tf_op jit(solution)/shard_map/ppermute | solution.py:156
  55.8 0.6 %copy-start.9 = (f32[72,128]{1,0:T(8,128)}, f32[72,128]{1,0:T(8,128)S(1)}, u32[]{:S(2)}) copy-start(f32[72,128]{1,0:T(8,128)S(1)} %collective-permute-done.14.other_ref) | copy-start | bytes 110596

commit v2 on v0

--- a/solution.py
+++ b/solution.py
@@ -3,10 +3,13 @@
 import jax
 import jax.numpy as jnp
 from jax import lax
+from jax.experimental import pallas as pl
+from jax.experimental.pallas import tpu as pltpu
 from jax.sharding import PartitionSpec as P
 
 FIRST_DILATION = 64
 SECOND_DILATION = 128
+AXES = ("lead", "gy", "gx")
 
 
 def passed_along(value, axis, steps):
@@ -63,20 +66,16 @@
     return (cols, jnp.concatenate(blocks, axis=0))
 
 
-def shards(inputs, lead_ids, film, flat_weights, cotangent):
+def general_shards(inputs, lead_ids, film, flat_weights, cotangent):
     tile_row_count, tile_column_count, patch_width = (
         inputs.shape[1],
         inputs.shape[2],
         inputs.shape[3],
     )
-    gathered = lax.all_gather(flat_weights, ("lead", "gy", "gx"), axis=1, tiled=True)
+    gathered = lax.all_gather(flat_weights, AXES, axis=1, tiled=True)
     weight_a = gathered[0].reshape(3, 3, patch_width, patch_width)
     weight_b = gathered[1].reshape(3, 3, patch_width, patch_width)
-    table_rows = film.shape[0]
-    picker = (jnp.arange(table_rows, dtype=jnp.int32) == lead_ids[0]).astype(jnp.float32)
-    film_row = jnp.dot(
-        picker, film.reshape(table_rows, -1), precision=lax.Precision.HIGHEST
-    ).reshape(4, patch_width)
+    film_row = lax.dynamic_index_in_dim(film, lead_ids[0], 0, keepdims=False)
     mult_a = 1.0 + film_row[0]
     shift_a = film_row[1]
     mult_b = 1.0 + film_row[2]
@@ -112,9 +111,7 @@
     column_gradient, matrix_t = lower(taps_grad, weight_b, True)
     back = upstream + jnp.dot(column_gradient, matrix_t, preferred_element_type=jnp.float32)
     grad_a = (back * mult_a * sig_a * (1.0 + pre_a * (1.0 - sig_a))).astype(jnp.bfloat16)
-    scale = 1.0 / math.sqrt(
-        lax.axis_size(("lead", "gy", "gx")) * tile_row_count * tile_column_count
-    )
+    scale = 1.0 / math.sqrt(lax.axis_size(AXES) * tile_row_count * tile_column_count)
     products = (
         lax.dot_general(
             input_columns, grad_a, (((0,), (0,)), ((), ())), preferred_element_type=jnp.float32
@@ -132,17 +129,366 @@
     return (outputs.reshape(inputs.shape), total.reshape(-1))
 
 
+def fits(mesh, rows, columns):
+    size = mesh.shape
+    return (
+        tuple(mesh.axis_names) == AXES
+        and (size["lead"], size["gy"], size["gx"]) == (2, 4, 4)
+        and FIRST_DILATION == rows
+        and SECOND_DILATION == 2 * rows
+        and FIRST_DILATION // columns >= size["gx"]
+    )
+
+
+def pairs(move):
+    number = lambda x, y, c, z: x * 16 + (2 * y + c) * 4 + z
+    return [
+        (number(x, y, c, z), number(*move(x, y, c, z)))
+        for x in range(2)
+        for y in range(2)
+        for c in range(2)
+        for z in range(4)
+    ]
+
+
+def moved(value, dx=0, dy=0, dc=0, dz=0):
+    return lax.ppermute(
+        value, AXES, pairs(lambda x, y, c, z: (x ^ dx, y ^ dy, c ^ dc, z ^ dz))
+    )
+
+
+Z_ORDER = (3, 2, 1)
+PLANE_ORDER = ((1, 1), (1, 0), (0, 1))
+
+
+def place():
+    x, gy, z = (lax.axis_index(axis) for axis in AXES)
+    return x, gy // 2, gy % 2, z
+
+
+def used_rows(width, shard_rows):
+    found = []
+    for block in range(3):
+        start = (3 * block + 1) * width
+        row = start
+        while row < start + width:
+            shard = row // shard_rows
+            stop = min((shard + 1) * shard_rows, start + width)
+            place = (shard // 16, shard // 8 % 2, shard // 4 % 2, shard % 4)
+            found.append((*place, row - shard * shard_rows, stop - row, block * width + row - start))
+            row = stop
+    return found
+
+
+def chosen(table, here, otherwise):
+    value = otherwise
+    for key, entry in table.items():
+        if entry != otherwise:
+            match = here[0] == key[0]
+            for mine, wanted in zip(here[1:], key[1:]):
+                match = match & (mine == wanted)
+            value = jnp.where(match, entry, value)
+    return value
+
+
+class Layout:
+    def __init__(self, width, shard_rows):
+        self.pieces = used_rows(width, shard_rows)
+        self.start, self.count, self.base, self.first, self.stop = {}, {}, {}, {}, {}
+        for cx, cy, cc, cz, first, count, row in self.pieces:
+            self.start[cx, cy] = min(self.start.get((cx, cy), 3 * width), row)
+            self.count[cx, cy] = self.count.get((cx, cy), 0) + count
+        for cx, cy, cc, cz, first, count, row in self.pieces:
+            self.base[cx, cy, cz, cc] = row - self.start[cx, cy] - first
+            self.first[cx, cy, cz, cc] = first
+            self.stop[cx, cy, cz, cc] = first + count
+        self.low = {
+            key[:3]: stop for key, stop in self.stop.items() if key[3] == 1
+        }
+        for key, first in self.first.items():
+            assert key[3] == 1 or self.low.get(key[:3], 0) <= first
+        self.column_rows = max(self.count.values())
+        assert all(start + self.column_rows <= 3 * width for start in self.start.values())
+        assert len(self.base) == len(self.pieces)
+
+
+def line_kernel(layout, own_ref, far0_ref, far1_ref, far2_ref, out_ref, total):
+    x, y, c, z = place()
+    rows = own_ref.shape[1]
+    total[...] = jnp.zeros_like(total)
+    row = lax.broadcasted_iota(jnp.int32, own_ref.shape[1:], 0)
+    for dz, ref in zip((0, *Z_ORDER), (own_ref, far0_ref, far1_ref, far2_ref)):
+        for core in range(2):
+            here = (x, y, z ^ dz, core)
+            first, stop = chosen(layout.first, here, 0), chosen(layout.stop, here, 0)
+            base = pl.multiple_of(rows + chosen(layout.base, here, -rows), 8)
+            used = (row >= first) & (row < stop)
+            for k in range(2):
+                value = jnp.where(used, ref[k].astype(jnp.float32), 0.0)
+                total[k, pl.ds(base, rows), :] += value
+    out_ref[...] = total[:, rows : rows + out_ref.shape[1], :].astype(out_ref.dtype)
+
+
+def slot(dx, dy):
+    found = 0
+    for number, (to_x, to_y) in enumerate(PLANE_ORDER):
+        found = jnp.where((dx == to_x) & (dy == to_y), number + 1, found)
+    return found
+
+
+def matrix(layout, own_ref, near_ref):
+    x, y, c, z = place()
+    halves = []
+    for ref in (own_ref, near_ref):
+        parts = [
+            ref[slot(cx ^ x, cy ^ y)][: layout.count[cx, cy]]
+            for cx, cy in sorted(layout.start, key=layout.start.get)
+        ]
+        halves.append(jnp.concatenate(parts, axis=0))
+    own, near = halves
+    return jnp.concatenate([jnp.where(c == 0, own, near), jnp.where(c == 0, near, own)], axis=1)
+
+
+def dot(a, b, dims=((1,), (0,))):
+    return lax.dot_general(a, b, (dims, ((), ())), preferred_element_type=jnp.float32)
+
+
+def first_kernel(
+    layout, mine_ref, other_ref, near0_ref, near1_ref, own_w, near_w, film_ref,
+    field_ref, pre_ref, hidden_ref,
+):
+    x, y, c, z = place()
+    half, width = mine_ref.shape
+    near0, near1 = near0_ref[...], near1_ref[...]
+    mine, other = mine_ref[...], other_ref[0]
+    lo, hi = jnp.where(y == 0, mine, other), jnp.where(y == 0, other, mine)
+    near_lo, near_hi = jnp.where(y == 0, near0, near1), jnp.where(y == 0, near1, near0)
+    field_ref[0] = jnp.zeros_like(lo)
+    field_ref[1] = jnp.where(c == 0, lo, near_lo)
+    field_ref[2] = jnp.where(c == 0, near_lo, lo)
+    field_ref[3] = jnp.where(c == 0, hi, near_hi)
+    field_ref[4] = jnp.where(c == 0, near_hi, hi)
+    field_ref[5] = jnp.zeros_like(lo)
+    above = jnp.concatenate([field_ref[c], field_ref[c + 2]], axis=0)
+    mid = jnp.concatenate([lo, hi], axis=0)
+    below = jnp.concatenate([field_ref[c + 2], field_ref[c + 4]], axis=0)
+    weight = matrix(layout, own_w, near_w)
+    conv = dot(above, weight[:width]) + dot(mid, weight[width : 2 * width])
+    conv = conv + dot(below, weight[2 * width :])
+    pre = conv * (1.0 + film_ref[0:1, :]) + film_ref[1:2, :]
+    pre_ref[...] = pre
+    hidden_ref[...] = (mid.astype(jnp.float32) + pre * jax.nn.sigmoid(pre)).astype(hidden_ref.dtype)
+
+
+def second_kernel(
+    layout, pre_ref, hidden_ref, mine_ct, other_ref, own_w, near_w, film_ref,
+    out_keep, out_send, grad_keep, grad_send,
+):
+    x, y, c, z = place()
+    half, width = mine_ct.shape
+    f32, bf16 = jnp.float32, jnp.bfloat16
+    lane = width // 2
+    mult_a = 1.0 + film_ref[0:1, :]
+    mult_b = 1.0 + film_ref[2:3, :]
+    weight = matrix(layout, own_w, near_w)
+    up, centre, down = weight[:width], weight[width : 2 * width], weight[2 * width :]
+    hidden = hidden_ref[...]
+    across = jnp.concatenate([dot(hidden[half:], down), dot(hidden[:half], up)], axis=0)
+    pre_b = (dot(hidden, centre) + across) * mult_b + film_ref[3:4, :]
+    sig_b = jax.nn.sigmoid(pre_b)
+    result = (hidden.astype(f32) + pre_b * sig_b).astype(bf16)
+    out_keep[...] = jnp.where(y == 0, result[:half], result[half:])
+    out_send[...] = jnp.where(y == 0, result[half:], result[:half])
+    mine, other = mine_ct[...], other_ref[1]
+    lo, hi = jnp.where(y == 0, mine, other), jnp.where(y == 0, other, mine)
+    upstream = jnp.concatenate([lo, hi], axis=0).astype(f32)
+    grad_b = (upstream * mult_b * sig_b * (1.0 + pre_b * (1.0 - sig_b))).astype(bf16)
+    turned = ((1,), (1,))
+    back = jnp.concatenate(
+        [dot(grad_b[half:], up, turned), dot(grad_b[:half], down, turned)], axis=0
+    )
+    back = upstream + dot(grad_b, centre, turned) + back
+    pre_a = pre_ref[...]
+    sig_a = jax.nn.sigmoid(pre_a)
+    grad_a = (back * mult_a * sig_a * (1.0 + pre_a * (1.0 - sig_a))).astype(bf16)
+    grad_keep[...] = jnp.where(c == 0, grad_a[:, :lane], grad_a[:, lane:])
+    grad_send[...] = jnp.where(c == 0, grad_a[:, lane:], grad_a[:, :lane])
+
+
+def term_kernel(
+    layout, scale, field_ref, keep_ref, near_ref, own_ref, far0_ref, far1_ref, far2_ref, total
+):
+    x, y, c, z = place()
+    half, width = field_ref.shape[1:]
+    keep, near = keep_ref[...], near_ref[...]
+    even, odd = jnp.where(c == 0, keep, near), jnp.where(c == 0, near, keep)
+    grad = jnp.concatenate([even[:half], odd[:half], even[half:], odd[half:]], axis=0)
+    field = jnp.concatenate([field_ref[tile] for tile in range(1, 5)], axis=0)
+    over = ((0,), (0,))
+    total[:width, :] = dot(field[: 3 * half], grad[half:], over) * scale
+    total[width : 2 * width, :] = dot(field, grad, over) * scale
+    total[2 * width :, :] = dot(field[half:], grad[: 3 * half], over) * scale
+    rows = own_ref.shape[0]
+    for (dx, dy), ref in zip(((0, 0), *PLANE_ORDER), (own_ref, far0_ref, far1_ref, far2_ref)):
+        start = pl.multiple_of(chosen(layout.start, (x ^ dx, y ^ dy), 0), 8)
+        ref[...] = total[pl.ds(start, rows), :].astype(ref.dtype)
+
+
+def chip_kernel(layout, own_ref, far0_ref, far1_ref, far2_ref, out0, out1, out2, out3, total):
+    x, y, c, z = place()
+    f32 = jnp.float32
+    rows, lane = own_ref.shape
+    piece_rows = out0.shape[0]
+    value = own_ref[...]
+    for ref in (far0_ref, far1_ref, far2_ref):
+        value = value + ref[...].astype(f32)
+    row = lax.broadcasted_iota(jnp.int32, value.shape, 0)
+    edge = jnp.zeros((piece_rows, lane), f32)
+    total[0:piece_rows, :] = edge
+    held = row < chosen(layout.count, (x, y), 0)
+    total[piece_rows : piece_rows + rows, :] = jnp.where(held, value, 0.0)
+    total[piece_rows + rows :, :] = edge
+    for dz, ref in zip((0, *Z_ORDER), (out0, out1, out2, out3)):
+        ends = []
+        for core in range(2):
+            base = piece_rows + chosen(layout.base, (x, y, z ^ dz, core), -piece_rows)
+            ends.append(total[pl.ds(pl.multiple_of(base, 8), piece_rows), :])
+        ref[...] = (ends[0] + ends[1]).astype(ref.dtype)
+
+
+def last_kernel(layout, own_ref, other_ref, out_ref):
+    x, y, c, z = place()
+    rows = own_ref.shape[0]
+    row = lax.broadcasted_iota(jnp.int32, own_ref.shape, 0)
+    held = jnp.logical_xor(row < chosen(layout.low, (x, y, z), 0), c == 0)
+    own = jnp.where(held, own_ref[...], 0.0)
+    other = jnp.where(held, other_ref[...], 0.0)
+    out_ref[pl.ds(0, rows, stride=2), :] = jnp.where(c == 0, own, other)
+    out_ref[pl.ds(1, rows, stride=2), :] = jnp.where(c == 0, other, own)
+
+
+def row_shards(inputs, lead_ids, film, flat_weights, cotangent):
+    rows, columns, width = inputs.shape[1:]
+    half = rows // 2 * columns
+    lane = width // 2
+    shard_rows = flat_weights.shape[1] // width
+    x, y, c, z = place()
+    layout = Layout(width, shard_rows)
+    bf16, f32 = jnp.bfloat16, jnp.float32
+    shape = jax.ShapeDtypeStruct
+
+    def call(name, body, out_shape, scratch, *operands, space=pltpu.VMEM, mib=16):
+        vmem = pl.BlockSpec(memory_space=pltpu.VMEM)
+        several = isinstance(out_shape, tuple)
+        return pl.pallas_call(
+            lambda *refs: body(layout, *refs),
+            out_shape=out_shape,
+            in_specs=[pl.BlockSpec(memory_space=space)] * len(operands),
+            out_specs=(vmem,) * len(out_shape) if several else vmem,
+            scratch_shapes=scratch,
+            compiler_params=pltpu.CompilerParams(vmem_limit_bytes=mib * 1024 * 1024),
+            name=name,
+        )(*operands)
+
+    shard = flat_weights.reshape(2, shard_rows, width)
+    left, right = shard[:, :, :lane], shard[:, :, lane:]
+    near = moved(jnp.where(c == 0, right, left), dc=1)
+    row = lax.broadcasted_iota(jnp.int32, near.shape, 1)
+    from_one = row < chosen(layout.low, (x, y, z), 0)
+    piece = jnp.where(from_one == (c == 1), jnp.where(c == 0, left, right), near)
+
+    halves_x, halves_ct = (array.reshape(2, half, width) for array in (inputs, cotangent))
+    pick = lambda halves, number: lax.dynamic_index_in_dim(halves, number, 0, keepdims=False)
+    other = moved(jnp.stack([pick(halves_x, 1 - y), pick(halves_ct, 1 - y)]), dy=1)
+    line = [piece, *(moved(piece, dz=dz) for dz in Z_ORDER)]
+    *line, other, halves_x, halves_ct, film = lax.optimization_barrier(
+        (*line, other, halves_x, halves_ct, film)
+    )
+    mine_x, mine_ct = pick(halves_x, y), pick(halves_ct, y)
+    film_row = lax.dynamic_index_in_dim(film, lead_ids[0], 0, keepdims=False)
+    near_x0 = moved(mine_x, dc=1)
+    line = call(
+        "line",
+        line_kernel,
+        shape((2, layout.column_rows, lane), bf16),
+        [pltpu.VMEM((2, layout.column_rows + 2 * shard_rows, lane), f32)],
+        *line,
+    )
+    near_x1 = moved(other[0], dc=1)
+    plane = [line, *(moved(line, dx=dx, dy=dy) for dx, dy in PLANE_ORDER)]
+    *plane, near_x0, near_x1, mine_x, mine_ct, film_row = lax.optimization_barrier(
+        (*plane, near_x0, near_x1, mine_x, mine_ct, film_row)
+    )
+    own_a, own_b = (jnp.stack([column[k] for column in plane]) for k in range(2))
+    near_a, near_b = moved(own_a, dc=1), moved(own_b, dc=1)
+
+    field, pre_a, hidden = call(
+        "block_one",
+        first_kernel,
+        (shape((6, half, width), bf16), shape((2 * half, width), f32), shape((2 * half, width), bf16)),
+        [],
+        *(mine_x, other, near_x0, near_x1, own_a, near_a, film_row),
+    )
+    out_keep, out_send, grad_keep, grad_send = call(
+        "block_two",
+        second_kernel,
+        (shape((half, width), bf16),) * 2 + (shape((2 * half, lane), bf16),) * 2,
+        [],
+        *(pre_a, hidden, mine_ct, other, own_b, near_b, film_row),
+    )
+
+    scale = 1.0 / math.sqrt(lax.axis_size(AXES) * rows * columns)
+    column = call(
+        "terms",
+        lambda layout, *refs: term_kernel(layout, scale, *refs),
+        (shape((layout.column_rows, lane), f32),) + (shape((layout.column_rows, lane), bf16),) * 3,
+        [pltpu.VMEM((3 * width, lane), f32)],
+        *(field, grad_keep, moved(grad_send, dc=1)),
+    )
+    other_out = moved(out_send, dy=1)
+    column = [column[0], *(moved(term, dx=dx, dy=dy) for term, (dx, dy) in zip(column[1:], PLANE_ORDER))]
+    chip = call(
+        "chips",
+        chip_kernel,
+        (shape((shard_rows, lane), f32),) + (shape((shard_rows, lane), bf16),) * 3,
+        [pltpu.VMEM((layout.column_rows + 2 * shard_rows, lane), f32)],
+        *column,
+    )
+    lane_sum = chip[0]
+    for term, dz in reversed(list(zip(chip[1:], Z_ORDER))):
+        lane_sum = lane_sum + moved(term, dz=dz).astype(f32)
+
+    first = jnp.where(y == 0, out_keep, other_out)
+    second = jnp.where(y == 0, other_out, out_keep)
+    outputs = jnp.stack([first, second]).reshape(inputs.shape)
+
+    total = call(
+        "total",
+        last_kernel,
+        shape((2 * shard_rows, lane), f32),
+        [],
+        *(lane_sum, moved(lane_sum, dc=1)),
+    )
+    return (outputs, total.reshape(-1))
+
+
 def solution(mesh):
-    return jax.shard_map(
-        shards,
-        mesh=mesh,
-        in_specs=(
-            P("lead", "gy", "gx", None),
-            P("lead"),
-            P(),
-            P(None, ("lead", "gy", "gx")),
-            P("lead", "gy", "gx", None),
-        ),
-        out_specs=(P("lead", "gy", "gx", None), P(("lead", "gy", "gx"))),
-        check_vma=False,
-    )
+    def whole(inputs, lead_ids, film, flat_weights, cotangent):
+        size = mesh.shape
+        rows, columns = inputs.shape[1] // size["gy"], inputs.shape[2] // size["gx"]
+        plan = row_shards if fits(mesh, rows, columns) else general_shards
+        return jax.shard_map(
+            plan,
+            mesh=mesh,
+            in_specs=(
+                P("lead", "gy", "gx", None),
+                P("lead"),
+                P(),
+                P(None, AXES),
+                P("lead", "gy", "gx", None),
+            ),
+            out_specs=(P("lead", "gy", "gx", None), P(AXES)),
+            check_vma=False,
+        )(inputs, lead_ids, film, flat_weights, cotangent)
+
+    return whole

time: 251 us -> 44.9 us (0.18)
  waiting for transfers between devices: 168 us -> 16.1 us
  local copies, waits for them, and re-layouts: 43.7 us -> 2.12 us
  between operations: 14.6 us -> 1.51 us
  matrix products: 7.43 us -> 0 us
  starting transfers between devices: 17.1 us -> 21.3 us
  Pallas kernels: 0 us -> 2.71 us
    unnamed x4 -> x0, waiting for transfers between devices: 55.2 us -> none
    all_gather x1 -> x0, waiting for transfers between devices: 55 us -> none  [shards(): lax.all_gather(flat_weights, ('lead', 'gy', 'gx'), axis=1, tiled=True)]
    reduce_scatter x1 -> x0, waiting for transfers between devices: 48.9 us -> none  [shards(): lax.psum_scatter(flat_term, 'gx', scatter_dimension=1, tiled=True)]
    slice x1 -> x4, local copies, waits for them, and re-layouts: 26.3 us -> 0.04 us  [row_shards(): column[k]]
    dot_general x4 -> x0, matrix products: 7.43 us -> none  [the longest x1 2.4 us: shards(): jnp.dot(input_columns, matrix_a, preferred_element_type=jnp.float32)]
    ppermute x6 -> x21, waiting for transfers between devices: 9.05 us -> 16.1 us  [moved(): lax.ppermute(value, AXES, pairs(lambda x, y, c, z: (x ^ dx, y ^ dy, c ^ d...]
    reshape x2 -> x0, local copies, waits for them, and re-layouts: 6.7 us -> none  [shards(): term.reshape(lax.axis_size(('lead', 'gy')), lax.axis_size('gx'), -1)]
    ppermute x6 -> x21, starting transfers between devices: 17 us -> 21.3 us  [moved(): lax.ppermute(value, AXES, pairs(lambda x, y, c, z: (x ^ dx, y ^ dy, c ^ d...]
  transfers between devices with their start and end apart: 9 -> 21, of which waited for: 7 -> 13; matrix products, arithmetic and copies ran while one was open for 12% -> 4% of each run, Pallas kernels for 0% -> 2%
where the time goes in v2:
time: 44.9 us; the launch traced here: 44.8 us
  starting transfers between devices  21.3 us (47%)
  waiting for transfers between devices  16.1 us (36%)
  Pallas kernels  2.71 us (6%)
  local copies, waits for them, and re-layouts  2.12 us (5%)
  between operations  1.51 us (3%)
  other arithmetic  0.96 us (2%)
    ppermute x21, starting transfers between devices, moved(): lax.ppermute(value, AXES, pairs(lambda x, y, c, z: (x ^ dx, y ^ dy, c ^ d...  21.3 us
    ppermute x21, waiting for transfers between devices, moved(): lax.ppermute(value, AXES, pairs(lambda x, y, c, z: (x ^ dx, y ^ dy, c ^ d...  16.1 us
    pallas_call x6, Pallas kernels, call(): pl.pallas_call(lambda *refs: body(layout, *refs), out_shape=out_shape, in...  2.71 us
    unnamed x7, local copies, waits for them, and re-layouts  1.06 us
    dynamic_slice x1, local copies, waits for them, and re-layouts, row_shards(): lax.dynamic_index_in_dim(halves, number, 0, keepdims=False)  0.98 us
  transfers between devices with their start and end apart: 21, of which 13 were waited for; matrix products, arithmetic and copies ran while one was open for 4% of the time, Pallas kernels for 2%

profile of v2, /device:TPU:0, one launch (start us, length us, event | category | flops | bytes accessed | tf_op | source)
XLA Modules:
  0.0 44.8 jit_solution(14343440911200896462)
XLA Ops:
  0.6 0.0 copy-start
  0.6 0.0 copy-start.2
  0.7 0.0 copy-start.1
  0.7 1.0 %copy.9 = bf16[1,2,72,256]{3,2,1,0:T(8,128)(2,1)S(1)} copy(bf16[1,2,72,256]{3,1,2,0:T(2,128)(2,1)} %bitcast.31) | data formatting | bytes 147456
  1.7 0.5 %collective-permute-start = (bf16[2,72,128]{2,1,0:T(8,128)(2,1)S(1)}, bf16[2,72,128]{2,1,0:T(8,128)(2,1)S(1)}, u32[]{:S(2)}, u32[]{:S(2)}) collective-permute-start(bf16[2,72,128]{2,1,0:T(8,128)(2,1)S(1)} %broadcast_select_fusion), channel_id=1, source_target_pairs={{0,4},{1,5},{2,6},{3,7},{4,0},{5,1},{6,2},{7,3},{8,12},{9,13},{10,... | collective-permute-start | bytes 110600 | tf_op jit(solution)/shard_map/ppermute | solution.py:155
  2.3 1.0 %constant_dynamic-slice_fusion = (bf16[1,256,256]{2,1,0:T(8,128)(2,1)S(1)}, bf16[1,256,256]{2,1,0:T(8,128)(2,1)S(1)}) fusion(bf16[2,256,256]{2,1,0:T(8,128)(2,1)} %bitcast.28, s32[]{:T(128)S(6)} %select_n.89, bf16[2,256,256]{2,1,0:T(8,128)(2,1)} %bitcast.26), kind=kLoop, calls=%fused_computation.15 | loop fusion | bytes 524292 | tf_op jit(solution)/shard_map/jit(dynamic_index_in_dim)/dynamic_slice | solution.py:401
  3.3 2.6 %collective-permute-start.4 = (bf16[2,256,256]{2,1,0:T(8,128)(2,1)S(1)}, bf16[2,256,256]{2,1,0:T(8,128)(2,1)S(1)}, u32[]{:S(2)}, u32[]{:S(2)}) collective-permute-start(bf16[2,256,256]{2,1,0:T(8,128)(2,1)S(1)} %pad_maximum_fusion), channel_id=1, source_target_pairs={{0,8},{1,9},{2,10},{3,11},{4,12},{5,13},{6,14},{7,15},{8,0},{9,1},... | collective-permute-start | bytes 786440 | tf_op jit(solution)/shard_map/ppermute | solution.py:155
  5.9 0.0 collective-permute-done
  5.9 0.1 select_select_fusion.refs_0_
  6.0 3.7 %collective-permute-start.1 = (bf16[2,72,128]{2,1,0:T(8,128)(2,1)S(1)}, bf16[2,72,128]{2,1,0:T(8,128)(2,1)S(1)}, u32[]{:S(2)}, u32[]{:S(2)}) collective-permute-start(bf16[2,72,128]{2,1,0:T(8,128)(2,1)S(1)} %select_select_fusion.refs_0_), channel_id=1, source_target_pairs={{0,3},{1,2},{2,1},{3,0},{4,7},{5,6},{6,5},{7,4},{8,11},{9,10},{10,... | collective-permute-start | bytes 110600 | tf_op jit(solution)/shard_map/ppermute | solution.py:155
  9.7 0.0 collective-permute-start.2
  9.7 0.8 %collective-permute-start.3 = (bf16[2,72,128]{2,1,0:T(8,128)(2,1)S(1)}, bf16[2,72,128]{2,1,0:T(8,128)(2,1)S(1)}, u32[]{:S(2)}, u32[]{:S(2)}) collective-permute-start(bf16[2,72,128]{2,1,0:T(8,128)(2,1)S(1)} %select_select_fusion.refs_0_), channel_id=1, source_target_pairs={{0,1},{1,0},{2,3},{3,2},{4,5},{5,4},{6,7},{7,6},{8,9},{9,8},{10,11... | collective-permute-start | bytes 110600 | tf_op jit(solution)/shard_map/ppermute | solution.py:155
  11.1 0.7 %collective-permute-done.1.refs_1_ = bf16[2,72,128]{2,1,0:T(8,128)(2,1)S(1)} collective-permute-done((bf16[2,72,128]{2,1,0:T(8,128)(2,1)S(1)}, bf16[2,72,128]{2,1,0:T(8,128)(2,1)S(1)}, u32[]{:S(2)}, u32[]{:S(2)}) %collective-permute-start.1) | collective-permute-done | bytes 36896 | tf_op jit(solution)/shard_map/ppermute | solution.py:155
  11.8 2.7 %collective-permute-done.2.refs_2_ = bf16[2,72,128]{2,1,0:T(8,128)(2,1)S(1)} collective-permute-done((bf16[2,72,128]{2,1,0:T(8,128)(2,1)S(1)}, bf16[2,72,128]{2,1,0:T(8,128)(2,1)S(1)}, u32[]{:S(2)}, u32[]{:S(2)}) %collective-permute-start.2) | collective-permute-done | bytes 36896 | tf_op jit(solution)/shard_map/ppermute | solution.py:155
  14.5 0.0 collective-permute-done.3.refs_3_
  14.5 0.0 collective-permute-done.4.refs_1_.refs_3_
  14.5 0.1 line.1
  14.7 1.5 %collective-permute-start.5 = (bf16[2,256,128]{2,1,0:T(8,128)(2,1)S(1)}, bf16[2,256,128]{2,1,0:T(8,128)(2,1)S(1)}, u32[]{:S(2)}, u32[]{:S(2)}) collective-permute-start(bf16[2,256,128]{2,1,0:T(8,128)(2,1)S(1)} %line.1), channel_id=1, source_target_pairs={{0,24},{1,25},{2,26},{3,27},{4,28},{5,29},{6,30},{7,31},{8,16},{9,... | collective-permute-start | bytes 393224 | tf_op jit(solution)/shard_map/ppermute | solution.py:155
  16.2 0.5 %collective-permute-start.6 = (bf16[2,256,128]{2,1,0:T(8,128)(2,1)S(1)}, bf16[2,256,128]{2,1,0:T(8,128)(2,1)S(1)}, u32[]{:S(2)}, u32[]{:S(2)}) collective-permute-start(bf16[2,256,128]{2,1,0:T(8,128)(2,1)S(1)} %line.1), channel_id=1, source_target_pairs={{0,16},{1,17},{2,18},{3,19},{4,20},{5,21},{6,22},{7,23},{8,24},{9,... | collective-permute-start | bytes 393224 | tf_op jit(solution)/shard_map/ppermute | solution.py:155
  16.7 1.5 %collective-permute-start.7 = (bf16[2,256,128]{2,1,0:T(8,128)(2,1)S(1)}, bf16[2,256,128]{2,1,0:T(8,128)(2,1)S(1)}, u32[]{:S(2)}, u32[]{:S(2)}) collective-permute-start(bf16[2,256,128]{2,1,0:T(8,128)(2,1)S(1)} %line.1), channel_id=1, source_target_pairs={{0,8},{1,9},{2,10},{3,11},{4,12},{5,13},{6,14},{7,15},{8,0},{9,1},... | collective-permute-start | bytes 393224 | tf_op jit(solution)/shard_map/ppermute | solution.py:155
  18.2 0.0 copy-done.1
  18.2 0.1 collective-permute-start.8
  18.3 0.6 %collective-permute-start.9 = (bf16[256,256]{1,0:T(8,128)(2,1)S(1)}, bf16[256,256]{1,0:T(8,128)(2,1)S(1)}, u32[]{:S(2)}, u32[]{:S(2)}) collective-permute-start(bf16[256,256]{1,0:T(8,128)(2,1)S(1)} %slice_bitcast_fusion), channel_id=1, source_target_pairs={{0,4},{1,5},{2,6},{3,7},{4,0},{5,1},{6,2},{7,3},{8,12},{9,13},{10,... | collective-permute-start | bytes 393224 | tf_op jit(solution)/shard_map/ppermute | solution.py:155
  18.9 0.0 copy-done
  18.9 0.0 copy-done.2
  18.9 2.7 %collective-permute-done.5 = bf16[2,256,128]{2,1,0:T(8,128)(2,1)S(1)} collective-permute-done((bf16[2,256,128]{2,1,0:T(8,128)(2,1)S(1)}, bf16[2,256,128]{2,1,0:T(8,128)(2,1)S(1)}, u32[]{:S(2)}, u32[]{:S(2)}) %collective-permute-start.5) | collective-permute-done | bytes 131104 | tf_op jit(solution)/shard_map/ppermute | solution.py:155
  21.7 0.5 %collective-permute-done.6 = bf16[2,256,128]{2,1,0:T(8,128)(2,1)S(1)} collective-permute-done((bf16[2,256,128]{2,1,0:T(8,128)(2,1)S(1)}, bf16[2,256,128]{2,1,0:T(8,128)(2,1)S(1)}, u32[]{:S(2)}, u32[]{:S(2)}) %collective-permute-start.6) | collective-permute-done | bytes 131104 | tf_op jit(solution)/shard_map/ppermute | solution.py:155
  22.1 0.9 %collective-permute-done.7 = bf16[2,256,128]{2,1,0:T(8,128)(2,1)S(1)} collective-permute-done((bf16[2,256,128]{2,1,0:T(8,128)(2,1)S(1)}, bf16[2,256,128]{2,1,0:T(8,128)(2,1)S(1)}, u32[]{:S(2)}, u32[]{:S(2)}) %collective-permute-start.7) | collective-permute-done | bytes 131104 | tf_op jit(solution)/shard_map/ppermute | solution.py:155
  23.0 0.0 collective-permute-done.8.refs_2_
  23.0 0.0 collective-permute-done.9.refs_3_
  23.1 0.1 collective-permute-start.10
  23.3 0.6 %collective-permute-start.11 = (bf16[4,256,128]{2,1,0:T(8,128)(2,1)S(1)}, bf16[4,256,128]{2,1,0:T(8,128)(2,1)S(1)}, u32[]{:S(2)}, u32[]{:S(2)}) collective-permute-start(bf16[4,256,128]{2,1,0:T(8,128)(2,1)S(1)} %pad_maximum_fusion.2.refs_4_), channel_id=1, source_target_pairs={{0,4},{1,5},{2,6},{3,7},{4,0},{5,1},{6,2},{7,3},{8,12},{9,13},{10,... | collective-permute-start | bytes 786440 | tf_op jit(solution)/shard_map/ppermute | solution.py:155
  23.8 0.9 %collective-permute-done.10.refs_5_ = bf16[4,256,128]{2,1,0:T(8,128)(2,1)S(1)} collective-permute-done((bf16[4,256,128]{2,1,0:T(8,128)(2,1)S(1)}, bf16[4,256,128]{2,1,0:T(8,128)(2,1)S(1)}, u32[]{:S(2)}, u32[]{:S(2)}) %collective-permute-start.10) | collective-permute-done | bytes 262176 | tf_op jit(solution)/shard_map/ppermute | solution.py:155
  24.8 0.4 block_one.1
  25.2 0.0 collective-permute-done.11.refs_5_
  25.2 0.8 %block_two.1 = (bf16[256,256]{1,0:T(8,128)(2,1)S(1)}, bf16[256,256]{1,0:T(8,128)(2,1)S(1)}, bf16[512,128]{1,0:T(8,128)(2,1)S(1)}, bf16[512,128]{1,0:T(8,128)(2,1)S(1)}) custom-call(f32[512,256]{1,0:T(8,128)S(1)} %get-tuple-element.50.refs_0_, bf16[512,256]{1,0:T(8,128)(2,1)S(1)} %get-tuple-element.51.refs_1_, ...), custom_call_target="tpu_custom_call" | custom-call | tf_op jit(solution)/shard_map/block_two/pallas_call | solution.py:383
  26.0 0.2 collective-permute-start.13
  26.2 0.6 %collective-permute-start.12 = (bf16[256,256]{1,0:T(8,128)(2,1)S(1)}, bf16[256,256]{1,0:T(8,128)(2,1)S(1)}, u32[]{:S(2)}, u32[]{:S(2)}) collective-permute-start(bf16[256,256]{1,0:T(8,128)(2,1)S(1)} %get-tuple-element.54), channel_id=1, source_target_pairs={{0,8},{1,9},{2,10},{3,11},{4,12},{5,13},{6,14},{7,15},{8,0},{9,1},... | collective-permute-start | bytes 393224 | tf_op jit(solution)/shard_map/ppermute | solution.py:155
  26.9 0.6 %collective-permute-done.13.refs_2_ = bf16[512,128]{1,0:T(8,128)(2,1)S(1)} collective-permute-done((bf16[512,128]{1,0:T(8,128)(2,1)S(1)}, bf16[512,128]{1,0:T(8,128)(2,1)S(1)}, u32[]{:S(2)}, u32[]{:S(2)}) %collective-permute-start.13) | collective-permute-done | bytes 131104 | tf_op jit(solution)/shard_map/ppermute | solution.py:155
  27.4 0.6 %terms.1 = (f32[256,128]{1,0:T(8,128)S(1)}, bf16[256,128]{1,0:T(8,128)(2,1)S(1)}, bf16[256,128]{1,0:T(8,128)(2,1)S(1)}, bf16[256,128]{1,0:T(8,128)(2,1)S(1)}) custom-call(bf16[6,256,256]{2,1,0:T(8,128)(2,1)S(1)} %get-tuple-element.55.refs_0_, bf16[512,128]{1,0:T(8,128)(2,1)S(1)} %get-tuple-element.56.refs_1_, ...), custom_call_target="tpu_custom_call" | custom-call | tf_op jit(solution)/shard_map/terms/pallas_call | solution.py:383
  28.0 1.8 %collective-permute-start.14 = (bf16[256,128]{1,0:T(8,128)(2,1)S(1)}, bf16[256,128]{1,0:T(8,128)(2,1)S(1)}, u32[]{:S(2)}, u32[]{:S(2)}) collective-permute-start(bf16[256,128]{1,0:T(8,128)(2,1)S(1)} %get-tuple-element.59), channel_id=1, source_target_pairs={{0,24},{1,25},{2,26},{3,27},{4,28},{5,29},{6,30},{7,31},{8,16},{9,... | collective-permute-start | bytes 196616 | tf_op jit(solution)/shard_map/ppermute | solution.py:155
  29.9 0.5 %collective-permute-start.15 = (bf16[256,128]{1,0:T(8,128)(2,1)S(1)}, bf16[256,128]{1,0:T(8,128)(2,1)S(1)}, u32[]{:S(2)}, u32[]{:S(2)}) collective-permute-start(bf16[256,128]{1,0:T(8,128)(2,1)S(1)} %get-tuple-element.60), channel_id=1, source_target_pairs={{0,16},{1,17},{2,18},{3,19},{4,20},{5,21},{6,22},{7,23},{8,24},{9,... | collective-permute-start | bytes 196616 | tf_op jit(solution)/shard_map/ppermute | solution.py:155
  30.4 1.2 %collective-permute-start.16 = (bf16[256,128]{1,0:T(8,128)(2,1)S(1)}, bf16[256,128]{1,0:T(8,128)(2,1)S(1)}, u32[]{:S(2)}, u32[]{:S(2)}) collective-permute-start(bf16[256,128]{1,0:T(8,128)(2,1)S(1)} %get-tuple-element.61), channel_id=1, source_target_pairs={{0,8},{1,9},{2,10},{3,11},{4,12},{5,13},{6,14},{7,15},{8,0},{9,1},... | collective-permute-start | bytes 196616 | tf_op jit(solution)/shard_map/ppermute | solution.py:155
  31.6 2.1 %collective-permute-done.14.refs_1_ = bf16[256,128]{1,0:T(8,128)(2,1)S(1)} collective-permute-done((bf16[256,128]{1,0:T(8,128)(2,1)S(1)}, bf16[256,128]{1,0:T(8,128)(2,1)S(1)}, u32[]{:S(2)}, u32[]{:S(2)}) %collective-permute-start.14) | collective-permute-done | bytes 65568 | tf_op jit(solution)/shard_map/ppermute | solution.py:155
  33.7 0.5 %collective-permute-done.15.refs_2_ = bf16[256,128]{1,0:T(8,128)(2,1)S(1)} collective-permute-done((bf16[256,128]{1,0:T(8,128)(2,1)S(1)}, bf16[256,128]{1,0:T(8,128)(2,1)S(1)}, u32[]{:S(2)}, u32[]{:S(2)}) %collective-permute-start.15) | collective-permute-done | bytes 65568 | tf_op jit(solution)/shard_map/ppermute | solution.py:155
  34.1 0.7 %collective-permute-done.16.refs_3_ = bf16[256,128]{1,0:T(8,128)(2,1)S(1)} collective-permute-done((bf16[256,128]{1,0:T(8,128)(2,1)S(1)}, bf16[256,128]{1,0:T(8,128)(2,1)S(1)}, u32[]{:S(2)}, u32[]{:S(2)}) %collective-permute-start.16) | collective-permute-done | bytes 65568 | tf_op jit(solution)/shard_map/ppermute | solution.py:155
  34.8 0.1 chips.1
  34.9 3.3 %collective-permute-start.19 = (bf16[72,128]{1,0:T(8,128)(2,1)S(1)}, bf16[72,128]{1,0:T(8,128)(2,1)S(1)}, u32[]{:S(2)}, u32[]{:S(2)}) collective-permute-start(bf16[72,128]{1,0:T(8,128)(2,1)S(1)} %get-tuple-element.65), channel_id=1, source_target_pairs={{0,3},{1,2},{2,1},{3,0},{4,7},{5,6},{6,5},{7,4},{8,11},{9,10},{10,... | collective-permute-start | bytes 55304 | tf_op jit(solution)/shard_map/ppermute | solution.py:155
  38.2 0.0 collective-permute-start.18
  38.2 1.2 %collective-permute-start.17 = (bf16[72,128]{1,0:T(8,128)(2,1)S(1)}, bf16[72,128]{1,0:T(8,128)(2,1)S(1)}, u32[]{:S(2)}, u32[]{:S(2)}) collective-permute-start(bf16[72,128]{1,0:T(8,128)(2,1)S(1)} %get-tuple-element.63), channel_id=1, source_target_pairs={{0,1},{1,0},{2,3},{3,2},{4,5},{5,4},{6,7},{7,6},{8,9},{9,8},{10,11... | collective-permute-start | bytes 55304 | tf_op jit(solution)/shard_map/ppermute | solution.py:155
  39.4 0.0 collective-permute-done.12
  39.4 1.1 %collective-permute-done.19 = bf16[72,128]{1,0:T(8,128)(2,1)S(1)} collective-permute-done((bf16[72,128]{1,0:T(8,128)(2,1)S(1)}, bf16[72,128]{1,0:T(8,128)(2,1)S(1)}, u32[]{:S(2)}, u32[]{:S(2)}) %collective-permute-start.19) | collective-permute-done | bytes 18464 | tf_op jit(solution)/shard_map/ppermute | solution.py:155
  40.5 2.3 %collective-permute-done.18 = bf16[72,128]{1,0:T(8,128)(2,1)S(1)} collective-permute-done((bf16[72,128]{1,0:T(8,128)(2,1)S(1)}, bf16[72,128]{1,0:T(8,128)(2,1)S(1)}, u32[]{:S(2)}, u32[]{:S(2)}) %collective-permute-start.18) | collective-permute-done | bytes 18464 | tf_op jit(solution)/shard_map/ppermute | solution.py:155
  42.8 0.0 collective-permute-done.17
  42.8 0.1 collective-permute-start.20
  42.9 0.7 %pad_maximum_fusion.3 = bf16[2,256,256]{2,1,0:T(8,128)(2,1)} fusion(bf16[1,256,256]{2,1,0:T(8,128)(2,1)S(1)} %get-tuple-element.67, bf16[1,256,256]{2,1,0:T(8,128)(2,1)S(1)} %get-tuple-element.66), kind=kLoop, calls=%fused_computation.3 | loop fusion | flops 131072 | bytes 524288 | tf_op jit(solution)/shard_map/stack | solution.py:463
  43.6 0.5 %collective-permute-done.20.refs_1_ = f32[72,128]{1,0:T(8,128)S(1)} collective-permute-done((f32[72,128]{1,0:T(8,128)S(1)}, f32[72,128]{1,0:T(8,128)S(1)}, u32[]{:S(2)}, u32[]{:S(2)}) %collective-permute-start.20) | collective-permute-done | bytes 36896 | tf_op jit(solution)/shard_map/ppermute | solution.py:155
  44.1 0.6 %total.1 = f32[144,128]{1,0:T(8,128)} custom-call(f32[72,128]{1,0:T(8,128)S(1)} %convert_add_fusion.refs_0_, f32[72,128]{1,0:T(8,128)S(1)} %collective-permute-done.20.refs_1_), custom_call_target="tpu_custom_call" | custom-call | tf_op jit(solution)/shard_map/total/pallas_call | solution.py:383
  (15 shorter events, 0.2 us)
Async XLA Ops:
  0.6 18.3 %copy-start = (f32[360,4,256]{2,1,0:T(4,128)S(1)}, f32[360,4,256]{2,1,0:T(4,128)}, u32[]{:S(2)}) copy-start(f32[360,4,256]{2,1,0:T(4,128)} %param.7) | copy-start | bytes 4423684
  0.6 18.3 %copy-start.2 = (bf16[1,64,8,256]{3,2,1,0:T(8,128)(2,1)S(1)}, bf16[1,64,8,256]{3,2,1,0:T(8,128)(2,1)}, u32[]{:S(2)}) copy-start(bf16[1,64,8,256]{3,2,1,0:T(8,128)(2,1)} %param.9) | copy-start | bytes 786436
  0.7 17.6 %copy-start.1 = (bf16[1,64,8,256]{3,2,1,0:T(8,128)(2,1)S(1)}, bf16[1,64,8,256]{3,2,1,0:T(8,128)(2,1)}, u32[]{:S(2)}) copy-start(bf16[1,64,8,256]{3,2,1,0:T(8,128)(2,1)} %param.5) | copy-start | bytes 786436
  1.7 4.2 %collective-permute-start = (bf16[2,72,128]{2,1,0:T(8,128)(2,1)S(1)}, bf16[2,72,128]{2,1,0:T(8,128)(2,1)S(1)}, u32[]{:S(2)}, u32[]{:S(2)}) collective-permute-start(bf16[2,72,128]{2,1,0:T(8,128)(2,1)S(1)} %broadcast_select_fusion), channel_id=1, source_target_pairs={{0,4},{1,5},{2,6},{3,7},{4,0},{5,1},{6,2},{7,3},{8,12},{9,13},{10,... | collective-permute-start | bytes 110600 | tf_op jit(solution)/shard_map/ppermute | solution.py:155
  3.3 11.2 %collective-permute-start.4 = (bf16[2,256,256]{2,1,0:T(8,128)(2,1)S(1)}, bf16[2,256,256]{2,1,0:T(8,128)(2,1)S(1)}, u32[]{:S(2)}, u32[]{:S(2)}) collective-permute-start(bf16[2,256,256]{2,1,0:T(8,128)(2,1)S(1)} %pad_maximum_fusion), channel_id=1, source_target_pairs={{0,8},{1,9},{2,10},{3,11},{4,12},{5,13},{6,14},{7,15},{8,0},{9,1},... | collective-permute-start | bytes 786440 | tf_op jit(solution)/shard_map/ppermute | solution.py:155
  6.0 5.8 %collective-permute-start.1 = (bf16[2,72,128]{2,1,0:T(8,128)(2,1)S(1)}, bf16[2,72,128]{2,1,0:T(8,128)(2,1)S(1)}, u32[]{:S(2)}, u32[]{:S(2)}) collective-permute-start(bf16[2,72,128]{2,1,0:T(8,128)(2,1)S(1)} %select_select_fusion.refs_0_), channel_id=1, source_target_pairs={{0,3},{1,2},{2,1},{3,0},{4,7},{5,6},{6,5},{7,4},{8,11},{9,10},{10,... | collective-permute-start | bytes 110600 | tf_op jit(solution)/shard_map/ppermute | solution.py:155
  9.7 4.9 %collective-permute-start.2 = (bf16[2,72,128]{2,1,0:T(8,128)(2,1)S(1)}, bf16[2,72,128]{2,1,0:T(8,128)(2,1)S(1)}, u32[]{:S(2)}, u32[]{:S(2)}) collective-permute-start(bf16[2,72,128]{2,1,0:T(8,128)(2,1)S(1)} %select_select_fusion.refs_0_), channel_id=1, source_target_pairs={{0,2},{1,3},{2,0},{3,1},{4,6},{5,7},{6,4},{7,5},{8,10},{9,11},{10,... | collective-permute-start | bytes 110600 | tf_op jit(solution)/shard_map/ppermute | solution.py:155
  9.7 4.9 %collective-permute-start.3 = (bf16[2,72,128]{2,1,0:T(8,128)(2,1)S(1)}, bf16[2,72,128]{2,1,0:T(8,128)(2,1)S(1)}, u32[]{:S(2)}, u32[]{:S(2)}) collective-permute-start(bf16[2,72,128]{2,1,0:T(8,128)(2,1)S(1)} %select_select_fusion.refs_0_), channel_id=1, source_target_pairs={{0,1},{1,0},{2,3},{3,2},{4,5},{5,4},{6,7},{7,6},{8,9},{9,8},{10,11... | collective-permute-start | bytes 110600 | tf_op jit(solution)/shard_map/ppermute | solution.py:155
  14.7 7.0 %collective-permute-start.5 = (bf16[2,256,128]{2,1,0:T(8,128)(2,1)S(1)}, bf16[2,256,128]{2,1,0:T(8,128)(2,1)S(1)}, u32[]{:S(2)}, u32[]{:S(2)}) collective-permute-start(bf16[2,256,128]{2,1,0:T(8,128)(2,1)S(1)} %line.1), channel_id=1, source_target_pairs={{0,24},{1,25},{2,26},{3,27},{4,28},{5,29},{6,30},{7,31},{8,16},{9,... | collective-permute-start | bytes 393224 | tf_op jit(solution)/shard_map/ppermute | solution.py:155
  16.2 5.9 %collective-permute-start.6 = (bf16[2,256,128]{2,1,0:T(8,128)(2,1)S(1)}, bf16[2,256,128]{2,1,0:T(8,128)(2,1)S(1)}, u32[]{:S(2)}, u32[]{:S(2)}) collective-permute-start(bf16[2,256,128]{2,1,0:T(8,128)(2,1)S(1)} %line.1), channel_id=1, source_target_pairs={{0,16},{1,17},{2,18},{3,19},{4,20},{5,21},{6,22},{7,23},{8,24},{9,... | collective-permute-start | bytes 393224 | tf_op jit(solution)/shard_map/ppermute | solution.py:155
  16.7 6.3 %collective-permute-start.7 = (bf16[2,256,128]{2,1,0:T(8,128)(2,1)S(1)}, bf16[2,256,128]{2,1,0:T(8,128)(2,1)S(1)}, u32[]{:S(2)}, u32[]{:S(2)}) collective-permute-start(bf16[2,256,128]{2,1,0:T(8,128)(2,1)S(1)} %line.1), channel_id=1, source_target_pairs={{0,8},{1,9},{2,10},{3,11},{4,12},{5,13},{6,14},{7,15},{8,0},{9,1},... | collective-permute-start | bytes 393224 | tf_op jit(solution)/shard_map/ppermute | solution.py:155
  18.2 4.8 %collective-permute-start.8 = (bf16[256,256]{1,0:T(8,128)(2,1)S(1)}, bf16[256,256]{1,0:T(8,128)(2,1)S(1)}, u32[]{:S(2)}, u32[]{:S(2)}) collective-permute-start(bf16[256,256]{1,0:T(8,128)(2,1)S(1)} %dynamic-slice_bitcast_fusion.1.refs_0_), channel_id=1, source_target_pairs={{0,4},{1,5},{2,6},{3,7},{4,0},{5,1},{6,2},{7,3},{8,12},{9,13},{10,... | collective-permute-start | bytes 393224 | tf_op jit(solution)/shard_map/ppermute | solution.py:155
  18.3 4.7 %collective-permute-start.9 = (bf16[256,256]{1,0:T(8,128)(2,1)S(1)}, bf16[256,256]{1,0:T(8,128)(2,1)S(1)}, u32[]{:S(2)}, u32[]{:S(2)}) collective-permute-start(bf16[256,256]{1,0:T(8,128)(2,1)S(1)} %slice_bitcast_fusion), channel_id=1, source_target_pairs={{0,4},{1,5},{2,6},{3,7},{4,0},{5,1},{6,2},{7,3},{8,12},{9,13},{10,... | collective-permute-start | bytes 393224 | tf_op jit(solution)/shard_map/ppermute | solution.py:155
  23.1 1.6 %collective-permute-start.10 = (bf16[4,256,128]{2,1,0:T(8,128)(2,1)S(1)}, bf16[4,256,128]{2,1,0:T(8,128)(2,1)S(1)}, u32[]{:S(2)}, u32[]{:S(2)}) collective-permute-start(bf16[4,256,128]{2,1,0:T(8,128)(2,1)S(1)} %pad_maximum_fusion.1.refs_4_), channel_id=1, source_target_pairs={{0,4},{1,5},{2,6},{3,7},{4,0},{5,1},{6,2},{7,3},{8,12},{9,13},{10,... | collective-permute-start | bytes 786440 | tf_op jit(solution)/shard_map/ppermute | solution.py:155
  23.3 1.9 %collective-permute-start.11 = (bf16[4,256,128]{2,1,0:T(8,128)(2,1)S(1)}, bf16[4,256,128]{2,1,0:T(8,128)(2,1)S(1)}, u32[]{:S(2)}, u32[]{:S(2)}) collective-permute-start(bf16[4,256,128]{2,1,0:T(8,128)(2,1)S(1)} %pad_maximum_fusion.2.refs_4_), channel_id=1, source_target_pairs={{0,4},{1,5},{2,6},{3,7},{4,0},{5,1},{6,2},{7,3},{8,12},{9,13},{10,... | collective-permute-start | bytes 786440 | tf_op jit(solution)/shard_map/ppermute | solution.py:155
  26.0 1.4 %collective-permute-start.13 = (bf16[512,128]{1,0:T(8,128)(2,1)S(1)}, bf16[512,128]{1,0:T(8,128)(2,1)S(1)}, u32[]{:S(2)}, u32[]{:S(2)}) collective-permute-start(bf16[512,128]{1,0:T(8,128)(2,1)S(1)} %get-tuple-element.57), channel_id=1, source_target_pairs={{0,4},{1,5},{2,6},{3,7},{4,0},{5,1},{6,2},{7,3},{8,12},{9,13},{10,... | collective-permute-start | bytes 393224 | tf_op jit(solution)/shard_map/ppermute | solution.py:155
  26.2 13.1 %collective-permute-start.12 = (bf16[256,256]{1,0:T(8,128)(2,1)S(1)}, bf16[256,256]{1,0:T(8,128)(2,1)S(1)}, u32[]{:S(2)}, u32[]{:S(2)}) collective-permute-start(bf16[256,256]{1,0:T(8,128)(2,1)S(1)} %get-tuple-element.54), channel_id=1, source_target_pairs={{0,8},{1,9},{2,10},{3,11},{4,12},{5,13},{6,14},{7,15},{8,0},{9,1},... | collective-permute-start | bytes 393224 | tf_op jit(solution)/shard_map/ppermute | solution.py:155
  28.0 5.6 %collective-permute-start.14 = (bf16[256,128]{1,0:T(8,128)(2,1)S(1)}, bf16[256,128]{1,0:T(8,128)(2,1)S(1)}, u32[]{:S(2)}, u32[]{:S(2)}) collective-permute-start(bf16[256,128]{1,0:T(8,128)(2,1)S(1)} %get-tuple-element.59), channel_id=1, source_target_pairs={{0,24},{1,25},{2,26},{3,27},{4,28},{5,29},{6,30},{7,31},{8,16},{9,... | collective-permute-start | bytes 196616 | tf_op jit(solution)/shard_map/ppermute | solution.py:155
  29.9 4.3 %collective-permute-start.15 = (bf16[256,128]{1,0:T(8,128)(2,1)S(1)}, bf16[256,128]{1,0:T(8,128)(2,1)S(1)}, u32[]{:S(2)}, u32[]{:S(2)}) collective-permute-start(bf16[256,128]{1,0:T(8,128)(2,1)S(1)} %get-tuple-element.60), channel_id=1, source_target_pairs={{0,16},{1,17},{2,18},{3,19},{4,20},{5,21},{6,22},{7,23},{8,24},{9,... | collective-permute-start | bytes 196616 | tf_op jit(solution)/shard_map/ppermute | solution.py:155
  30.4 4.4 %collective-permute-start.16 = (bf16[256,128]{1,0:T(8,128)(2,1)S(1)}, bf16[256,128]{1,0:T(8,128)(2,1)S(1)}, u32[]{:S(2)}, u32[]{:S(2)}) collective-permute-start(bf16[256,128]{1,0:T(8,128)(2,1)S(1)} %get-tuple-element.61), channel_id=1, source_target_pairs={{0,8},{1,9},{2,10},{3,11},{4,12},{5,13},{6,14},{7,15},{8,0},{9,1},... | collective-permute-start | bytes 196616 | tf_op jit(solution)/shard_map/ppermute | solution.py:155
  34.9 5.6 %collective-permute-start.19 = (bf16[72,128]{1,0:T(8,128)(2,1)S(1)}, bf16[72,128]{1,0:T(8,128)(2,1)S(1)}, u32[]{:S(2)}, u32[]{:S(2)}) collective-permute-start(bf16[72,128]{1,0:T(8,128)(2,1)S(1)} %get-tuple-element.65), channel_id=1, source_target_pairs={{0,3},{1,2},{2,1},{3,0},{4,7},{5,6},{6,5},{7,4},{8,11},{9,10},{10,... | collective-permute-start | bytes 55304 | tf_op jit(solution)/shard_map/ppermute | solution.py:155
  38.2 4.7 %collective-permute-start.18 = (bf16[72,128]{1,0:T(8,128)(2,1)S(1)}, bf16[72,128]{1,0:T(8,128)(2,1)S(1)}, u32[]{:S(2)}, u32[]{:S(2)}) collective-permute-start(bf16[72,128]{1,0:T(8,128)(2,1)S(1)} %get-tuple-element.64), channel_id=1, source_target_pairs={{0,2},{1,3},{2,0},{3,1},{4,6},{5,7},{6,4},{7,5},{8,10},{9,11},{10,... | collective-permute-start | bytes 55304 | tf_op jit(solution)/shard_map/ppermute | solution.py:155
  38.2 4.7 %collective-permute-start.17 = (bf16[72,128]{1,0:T(8,128)(2,1)S(1)}, bf16[72,128]{1,0:T(8,128)(2,1)S(1)}, u32[]{:S(2)}, u32[]{:S(2)}) collective-permute-start(bf16[72,128]{1,0:T(8,128)(2,1)S(1)} %get-tuple-element.63), channel_id=1, source_target_pairs={{0,1},{1,0},{2,3},{3,2},{4,5},{5,4},{6,7},{7,6},{8,9},{9,8},{10,11... | collective-permute-start | bytes 55304 | tf_op jit(solution)/shard_map/ppermute | solution.py:155
  42.8 1.3 %collective-permute-start.20 = (f32[72,128]{1,0:T(8,128)S(1)}, f32[72,128]{1,0:T(8,128)S(1)}, u32[]{:S(2)}, u32[]{:S(2)}) collective-permute-start(f32[72,128]{1,0:T(8,128)S(1)} %convert_add_fusion.refs_0_), channel_id=1, source_target_pairs={{0,4},{1,5},{2,6},{3,7},{4,0},{5,1},{6,2},{7,3},{8,12},{9,13},{10,... | collective-permute-start | bytes 110600 | tf_op jit(solution)/shard_map/ppermute | solution.py:155

commit v3 on v2

--- a/solution.py
+++ b/solution.py
@@ -377,16 +377,16 @@
     bf16, f32 = jnp.bfloat16, jnp.float32
     shape = jax.ShapeDtypeStruct
 
-    def call(name, body, out_shape, scratch, *operands, space=pltpu.VMEM, mib=16):
+    def call(name, body, out_shape, scratch, *operands):
         vmem = pl.BlockSpec(memory_space=pltpu.VMEM)
         several = isinstance(out_shape, tuple)
         return pl.pallas_call(
             lambda *refs: body(layout, *refs),
             out_shape=out_shape,
-            in_specs=[pl.BlockSpec(memory_space=space)] * len(operands),
+            in_specs=[vmem] * len(operands),
             out_specs=(vmem,) * len(out_shape) if several else vmem,
             scratch_shapes=scratch,
-            compiler_params=pltpu.CompilerParams(vmem_limit_bytes=mib * 1024 * 1024),
+            compiler_params=pltpu.CompilerParams(vmem_limit_bytes=16 * 1024 * 1024),
             name=name,
         )(*operands)
 
@@ -401,8 +401,8 @@
     pick = lambda halves, number: lax.dynamic_index_in_dim(halves, number, 0, keepdims=False)
     other = moved(jnp.stack([pick(halves_x, 1 - y), pick(halves_ct, 1 - y)]), dy=1)
     line = [piece, *(moved(piece, dz=dz) for dz in Z_ORDER)]
-    *line, other, halves_x, halves_ct, film = lax.optimization_barrier(
-        (*line, other, halves_x, halves_ct, film)
+    *line, halves_x, halves_ct, film = lax.optimization_barrier(
+        (*line, halves_x, halves_ct, film)
     )
     mine_x, mine_ct = pick(halves_x, y), pick(halves_ct, y)
     film_row = lax.dynamic_index_in_dim(film, lead_ids[0], 0, keepdims=False)

time: 44.9 us -> 43.5 us (0.969)
  waiting for transfers between devices: 16.1 us -> 14.7 us
    ppermute x21, waiting for transfers between devices: 16.1 us -> 14.7 us  [moved(): lax.ppermute(value, AXES, pairs(lambda x, y, c, z: (x ^ dx, y ^ dy, c ^ d...]
  transfers between devices with their start and end apart: 21 -> 21, of which waited for: 13 -> 13; matrix products, arithmetic and copies ran while one was open for 4% -> 4% of each run, Pallas kernels for 2% -> 3%
where the time goes in v3:
time: 43.5 us; the launch traced here: 43.3 us
  starting transfers between devices  21.3 us (49%)
  waiting for transfers between devices  14.7 us (34%)
  Pallas kernels  2.71 us (6%)
  local copies, waits for them, and re-layouts  2.11 us (5%)
  between operations  1.52 us (3%)
  other arithmetic  0.96 us (2%)
    ppermute x21, starting transfers between devices, moved(): lax.ppermute(value, AXES, pairs(lambda x, y, c, z: (x ^ dx, y ^ dy, c ^ d...  21.3 us
    ppermute x21, waiting for transfers between devices, moved(): lax.ppermute(value, AXES, pairs(lambda x, y, c, z: (x ^ dx, y ^ dy, c ^ d...  14.7 us
    pallas_call x6, Pallas kernels, call(): pl.pallas_call(lambda *refs: body(layout, *refs), out_shape=out_shape, in...  2.71 us
    unnamed x7, local copies, waits for them, and re-layouts  1.05 us
    dynamic_slice x1, local copies, waits for them, and re-layouts, row_shards(): lax.dynamic_index_in_dim(halves, number, 0, keepdims=False)  0.98 us
  transfers between devices with their start and end apart: 21, of which 13 were waited for; matrix products, arithmetic and copies ran while one was open for 4% of the time, Pallas kernels for 3%

profile of v3, /device:TPU:0, one launch (start us, length us, event | category | flops | bytes accessed | tf_op | source)
XLA Modules:
  0.0 43.3 jit_solution(1411482631308118834)
XLA Ops:
  0.6 0.0 copy-start
  0.6 0.0 copy-start.1
  0.7 0.0 copy-start.2
  0.7 1.0 %copy.9 = bf16[1,2,72,256]{3,2,1,0:T(8,128)(2,1)S(1)} copy(bf16[1,2,72,256]{3,1,2,0:T(2,128)(2,1)} %bitcast.31) | data formatting | bytes 147456
  1.7 0.5 %collective-permute-start = (bf16[2,72,128]{2,1,0:T(8,128)(2,1)S(1)}, bf16[2,72,128]{2,1,0:T(8,128)(2,1)S(1)}, u32[]{:S(2)}, u32[]{:S(2)}) collective-permute-start(bf16[2,72,128]{2,1,0:T(8,128)(2,1)S(1)} %broadcast_select_fusion), channel_id=1, source_target_pairs={{0,4},{1,5},{2,6},{3,7},{4,0},{5,1},{6,2},{7,3},{8,12},{9,13},{10,... | collective-permute-start | bytes 110600 | tf_op jit(solution)/shard_map/ppermute | solution.py:155
  2.3 1.0 %constant_dynamic-slice_fusion = (bf16[1,256,256]{2,1,0:T(8,128)(2,1)S(1)}, bf16[1,256,256]{2,1,0:T(8,128)(2,1)S(1)}) fusion(bf16[2,256,256]{2,1,0:T(8,128)(2,1)} %bitcast.28, s32[]{:T(128)S(6)} %select_n.90, bf16[2,256,256]{2,1,0:T(8,128)(2,1)} %bitcast.26), kind=kLoop, calls=%fused_computation.15 | loop fusion | bytes 524292 | tf_op jit(solution)/shard_map/jit(dynamic_index_in_dim)/dynamic_slice | solution.py:401
  3.3 2.6 %collective-permute-start.8 = (bf16[2,256,256]{2,1,0:T(8,128)(2,1)S(1)}, bf16[2,256,256]{2,1,0:T(8,128)(2,1)S(1)}, u32[]{:S(2)}, u32[]{:S(2)}) collective-permute-start(bf16[2,256,256]{2,1,0:T(8,128)(2,1)S(1)} %pad_maximum_fusion), channel_id=1, source_target_pairs={{0,8},{1,9},{2,10},{3,11},{4,12},{5,13},{6,14},{7,15},{8,0},{9,1},... | collective-permute-start | bytes 786440 | tf_op jit(solution)/shard_map/ppermute | solution.py:155
  5.9 0.0 collective-permute-done
  5.9 0.1 select_select_fusion.refs_0_
  6.0 3.7 %collective-permute-start.1 = (bf16[2,72,128]{2,1,0:T(8,128)(2,1)S(1)}, bf16[2,72,128]{2,1,0:T(8,128)(2,1)S(1)}, u32[]{:S(2)}, u32[]{:S(2)}) collective-permute-start(bf16[2,72,128]{2,1,0:T(8,128)(2,1)S(1)} %select_select_fusion.refs_0_), channel_id=1, source_target_pairs={{0,3},{1,2},{2,1},{3,0},{4,7},{5,6},{6,5},{7,4},{8,11},{9,10},{10,... | collective-permute-start | bytes 110600 | tf_op jit(solution)/shard_map/ppermute | solution.py:155
  9.7 0.0 collective-permute-start.2
  9.7 0.8 %collective-permute-start.3 = (bf16[2,72,128]{2,1,0:T(8,128)(2,1)S(1)}, bf16[2,72,128]{2,1,0:T(8,128)(2,1)S(1)}, u32[]{:S(2)}, u32[]{:S(2)}) collective-permute-start(bf16[2,72,128]{2,1,0:T(8,128)(2,1)S(1)} %select_select_fusion.refs_0_), channel_id=1, source_target_pairs={{0,1},{1,0},{2,3},{3,2},{4,5},{5,4},{6,7},{7,6},{8,9},{9,8},{10,11... | collective-permute-start | bytes 110600 | tf_op jit(solution)/shard_map/ppermute | solution.py:155
  11.1 0.7 %collective-permute-done.1.refs_1_ = bf16[2,72,128]{2,1,0:T(8,128)(2,1)S(1)} collective-permute-done((bf16[2,72,128]{2,1,0:T(8,128)(2,1)S(1)}, bf16[2,72,128]{2,1,0:T(8,128)(2,1)S(1)}, u32[]{:S(2)}, u32[]{:S(2)}) %collective-permute-start.1) | collective-permute-done | bytes 36896 | tf_op jit(solution)/shard_map/ppermute | solution.py:155
  11.8 2.7 %collective-permute-done.2.refs_2_ = bf16[2,72,128]{2,1,0:T(8,128)(2,1)S(1)} collective-permute-done((bf16[2,72,128]{2,1,0:T(8,128)(2,1)S(1)}, bf16[2,72,128]{2,1,0:T(8,128)(2,1)S(1)}, u32[]{:S(2)}, u32[]{:S(2)}) %collective-permute-start.2) | collective-permute-done | bytes 36896 | tf_op jit(solution)/shard_map/ppermute | solution.py:155
  14.5 0.0 collective-permute-done.3.refs_3_
  14.5 0.1 line.1
  14.7 1.5 %collective-permute-start.4 = (bf16[2,256,128]{2,1,0:T(8,128)(2,1)S(1)}, bf16[2,256,128]{2,1,0:T(8,128)(2,1)S(1)}, u32[]{:S(2)}, u32[]{:S(2)}) collective-permute-start(bf16[2,256,128]{2,1,0:T(8,128)(2,1)S(1)} %line.1), channel_id=1, source_target_pairs={{0,24},{1,25},{2,26},{3,27},{4,28},{5,29},{6,30},{7,31},{8,16},{9,... | collective-permute-start | bytes 393224 | tf_op jit(solution)/shard_map/ppermute | solution.py:155
  16.2 0.5 %collective-permute-start.5 = (bf16[2,256,128]{2,1,0:T(8,128)(2,1)S(1)}, bf16[2,256,128]{2,1,0:T(8,128)(2,1)S(1)}, u32[]{:S(2)}, u32[]{:S(2)}) collective-permute-start(bf16[2,256,128]{2,1,0:T(8,128)(2,1)S(1)} %line.1), channel_id=1, source_target_pairs={{0,16},{1,17},{2,18},{3,19},{4,20},{5,21},{6,22},{7,23},{8,24},{9,... | collective-permute-start | bytes 393224 | tf_op jit(solution)/shard_map/ppermute | solution.py:155
  16.7 1.5 %collective-permute-start.6 = (bf16[2,256,128]{2,1,0:T(8,128)(2,1)S(1)}, bf16[2,256,128]{2,1,0:T(8,128)(2,1)S(1)}, u32[]{:S(2)}, u32[]{:S(2)}) collective-permute-start(bf16[2,256,128]{2,1,0:T(8,128)(2,1)S(1)} %line.1), channel_id=1, source_target_pairs={{0,8},{1,9},{2,10},{3,11},{4,12},{5,13},{6,14},{7,15},{8,0},{9,1},... | collective-permute-start | bytes 393224 | tf_op jit(solution)/shard_map/ppermute | solution.py:155
  18.2 0.0 copy-done.1
  18.2 0.1 collective-permute-start.7
  18.3 0.0 collective-permute-done.8.refs_1_.refs_3_
  18.3 0.6 %collective-permute-start.9 = (bf16[256,256]{1,0:T(8,128)(2,1)S(1)}, bf16[256,256]{1,0:T(8,128)(2,1)S(1)}, u32[]{:S(2)}, u32[]{:S(2)}) collective-permute-start(bf16[256,256]{1,0:T(8,128)(2,1)S(1)} %slice_bitcast_fusion), channel_id=1, source_target_pairs={{0,4},{1,5},{2,6},{3,7},{4,0},{5,1},{6,2},{7,3},{8,12},{9,13},{10,... | collective-permute-start | bytes 393224 | tf_op jit(solution)/shard_map/ppermute | solution.py:155
  18.9 0.0 copy-done
  18.9 0.0 copy-done.2
  18.9 2.7 %collective-permute-done.4 = bf16[2,256,128]{2,1,0:T(8,128)(2,1)S(1)} collective-permute-done((bf16[2,256,128]{2,1,0:T(8,128)(2,1)S(1)}, bf16[2,256,128]{2,1,0:T(8,128)(2,1)S(1)}, u32[]{:S(2)}, u32[]{:S(2)}) %collective-permute-start.4) | collective-permute-done | bytes 131104 | tf_op jit(solution)/shard_map/ppermute | solution.py:155
  21.7 0.4 collective-permute-done.5
  22.1 1.0 %collective-permute-done.6 = bf16[2,256,128]{2,1,0:T(8,128)(2,1)S(1)} collective-permute-done((bf16[2,256,128]{2,1,0:T(8,128)(2,1)S(1)}, bf16[2,256,128]{2,1,0:T(8,128)(2,1)S(1)}, u32[]{:S(2)}, u32[]{:S(2)}) %collective-permute-start.6) | collective-permute-done | bytes 131104 | tf_op jit(solution)/shard_map/ppermute | solution.py:155
  23.0 0.0 collective-permute-done.7.refs_2_
  23.0 0.0 collective-permute-done.9.refs_3_
  23.1 0.1 collective-permute-start.10
  23.3 0.6 %collective-permute-start.11 = (bf16[4,256,128]{2,1,0:T(8,128)(2,1)S(1)}, bf16[4,256,128]{2,1,0:T(8,128)(2,1)S(1)}, u32[]{:S(2)}, u32[]{:S(2)}) collective-permute-start(bf16[4,256,128]{2,1,0:T(8,128)(2,1)S(1)} %pad_maximum_fusion.2.refs_4_), channel_id=1, source_target_pairs={{0,4},{1,5},{2,6},{3,7},{4,0},{5,1},{6,2},{7,3},{8,12},{9,13},{10,... | collective-permute-start | bytes 786440 | tf_op jit(solution)/shard_map/ppermute | solution.py:155
  23.8 0.9 %collective-permute-done.10.refs_5_ = bf16[4,256,128]{2,1,0:T(8,128)(2,1)S(1)} collective-permute-done((bf16[4,256,128]{2,1,0:T(8,128)(2,1)S(1)}, bf16[4,256,128]{2,1,0:T(8,128)(2,1)S(1)}, u32[]{:S(2)}, u32[]{:S(2)}) %collective-permute-start.10) | collective-permute-done | bytes 262176 | tf_op jit(solution)/shard_map/ppermute | solution.py:155
  24.7 0.4 block_one.1
  25.2 0.0 collective-permute-done.11.refs_5_
  25.2 0.8 %block_two.1 = (bf16[256,256]{1,0:T(8,128)(2,1)S(1)}, bf16[256,256]{1,0:T(8,128)(2,1)S(1)}, bf16[512,128]{1,0:T(8,128)(2,1)S(1)}, bf16[512,128]{1,0:T(8,128)(2,1)S(1)}) custom-call(f32[512,256]{1,0:T(8,128)S(1)} %get-tuple-element.48.refs_0_, bf16[512,256]{1,0:T(8,128)(2,1)S(1)} %get-tuple-element.49.refs_1_, ...), custom_call_target="tpu_custom_call" | custom-call | tf_op jit(solution)/shard_map/block_two/pallas_call | solution.py:383
  26.0 0.2 collective-permute-start.13
  26.2 0.6 %collective-permute-start.12 = (bf16[256,256]{1,0:T(8,128)(2,1)S(1)}, bf16[256,256]{1,0:T(8,128)(2,1)S(1)}, u32[]{:S(2)}, u32[]{:S(2)}) collective-permute-start(bf16[256,256]{1,0:T(8,128)(2,1)S(1)} %get-tuple-element.52), channel_id=1, source_target_pairs={{0,8},{1,9},{2,10},{3,11},{4,12},{5,13},{6,14},{7,15},{8,0},{9,1},... | collective-permute-start | bytes 393224 | tf_op jit(solution)/shard_map/ppermute | solution.py:155
  26.9 0.6 %collective-permute-done.13.refs_2_ = bf16[512,128]{1,0:T(8,128)(2,1)S(1)} collective-permute-done((bf16[512,128]{1,0:T(8,128)(2,1)S(1)}, bf16[512,128]{1,0:T(8,128)(2,1)S(1)}, u32[]{:S(2)}, u32[]{:S(2)}) %collective-permute-start.13) | collective-permute-done | bytes 131104 | tf_op jit(solution)/shard_map/ppermute | solution.py:155
  27.4 0.6 %terms.1 = (f32[256,128]{1,0:T(8,128)S(1)}, bf16[256,128]{1,0:T(8,128)(2,1)S(1)}, bf16[256,128]{1,0:T(8,128)(2,1)S(1)}, bf16[256,128]{1,0:T(8,128)(2,1)S(1)}) custom-call(bf16[6,256,256]{2,1,0:T(8,128)(2,1)S(1)} %get-tuple-element.53.refs_0_, bf16[512,128]{1,0:T(8,128)(2,1)S(1)} %get-tuple-element.54.refs_1_, ...), custom_call_target="tpu_custom_call" | custom-call | tf_op jit(solution)/shard_map/terms/pallas_call | solution.py:383
  28.0 1.8 %collective-permute-start.14 = (bf16[256,128]{1,0:T(8,128)(2,1)S(1)}, bf16[256,128]{1,0:T(8,128)(2,1)S(1)}, u32[]{:S(2)}, u32[]{:S(2)}) collective-permute-start(bf16[256,128]{1,0:T(8,128)(2,1)S(1)} %get-tuple-element.57), channel_id=1, source_target_pairs={{0,24},{1,25},{2,26},{3,27},{4,28},{5,29},{6,30},{7,31},{8,16},{9,... | collective-permute-start | bytes 196616 | tf_op jit(solution)/shard_map/ppermute | solution.py:155
  29.9 0.5 %collective-permute-start.15 = (bf16[256,128]{1,0:T(8,128)(2,1)S(1)}, bf16[256,128]{1,0:T(8,128)(2,1)S(1)}, u32[]{:S(2)}, u32[]{:S(2)}) collective-permute-start(bf16[256,128]{1,0:T(8,128)(2,1)S(1)} %get-tuple-element.58), channel_id=1, source_target_pairs={{0,16},{1,17},{2,18},{3,19},{4,20},{5,21},{6,22},{7,23},{8,24},{9,... | collective-permute-start | bytes 196616 | tf_op jit(solution)/shard_map/ppermute | solution.py:155
  30.4 1.2 %collective-permute-start.16 = (bf16[256,128]{1,0:T(8,128)(2,1)S(1)}, bf16[256,128]{1,0:T(8,128)(2,1)S(1)}, u32[]{:S(2)}, u32[]{:S(2)}) collective-permute-start(bf16[256,128]{1,0:T(8,128)(2,1)S(1)} %get-tuple-element.59), channel_id=1, source_target_pairs={{0,8},{1,9},{2,10},{3,11},{4,12},{5,13},{6,14},{7,15},{8,0},{9,1},... | collective-permute-start | bytes 196616 | tf_op jit(solution)/shard_map/ppermute | solution.py:155
  31.6 2.1 %collective-permute-done.14.refs_1_ = bf16[256,128]{1,0:T(8,128)(2,1)S(1)} collective-permute-done((bf16[256,128]{1,0:T(8,128)(2,1)S(1)}, bf16[256,128]{1,0:T(8,128)(2,1)S(1)}, u32[]{:S(2)}, u32[]{:S(2)}) %collective-permute-start.14) | collective-permute-done | bytes 65568 | tf_op jit(solution)/shard_map/ppermute | solution.py:155
  33.7 0.5 %collective-permute-done.15.refs_2_ = bf16[256,128]{1,0:T(8,128)(2,1)S(1)} collective-permute-done((bf16[256,128]{1,0:T(8,128)(2,1)S(1)}, bf16[256,128]{1,0:T(8,128)(2,1)S(1)}, u32[]{:S(2)}, u32[]{:S(2)}) %collective-permute-start.15) | collective-permute-done | bytes 65568 | tf_op jit(solution)/shard_map/ppermute | solution.py:155
  34.1 0.7 %collective-permute-done.16.refs_3_ = bf16[256,128]{1,0:T(8,128)(2,1)S(1)} collective-permute-done((bf16[256,128]{1,0:T(8,128)(2,1)S(1)}, bf16[256,128]{1,0:T(8,128)(2,1)S(1)}, u32[]{:S(2)}, u32[]{:S(2)}) %collective-permute-start.16) | collective-permute-done | bytes 65568 | tf_op jit(solution)/shard_map/ppermute | solution.py:155
  34.8 0.1 chips.1
  34.9 1.6 %collective-permute-start.19 = (bf16[72,128]{1,0:T(8,128)(2,1)S(1)}, bf16[72,128]{1,0:T(8,128)(2,1)S(1)}, u32[]{:S(2)}, u32[]{:S(2)}) collective-permute-start(bf16[72,128]{1,0:T(8,128)(2,1)S(1)} %get-tuple-element.63), channel_id=1, source_target_pairs={{0,3},{1,2},{2,1},{3,0},{4,7},{5,6},{6,5},{7,4},{8,11},{9,10},{10,... | collective-permute-start | bytes 55304 | tf_op jit(solution)/shard_map/ppermute | solution.py:155
  36.5 0.4 collective-permute-start.18
  36.9 2.4 %collective-permute-start.17 = (bf16[72,128]{1,0:T(8,128)(2,1)S(1)}, bf16[72,128]{1,0:T(8,128)(2,1)S(1)}, u32[]{:S(2)}, u32[]{:S(2)}) collective-permute-start(bf16[72,128]{1,0:T(8,128)(2,1)S(1)} %get-tuple-element.61), channel_id=1, source_target_pairs={{0,1},{1,0},{2,3},{3,2},{4,5},{5,4},{6,7},{7,6},{8,9},{9,8},{10,11... | collective-permute-start | bytes 55304 | tf_op jit(solution)/shard_map/ppermute | solution.py:155
  39.3 0.0 collective-permute-done.12
  39.4 1.2 %collective-permute-done.19 = bf16[72,128]{1,0:T(8,128)(2,1)S(1)} collective-permute-done((bf16[72,128]{1,0:T(8,128)(2,1)S(1)}, bf16[72,128]{1,0:T(8,128)(2,1)S(1)}, u32[]{:S(2)}, u32[]{:S(2)}) %collective-permute-start.19) | collective-permute-done | bytes 18464 | tf_op jit(solution)/shard_map/ppermute | solution.py:155
  40.6 0.8 %collective-permute-done.18 = bf16[72,128]{1,0:T(8,128)(2,1)S(1)} collective-permute-done((bf16[72,128]{1,0:T(8,128)(2,1)S(1)}, bf16[72,128]{1,0:T(8,128)(2,1)S(1)}, u32[]{:S(2)}, u32[]{:S(2)}) %collective-permute-start.18) | collective-permute-done | bytes 18464 | tf_op jit(solution)/shard_map/ppermute | solution.py:155
  41.4 0.0 collective-permute-done.17
  41.4 0.1 collective-permute-start.20
  41.5 0.7 %pad_maximum_fusion.3 = bf16[2,256,256]{2,1,0:T(8,128)(2,1)} fusion(bf16[1,256,256]{2,1,0:T(8,128)(2,1)S(1)} %get-tuple-element.65, bf16[1,256,256]{2,1,0:T(8,128)(2,1)S(1)} %get-tuple-element.64), kind=kLoop, calls=%fused_computation.3 | loop fusion | flops 131072 | bytes 524288 | tf_op jit(solution)/shard_map/stack | solution.py:463
  42.2 0.5 %collective-permute-done.20.refs_1_ = f32[72,128]{1,0:T(8,128)S(1)} collective-permute-done((f32[72,128]{1,0:T(8,128)S(1)}, f32[72,128]{1,0:T(8,128)S(1)}, u32[]{:S(2)}, u32[]{:S(2)}) %collective-permute-start.20) | collective-permute-done | bytes 36896 | tf_op jit(solution)/shard_map/ppermute | solution.py:155
  42.7 0.6 %total.1 = f32[144,128]{1,0:T(8,128)} custom-call(f32[72,128]{1,0:T(8,128)S(1)} %convert_add_fusion.refs_0_, f32[72,128]{1,0:T(8,128)S(1)} %collective-permute-done.20.refs_1_), custom_call_target="tpu_custom_call" | custom-call | tf_op jit(solution)/shard_map/total/pallas_call | solution.py:383
  (15 shorter events, 0.2 us)
Async XLA Ops:
  0.6 18.3 %copy-start = (f32[360,4,256]{2,1,0:T(4,128)S(1)}, f32[360,4,256]{2,1,0:T(4,128)}, u32[]{:S(2)}) copy-start(f32[360,4,256]{2,1,0:T(4,128)} %param.7) | copy-start | bytes 4423684
  0.6 17.6 %copy-start.1 = (bf16[1,64,8,256]{3,2,1,0:T(8,128)(2,1)S(1)}, bf16[1,64,8,256]{3,2,1,0:T(8,128)(2,1)}, u32[]{:S(2)}) copy-start(bf16[1,64,8,256]{3,2,1,0:T(8,128)(2,1)} %param.5) | copy-start | bytes 786436
  0.7 18.2 %copy-start.2 = (bf16[1,64,8,256]{3,2,1,0:T(8,128)(2,1)S(1)}, bf16[1,64,8,256]{3,2,1,0:T(8,128)(2,1)}, u32[]{:S(2)}) copy-start(bf16[1,64,8,256]{3,2,1,0:T(8,128)(2,1)} %param.9) | copy-start | bytes 786436
  1.7 4.2 %collective-permute-start = (bf16[2,72,128]{2,1,0:T(8,128)(2,1)S(1)}, bf16[2,72,128]{2,1,0:T(8,128)(2,1)S(1)}, u32[]{:S(2)}, u32[]{:S(2)}) collective-permute-start(bf16[2,72,128]{2,1,0:T(8,128)(2,1)S(1)} %broadcast_select_fusion), channel_id=1, source_target_pairs={{0,4},{1,5},{2,6},{3,7},{4,0},{5,1},{6,2},{7,3},{8,12},{9,13},{10,... | collective-permute-start | bytes 110600 | tf_op jit(solution)/shard_map/ppermute | solution.py:155
  3.3 15.0 %collective-permute-start.8 = (bf16[2,256,256]{2,1,0:T(8,128)(2,1)S(1)}, bf16[2,256,256]{2,1,0:T(8,128)(2,1)S(1)}, u32[]{:S(2)}, u32[]{:S(2)}) collective-permute-start(bf16[2,256,256]{2,1,0:T(8,128)(2,1)S(1)} %pad_maximum_fusion), channel_id=1, source_target_pairs={{0,8},{1,9},{2,10},{3,11},{4,12},{5,13},{6,14},{7,15},{8,0},{9,1},... | collective-permute-start | bytes 786440 | tf_op jit(solution)/shard_map/ppermute | solution.py:155
  6.0 5.8 %collective-permute-start.1 = (bf16[2,72,128]{2,1,0:T(8,128)(2,1)S(1)}, bf16[2,72,128]{2,1,0:T(8,128)(2,1)S(1)}, u32[]{:S(2)}, u32[]{:S(2)}) collective-permute-start(bf16[2,72,128]{2,1,0:T(8,128)(2,1)S(1)} %select_select_fusion.refs_0_), channel_id=1, source_target_pairs={{0,3},{1,2},{2,1},{3,0},{4,7},{5,6},{6,5},{7,4},{8,11},{9,10},{10,... | collective-permute-start | bytes 110600 | tf_op jit(solution)/shard_map/ppermute | solution.py:155
  9.7 4.9 %collective-permute-start.2 = (bf16[2,72,128]{2,1,0:T(8,128)(2,1)S(1)}, bf16[2,72,128]{2,1,0:T(8,128)(2,1)S(1)}, u32[]{:S(2)}, u32[]{:S(2)}) collective-permute-start(bf16[2,72,128]{2,1,0:T(8,128)(2,1)S(1)} %select_select_fusion.refs_0_), channel_id=1, source_target_pairs={{0,2},{1,3},{2,0},{3,1},{4,6},{5,7},{6,4},{7,5},{8,10},{9,11},{10,... | collective-permute-start | bytes 110600 | tf_op jit(solution)/shard_map/ppermute | solution.py:155
  9.7 4.9 %collective-permute-start.3 = (bf16[2,72,128]{2,1,0:T(8,128)(2,1)S(1)}, bf16[2,72,128]{2,1,0:T(8,128)(2,1)S(1)}, u32[]{:S(2)}, u32[]{:S(2)}) collective-permute-start(bf16[2,72,128]{2,1,0:T(8,128)(2,1)S(1)} %select_select_fusion.refs_0_), channel_id=1, source_target_pairs={{0,1},{1,0},{2,3},{3,2},{4,5},{5,4},{6,7},{7,6},{8,9},{9,8},{10,11... | collective-permute-start | bytes 110600 | tf_op jit(solution)/shard_map/ppermute | solution.py:155
  14.7 7.0 %collective-permute-start.4 = (bf16[2,256,128]{2,1,0:T(8,128)(2,1)S(1)}, bf16[2,256,128]{2,1,0:T(8,128)(2,1)S(1)}, u32[]{:S(2)}, u32[]{:S(2)}) collective-permute-start(bf16[2,256,128]{2,1,0:T(8,128)(2,1)S(1)} %line.1), channel_id=1, source_target_pairs={{0,24},{1,25},{2,26},{3,27},{4,28},{5,29},{6,30},{7,31},{8,16},{9,... | collective-permute-start | bytes 393224 | tf_op jit(solution)/shard_map/ppermute | solution.py:155
  16.2 5.9 %collective-permute-start.5 = (bf16[2,256,128]{2,1,0:T(8,128)(2,1)S(1)}, bf16[2,256,128]{2,1,0:T(8,128)(2,1)S(1)}, u32[]{:S(2)}, u32[]{:S(2)}) collective-permute-start(bf16[2,256,128]{2,1,0:T(8,128)(2,1)S(1)} %line.1), channel_id=1, source_target_pairs={{0,16},{1,17},{2,18},{3,19},{4,20},{5,21},{6,22},{7,23},{8,24},{9,... | collective-permute-start | bytes 393224 | tf_op jit(solution)/shard_map/ppermute | solution.py:155
  16.7 6.3 %collective-permute-start.6 = (bf16[2,256,128]{2,1,0:T(8,128)(2,1)S(1)}, bf16[2,256,128]{2,1,0:T(8,128)(2,1)S(1)}, u32[]{:S(2)}, u32[]{:S(2)}) collective-permute-start(bf16[2,256,128]{2,1,0:T(8,128)(2,1)S(1)} %line.1), channel_id=1, source_target_pairs={{0,8},{1,9},{2,10},{3,11},{4,12},{5,13},{6,14},{7,15},{8,0},{9,1},... | collective-permute-start | bytes 393224 | tf_op jit(solution)/shard_map/ppermute | solution.py:155
  18.2 4.8 %collective-permute-start.7 = (bf16[256,256]{1,0:T(8,128)(2,1)S(1)}, bf16[256,256]{1,0:T(8,128)(2,1)S(1)}, u32[]{:S(2)}, u32[]{:S(2)}) collective-permute-start(bf16[256,256]{1,0:T(8,128)(2,1)S(1)} %dynamic-slice_bitcast_fusion.1.refs_0_), channel_id=1, source_target_pairs={{0,4},{1,5},{2,6},{3,7},{4,0},{5,1},{6,2},{7,3},{8,12},{9,13},{10,... | collective-permute-start | bytes 393224 | tf_op jit(solution)/shard_map/ppermute | solution.py:155
  18.3 4.7 %collective-permute-start.9 = (bf16[256,256]{1,0:T(8,128)(2,1)S(1)}, bf16[256,256]{1,0:T(8,128)(2,1)S(1)}, u32[]{:S(2)}, u32[]{:S(2)}) collective-permute-start(bf16[256,256]{1,0:T(8,128)(2,1)S(1)} %slice_bitcast_fusion), channel_id=1, source_target_pairs={{0,4},{1,5},{2,6},{3,7},{4,0},{5,1},{6,2},{7,3},{8,12},{9,13},{10,... | collective-permute-start | bytes 393224 | tf_op jit(solution)/shard_map/ppermute | solution.py:155
  23.1 1.6 %collective-permute-start.10 = (bf16[4,256,128]{2,1,0:T(8,128)(2,1)S(1)}, bf16[4,256,128]{2,1,0:T(8,128)(2,1)S(1)}, u32[]{:S(2)}, u32[]{:S(2)}) collective-permute-start(bf16[4,256,128]{2,1,0:T(8,128)(2,1)S(1)} %pad_maximum_fusion.1.refs_4_), channel_id=1, source_target_pairs={{0,4},{1,5},{2,6},{3,7},{4,0},{5,1},{6,2},{7,3},{8,12},{9,13},{10,... | collective-permute-start | bytes 786440 | tf_op jit(solution)/shard_map/ppermute | solution.py:155
  23.3 1.9 %collective-permute-start.11 = (bf16[4,256,128]{2,1,0:T(8,128)(2,1)S(1)}, bf16[4,256,128]{2,1,0:T(8,128)(2,1)S(1)}, u32[]{:S(2)}, u32[]{:S(2)}) collective-permute-start(bf16[4,256,128]{2,1,0:T(8,128)(2,1)S(1)} %pad_maximum_fusion.2.refs_4_), channel_id=1, source_target_pairs={{0,4},{1,5},{2,6},{3,7},{4,0},{5,1},{6,2},{7,3},{8,12},{9,13},{10,... | collective-permute-start | bytes 786440 | tf_op jit(solution)/shard_map/ppermute | solution.py:155
  26.0 1.4 %collective-permute-start.13 = (bf16[512,128]{1,0:T(8,128)(2,1)S(1)}, bf16[512,128]{1,0:T(8,128)(2,1)S(1)}, u32[]{:S(2)}, u32[]{:S(2)}) collective-permute-start(bf16[512,128]{1,0:T(8,128)(2,1)S(1)} %get-tuple-element.55), channel_id=1, source_target_pairs={{0,4},{1,5},{2,6},{3,7},{4,0},{5,1},{6,2},{7,3},{8,12},{9,13},{10,... | collective-permute-start | bytes 393224 | tf_op jit(solution)/shard_map/ppermute | solution.py:155
  26.2 13.1 %collective-permute-start.12 = (bf16[256,256]{1,0:T(8,128)(2,1)S(1)}, bf16[256,256]{1,0:T(8,128)(2,1)S(1)}, u32[]{:S(2)}, u32[]{:S(2)}) collective-permute-start(bf16[256,256]{1,0:T(8,128)(2,1)S(1)} %get-tuple-element.52), channel_id=1, source_target_pairs={{0,8},{1,9},{2,10},{3,11},{4,12},{5,13},{6,14},{7,15},{8,0},{9,1},... | collective-permute-start | bytes 393224 | tf_op jit(solution)/shard_map/ppermute | solution.py:155
  28.0 5.6 %collective-permute-start.14 = (bf16[256,128]{1,0:T(8,128)(2,1)S(1)}, bf16[256,128]{1,0:T(8,128)(2,1)S(1)}, u32[]{:S(2)}, u32[]{:S(2)}) collective-permute-start(bf16[256,128]{1,0:T(8,128)(2,1)S(1)} %get-tuple-element.57), channel_id=1, source_target_pairs={{0,24},{1,25},{2,26},{3,27},{4,28},{5,29},{6,30},{7,31},{8,16},{9,... | collective-permute-start | bytes 196616 | tf_op jit(solution)/shard_map/ppermute | solution.py:155
  29.9 4.3 %collective-permute-start.15 = (bf16[256,128]{1,0:T(8,128)(2,1)S(1)}, bf16[256,128]{1,0:T(8,128)(2,1)S(1)}, u32[]{:S(2)}, u32[]{:S(2)}) collective-permute-start(bf16[256,128]{1,0:T(8,128)(2,1)S(1)} %get-tuple-element.58), channel_id=1, source_target_pairs={{0,16},{1,17},{2,18},{3,19},{4,20},{5,21},{6,22},{7,23},{8,24},{9,... | collective-permute-start | bytes 196616 | tf_op jit(solution)/shard_map/ppermute | solution.py:155
  30.4 4.4 %collective-permute-start.16 = (bf16[256,128]{1,0:T(8,128)(2,1)S(1)}, bf16[256,128]{1,0:T(8,128)(2,1)S(1)}, u32[]{:S(2)}, u32[]{:S(2)}) collective-permute-start(bf16[256,128]{1,0:T(8,128)(2,1)S(1)} %get-tuple-element.59), channel_id=1, source_target_pairs={{0,8},{1,9},{2,10},{3,11},{4,12},{5,13},{6,14},{7,15},{8,0},{9,1},... | collective-permute-start | bytes 196616 | tf_op jit(solution)/shard_map/ppermute | solution.py:155
  34.9 5.7 %collective-permute-start.19 = (bf16[72,128]{1,0:T(8,128)(2,1)S(1)}, bf16[72,128]{1,0:T(8,128)(2,1)S(1)}, u32[]{:S(2)}, u32[]{:S(2)}) collective-permute-start(bf16[72,128]{1,0:T(8,128)(2,1)S(1)} %get-tuple-element.63), channel_id=1, source_target_pairs={{0,3},{1,2},{2,1},{3,0},{4,7},{5,6},{6,5},{7,4},{8,11},{9,10},{10,... | collective-permute-start | bytes 55304 | tf_op jit(solution)/shard_map/ppermute | solution.py:155
  36.5 4.9 %collective-permute-start.18 = (bf16[72,128]{1,0:T(8,128)(2,1)S(1)}, bf16[72,128]{1,0:T(8,128)(2,1)S(1)}, u32[]{:S(2)}, u32[]{:S(2)}) collective-permute-start(bf16[72,128]{1,0:T(8,128)(2,1)S(1)} %get-tuple-element.62), channel_id=1, source_target_pairs={{0,2},{1,3},{2,0},{3,1},{4,6},{5,7},{6,4},{7,5},{8,10},{9,11},{10,... | collective-permute-start | bytes 55304 | tf_op jit(solution)/shard_map/ppermute | solution.py:155
  36.9 4.5 %collective-permute-start.17 = (bf16[72,128]{1,0:T(8,128)(2,1)S(1)}, bf16[72,128]{1,0:T(8,128)(2,1)S(1)}, u32[]{:S(2)}, u32[]{:S(2)}) collective-permute-start(bf16[72,128]{1,0:T(8,128)(2,1)S(1)} %get-tuple-element.61), channel_id=1, source_target_pairs={{0,1},{1,0},{2,3},{3,2},{4,5},{5,4},{6,7},{7,6},{8,9},{9,8},{10,11... | collective-permute-start | bytes 55304 | tf_op jit(solution)/shard_map/ppermute | solution.py:155
  41.4 1.3 %collective-permute-start.20 = (f32[72,128]{1,0:T(8,128)S(1)}, f32[72,128]{1,0:T(8,128)S(1)}, u32[]{:S(2)}, u32[]{:S(2)}) collective-permute-start(f32[72,128]{1,0:T(8,128)S(1)} %convert_add_fusion.refs_0_), channel_id=1, source_target_pairs={{0,4},{1,5},{2,6},{3,7},{4,0},{5,1},{6,2},{7,3},{8,12},{9,13},{10,... | collective-permute-start | bytes 110600 | tf_op jit(solution)/shard_map/ppermute | solution.py:155

commit v4 on v3

--- a/solution.py
+++ b/solution.py
@@ -210,6 +210,10 @@
         self.column_rows = max(self.count.values())
         assert all(start + self.column_rows <= 3 * width for start in self.start.values())
         assert len(self.base) == len(self.pieces)
+
+
+def copy_kernel(layout, value_ref, out_ref):
+    out_ref[...] = value_ref[...]
 
 
 def line_kernel(layout, own_ref, far0_ref, far1_ref, far2_ref, out_ref, total):
@@ -377,7 +381,7 @@
     bf16, f32 = jnp.bfloat16, jnp.float32
     shape = jax.ShapeDtypeStruct
 
-    def call(name, body, out_shape, scratch, *operands):
+    def call(name, body, out_shape, scratch, *operands, cost=0):
         vmem = pl.BlockSpec(memory_space=pltpu.VMEM)
         several = isinstance(out_shape, tuple)
         return pl.pallas_call(
@@ -387,19 +391,27 @@
             out_specs=(vmem,) * len(out_shape) if several else vmem,
             scratch_shapes=scratch,
             compiler_params=pltpu.CompilerParams(vmem_limit_bytes=16 * 1024 * 1024),
+            cost_estimate=pl.CostEstimate(flops=cost * 10**9, bytes_accessed=0, transcendentals=0) if cost else None,
             name=name,
         )(*operands)
 
-    shard = flat_weights.reshape(2, shard_rows, width)
+    near_flat = moved(flat_weights, dc=1)
+    halves_x, halves_ct = (array.reshape(2, half, width) for array in (inputs, cotangent))
+    pick = lambda halves, number: lax.dynamic_index_in_dim(halves, number, 0, keepdims=False)
+    give = jnp.stack([pick(halves_x, 1 - y), pick(halves_ct, 1 - y)])
+    near_flat, give = lax.optimization_barrier((near_flat, give))
+    shard = moved(near_flat, dc=1).reshape(2, shard_rows, width)
+    give = call("give", copy_kernel, shape(give.shape, bf16), [], give, cost=3)
+    other = moved(give, dy=1)
     left, right = shard[:, :, :lane], shard[:, :, lane:]
-    near = moved(jnp.where(c == 0, right, left), dc=1)
+    near = near_flat.reshape(shard.shape)
+    near = jnp.where(c == 0, near[:, :, :lane], near[:, :, lane:])
     row = lax.broadcasted_iota(jnp.int32, near.shape, 1)
     from_one = row < chosen(layout.low, (x, y, z), 0)
     piece = jnp.where(from_one == (c == 1), jnp.where(c == 0, left, right), near)
 
     halves_x, halves_ct = (array.reshape(2, half, width) for array in (inputs, cotangent))
     pick = lambda halves, number: lax.dynamic_index_in_dim(halves, number, 0, keepdims=False)
-    other = moved(jnp.stack([pick(halves_x, 1 - y), pick(halves_ct, 1 - y)]), dy=1)
     line = [piece, *(moved(piece, dz=dz) for dz in Z_ORDER)]
     *line, halves_x, halves_ct, film = lax.optimization_barrier(
         (*line, halves_x, halves_ct, film)

time: 43.5 us -> 43.1 us (level)
  starting transfers between devices: 21.3 us -> 22.4 us
  local copies, waits for them, and re-layouts: 2.11 us -> 1.1 us
  waiting for transfers between devices: 14.7 us -> 14.2 us
    ppermute x21 -> x22, starting transfers between devices: 21.3 us -> 22.4 us  [moved(): lax.ppermute(value, AXES, pairs(lambda x, y, c, z: (x ^ dx, y ^ dy, c ^ d...]
    unnamed x7 -> x8, local copies, waits for them, and re-layouts: 1.05 us -> 0.04 us
    ppermute x21 -> x22, waiting for transfers between devices: 14.7 us -> 14.2 us  [moved(): lax.ppermute(value, AXES, pairs(lambda x, y, c, z: (x ^ dx, y ^ dy, c ^ d...]
    pallas_call x6 -> x7, Pallas kernels: 2.71 us -> 2.73 us  [call(): pl.pallas_call(lambda *refs: body(layout, *refs), out_shape=out_shape, in...]
  transfers between devices with their start and end apart: 21 -> 22, of which waited for: 13 -> 12; matrix products, arithmetic and copies ran while one was open for 4% -> 5% of each run, Pallas kernels for 3% -> 3%
where the time goes in v4:
time: 43.1 us; the launch traced here: 42.9 us
  starting transfers between devices  22.4 us (52%)
  waiting for transfers between devices  14.2 us (33%)
  Pallas kernels  2.73 us (6%)
  between operations  1.55 us (4%)
  local copies, waits for them, and re-layouts  1.1 us (3%)
  other arithmetic  0.95 us (2%)
    ppermute x22, starting transfers between devices, moved(): lax.ppermute(value, AXES, pairs(lambda x, y, c, z: (x ^ dx, y ^ dy, c ^ d...  22.4 us
    ppermute x22, waiting for transfers between devices, moved(): lax.ppermute(value, AXES, pairs(lambda x, y, c, z: (x ^ dx, y ^ dy, c ^ d...  14.2 us
    pallas_call x7, Pallas kernels, call(): pl.pallas_call(lambda *refs: body(layout, *refs), out_shape=out_shape, in...  2.73 us
    dynamic_slice x1, local copies, waits for them, and re-layouts, row_shards(): lax.dynamic_index_in_dim(halves, number, 0, keepdims=False)  0.98 us
  transfers between devices with their start and end apart: 22, of which 12 were waited for; matrix products, arithmetic and copies ran while one was open for 5% of the time, Pallas kernels for 3%

profile of v4, /device:TPU:0, one launch (start us, length us, event | category | flops | bytes accessed | tf_op | source)
XLA Modules:
  0.0 42.9 jit_solution(9316963538235602615)
XLA Ops:
  0.6 0.0 copy-start
  0.6 0.5 %collective-permute-start = (bf16[2,18432]{1,0:T(2,128)(2,1)}, bf16[2,18432]{1,0:T(2,128)(2,1)S(1)}, u32[]{:S(2)}, u32[]{:S(2)}) collective-permute-start(bf16[2,18432]{1,0:T(2,128)(2,1)} %param.8), channel_id=1, source_target_pairs={{0,4},{1,5},{2,6},{3,7},{4,0},{5,1},{6,2},{7,3},{8,12},{9,13},{10,... | collective-permute-start | bytes 221192 | tf_op jit(solution)/shard_map/ppermute | solution.py:155
  1.2 1.0 %constant_dynamic-slice_fusion = (bf16[1,256,256]{2,1,0:T(8,128)(2,1)S(1)}, bf16[1,256,256]{2,1,0:T(8,128)(2,1)S(1)}) fusion(bf16[2,256,256]{2,1,0:T(8,128)(2,1)} %bitcast.32, s32[]{:T(128)S(6)} %select_n.86, bf16[2,256,256]{2,1,0:T(8,128)(2,1)} %bitcast.30), kind=kLoop, calls=%fused_computation.17 | loop fusion | bytes 524292 | tf_op jit(solution)/shard_map/jit(dynamic_index_in_dim)/dynamic_slice | solution.py:400
  2.2 0.0 copy-start.1
  2.3 0.0 copy-start.2
  2.3 0.0 collective-permute-done
  2.3 0.4 collective-permute-start.1
  2.7 2.8 %collective-permute-start.9 = (bf16[2,256,256]{2,1,0:T(8,128)(2,1)S(1)}, bf16[2,256,256]{2,1,0:T(8,128)(2,1)S(1)}, u32[]{:S(2)}, u32[]{:S(2)}) collective-permute-start(bf16[2,256,256]{2,1,0:T(8,128)(2,1)S(1)} %give.1), channel_id=1, source_target_pairs={{0,8},{1,9},{2,10},{3,11},{4,12},{5,13},{6,14},{7,15},{8,0},{9,1},... | collective-permute-start | bytes 786440 | tf_op jit(solution)/shard_map/ppermute | solution.py:155
  5.5 0.0 collective-permute-done.1
  5.5 0.1 fusion.refs_0_
  5.6 3.7 %collective-permute-start.2 = (bf16[2,72,128]{2,1,0:T(8,128)(2,1)S(1)}, bf16[2,72,128]{2,1,0:T(8,128)(2,1)S(1)}, u32[]{:S(2)}, u32[]{:S(2)}) collective-permute-start(bf16[2,72,128]{2,1,0:T(8,128)(2,1)S(1)} %fusion.refs_0_), channel_id=1, source_target_pairs={{0,3},{1,2},{2,1},{3,0},{4,7},{5,6},{6,5},{7,4},{8,11},{9,10},{10,... | collective-permute-start | bytes 110600 | tf_op jit(solution)/shard_map/ppermute | solution.py:155
  9.2 0.0 collective-permute-start.3
  9.2 0.8 %collective-permute-start.4 = (bf16[2,72,128]{2,1,0:T(8,128)(2,1)S(1)}, bf16[2,72,128]{2,1,0:T(8,128)(2,1)S(1)}, u32[]{:S(2)}, u32[]{:S(2)}) collective-permute-start(bf16[2,72,128]{2,1,0:T(8,128)(2,1)S(1)} %fusion.refs_0_), channel_id=1, source_target_pairs={{0,1},{1,0},{2,3},{3,2},{4,5},{5,4},{6,7},{7,6},{8,9},{9,8},{10,11... | collective-permute-start | bytes 110600 | tf_op jit(solution)/shard_map/ppermute | solution.py:155
  10.7 0.7 %collective-permute-done.2.refs_1_ = bf16[2,72,128]{2,1,0:T(8,128)(2,1)S(1)} collective-permute-done((bf16[2,72,128]{2,1,0:T(8,128)(2,1)S(1)}, bf16[2,72,128]{2,1,0:T(8,128)(2,1)S(1)}, u32[]{:S(2)}, u32[]{:S(2)}) %collective-permute-start.2) | collective-permute-done | bytes 36896 | tf_op jit(solution)/shard_map/ppermute | solution.py:155
  11.4 2.7 %collective-permute-done.3.refs_2_ = bf16[2,72,128]{2,1,0:T(8,128)(2,1)S(1)} collective-permute-done((bf16[2,72,128]{2,1,0:T(8,128)(2,1)S(1)}, bf16[2,72,128]{2,1,0:T(8,128)(2,1)S(1)}, u32[]{:S(2)}, u32[]{:S(2)}) %collective-permute-start.3) | collective-permute-done | bytes 36896 | tf_op jit(solution)/shard_map/ppermute | solution.py:155
  14.1 0.0 collective-permute-done.4.refs_3_
  14.1 0.1 line.1
  14.2 1.9 %collective-permute-start.5 = (bf16[2,256,128]{2,1,0:T(8,128)(2,1)S(1)}, bf16[2,256,128]{2,1,0:T(8,128)(2,1)S(1)}, u32[]{:S(2)}, u32[]{:S(2)}) collective-permute-start(bf16[2,256,128]{2,1,0:T(8,128)(2,1)S(1)} %line.1), channel_id=1, source_target_pairs={{0,24},{1,25},{2,26},{3,27},{4,28},{5,29},{6,30},{7,31},{8,16},{9,... | collective-permute-start | bytes 393224 | tf_op jit(solution)/shard_map/ppermute | solution.py:155
  16.2 0.5 %collective-permute-start.6 = (bf16[2,256,128]{2,1,0:T(8,128)(2,1)S(1)}, bf16[2,256,128]{2,1,0:T(8,128)(2,1)S(1)}, u32[]{:S(2)}, u32[]{:S(2)}) collective-permute-start(bf16[2,256,128]{2,1,0:T(8,128)(2,1)S(1)} %line.1), channel_id=1, source_target_pairs={{0,16},{1,17},{2,18},{3,19},{4,20},{5,21},{6,22},{7,23},{8,24},{9,... | collective-permute-start | bytes 393224 | tf_op jit(solution)/shard_map/ppermute | solution.py:155
  16.7 1.1 %collective-permute-start.7 = (bf16[2,256,128]{2,1,0:T(8,128)(2,1)S(1)}, bf16[2,256,128]{2,1,0:T(8,128)(2,1)S(1)}, u32[]{:S(2)}, u32[]{:S(2)}) collective-permute-start(bf16[2,256,128]{2,1,0:T(8,128)(2,1)S(1)} %line.1), channel_id=1, source_target_pairs={{0,8},{1,9},{2,10},{3,11},{4,12},{5,13},{6,14},{7,15},{8,0},{9,1},... | collective-permute-start | bytes 393224 | tf_op jit(solution)/shard_map/ppermute | solution.py:155
  17.8 0.0 copy-done.1
  17.8 0.1 collective-permute-start.8
  17.9 0.0 collective-permute-done.9.refs_1_.refs_3_
  17.9 0.6 %collective-permute-start.10 = (bf16[256,256]{1,0:T(8,128)(2,1)S(1)}, bf16[256,256]{1,0:T(8,128)(2,1)S(1)}, u32[]{:S(2)}, u32[]{:S(2)}) collective-permute-start(bf16[256,256]{1,0:T(8,128)(2,1)S(1)} %slice_bitcast_fusion), channel_id=1, source_target_pairs={{0,4},{1,5},{2,6},{3,7},{4,0},{5,1},{6,2},{7,3},{8,12},{9,13},{10,... | collective-permute-start | bytes 393224 | tf_op jit(solution)/shard_map/ppermute | solution.py:155
  18.5 0.0 copy-done
  18.5 0.0 copy-done.2
  18.5 2.6 %collective-permute-done.5 = bf16[2,256,128]{2,1,0:T(8,128)(2,1)S(1)} collective-permute-done((bf16[2,256,128]{2,1,0:T(8,128)(2,1)S(1)}, bf16[2,256,128]{2,1,0:T(8,128)(2,1)S(1)}, u32[]{:S(2)}, u32[]{:S(2)}) %collective-permute-start.5) | collective-permute-done | bytes 131104 | tf_op jit(solution)/shard_map/ppermute | solution.py:155
  21.1 1.0 %collective-permute-done.6 = bf16[2,256,128]{2,1,0:T(8,128)(2,1)S(1)} collective-permute-done((bf16[2,256,128]{2,1,0:T(8,128)(2,1)S(1)}, bf16[2,256,128]{2,1,0:T(8,128)(2,1)S(1)}, u32[]{:S(2)}, u32[]{:S(2)}) %collective-permute-start.6) | collective-permute-done | bytes 131104 | tf_op jit(solution)/shard_map/ppermute | solution.py:155
  22.1 0.3 collective-permute-done.7
  22.4 0.0 collective-permute-done.8.refs_2_
  22.4 0.0 collective-permute-done.10.refs_3_
  22.5 0.1 collective-permute-start.11
  22.7 0.6 %collective-permute-start.12 = (bf16[4,256,128]{2,1,0:T(8,128)(2,1)S(1)}, bf16[4,256,128]{2,1,0:T(8,128)(2,1)S(1)}, u32[]{:S(2)}, u32[]{:S(2)}) collective-permute-start(bf16[4,256,128]{2,1,0:T(8,128)(2,1)S(1)} %pad_maximum_fusion.2.refs_4_), channel_id=1, source_target_pairs={{0,4},{1,5},{2,6},{3,7},{4,0},{5,1},{6,2},{7,3},{8,12},{9,13},{10,... | collective-permute-start | bytes 786440 | tf_op jit(solution)/shard_map/ppermute | solution.py:155
  23.2 0.9 %collective-permute-done.11.refs_5_ = bf16[4,256,128]{2,1,0:T(8,128)(2,1)S(1)} collective-permute-done((bf16[4,256,128]{2,1,0:T(8,128)(2,1)S(1)}, bf16[4,256,128]{2,1,0:T(8,128)(2,1)S(1)}, u32[]{:S(2)}, u32[]{:S(2)}) %collective-permute-start.11) | collective-permute-done | bytes 262176 | tf_op jit(solution)/shard_map/ppermute | solution.py:155
  24.1 0.4 %block_one.1 = (bf16[6,256,256]{2,1,0:T(8,128)(2,1)S(1)}, f32[512,256]{1,0:T(8,128)S(1)}, bf16[512,256]{1,0:T(8,128)(2,1)S(1)}) custom-call(bf16[256,256]{1,0:T(8,128)(2,1)S(1)} %dynamic-slice_bitcast_fusion.1.refs_0_, bf16[2,256,256]{2,1,0:T(8,128)(2,1)S(1)} %collective-permute-done.9.refs_1_.refs_3_, bf16[256,256]{1,0:T(8,128)(2,1)S(1)} %collective-permute-done.8.refs_2_, ...), custom_call_target="tpu_custom_call" | custom-call | tf_op jit(solution)/shard_map/block_one/pallas_call | solution.py:387
  24.6 0.0 collective-permute-done.12.refs_5_
  24.6 0.8 %block_two.1 = (bf16[256,256]{1,0:T(8,128)(2,1)S(1)}, bf16[256,256]{1,0:T(8,128)(2,1)S(1)}, bf16[512,128]{1,0:T(8,128)(2,1)S(1)}, bf16[512,128]{1,0:T(8,128)(2,1)S(1)}) custom-call(f32[512,256]{1,0:T(8,128)S(1)} %get-tuple-element.52.refs_0_, bf16[512,256]{1,0:T(8,128)(2,1)S(1)} %get-tuple-element.53.refs_1_, ...), custom_call_target="tpu_custom_call" | custom-call | tf_op jit(solution)/shard_map/block_two/pallas_call | solution.py:387
  25.4 0.2 collective-permute-start.14
  25.6 1.2 %collective-permute-start.13 = (bf16[256,256]{1,0:T(8,128)(2,1)S(1)}, bf16[256,256]{1,0:T(8,128)(2,1)S(1)}, u32[]{:S(2)}, u32[]{:S(2)}) collective-permute-start(bf16[256,256]{1,0:T(8,128)(2,1)S(1)} %get-tuple-element.56), channel_id=1, source_target_pairs={{0,8},{1,9},{2,10},{3,11},{4,12},{5,13},{6,14},{7,15},{8,0},{9,1},... | collective-permute-start | bytes 393224 | tf_op jit(solution)/shard_map/ppermute | solution.py:155
  26.8 0.1 collective-permute-done.14.refs_2_
  26.8 0.6 %terms.1 = (f32[256,128]{1,0:T(8,128)S(1)}, bf16[256,128]{1,0:T(8,128)(2,1)S(1)}, bf16[256,128]{1,0:T(8,128)(2,1)S(1)}, bf16[256,128]{1,0:T(8,128)(2,1)S(1)}) custom-call(bf16[6,256,256]{2,1,0:T(8,128)(2,1)S(1)} %get-tuple-element.57.refs_0_, bf16[512,128]{1,0:T(8,128)(2,1)S(1)} %get-tuple-element.58.refs_1_, ...), custom_call_target="tpu_custom_call" | custom-call | tf_op jit(solution)/shard_map/terms/pallas_call | solution.py:387
  27.4 2.1 %collective-permute-start.15 = (bf16[256,128]{1,0:T(8,128)(2,1)S(1)}, bf16[256,128]{1,0:T(8,128)(2,1)S(1)}, u32[]{:S(2)}, u32[]{:S(2)}) collective-permute-start(bf16[256,128]{1,0:T(8,128)(2,1)S(1)} %get-tuple-element.61), channel_id=1, source_target_pairs={{0,24},{1,25},{2,26},{3,27},{4,28},{5,29},{6,30},{7,31},{8,16},{9,... | collective-permute-start | bytes 196616 | tf_op jit(solution)/shard_map/ppermute | solution.py:155
  29.6 0.5 %collective-permute-start.16 = (bf16[256,128]{1,0:T(8,128)(2,1)S(1)}, bf16[256,128]{1,0:T(8,128)(2,1)S(1)}, u32[]{:S(2)}, u32[]{:S(2)}) collective-permute-start(bf16[256,128]{1,0:T(8,128)(2,1)S(1)} %get-tuple-element.62), channel_id=1, source_target_pairs={{0,16},{1,17},{2,18},{3,19},{4,20},{5,21},{6,22},{7,23},{8,24},{9,... | collective-permute-start | bytes 196616 | tf_op jit(solution)/shard_map/ppermute | solution.py:155
  30.1 0.9 %collective-permute-start.17 = (bf16[256,128]{1,0:T(8,128)(2,1)S(1)}, bf16[256,128]{1,0:T(8,128)(2,1)S(1)}, u32[]{:S(2)}, u32[]{:S(2)}) collective-permute-start(bf16[256,128]{1,0:T(8,128)(2,1)S(1)} %get-tuple-element.63), channel_id=1, source_target_pairs={{0,8},{1,9},{2,10},{3,11},{4,12},{5,13},{6,14},{7,15},{8,0},{9,1},... | collective-permute-start | bytes 196616 | tf_op jit(solution)/shard_map/ppermute | solution.py:155
  31.0 2.1 %collective-permute-done.15.refs_1_ = bf16[256,128]{1,0:T(8,128)(2,1)S(1)} collective-permute-done((bf16[256,128]{1,0:T(8,128)(2,1)S(1)}, bf16[256,128]{1,0:T(8,128)(2,1)S(1)}, u32[]{:S(2)}, u32[]{:S(2)}) %collective-permute-start.15) | collective-permute-done | bytes 65568 | tf_op jit(solution)/shard_map/ppermute | solution.py:155
  33.1 0.8 %collective-permute-done.16.refs_2_ = bf16[256,128]{1,0:T(8,128)(2,1)S(1)} collective-permute-done((bf16[256,128]{1,0:T(8,128)(2,1)S(1)}, bf16[256,128]{1,0:T(8,128)(2,1)S(1)}, u32[]{:S(2)}, u32[]{:S(2)}) %collective-permute-start.16) | collective-permute-done | bytes 65568 | tf_op jit(solution)/shard_map/ppermute | solution.py:155
  33.8 0.5 %collective-permute-done.17.refs_3_ = bf16[256,128]{1,0:T(8,128)(2,1)S(1)} collective-permute-done((bf16[256,128]{1,0:T(8,128)(2,1)S(1)}, bf16[256,128]{1,0:T(8,128)(2,1)S(1)}, u32[]{:S(2)}, u32[]{:S(2)}) %collective-permute-start.17) | collective-permute-done | bytes 65568 | tf_op jit(solution)/shard_map/ppermute | solution.py:155
  34.4 0.1 chips.1
  34.5 1.7 %collective-permute-start.20 = (bf16[72,128]{1,0:T(8,128)(2,1)S(1)}, bf16[72,128]{1,0:T(8,128)(2,1)S(1)}, u32[]{:S(2)}, u32[]{:S(2)}) collective-permute-start(bf16[72,128]{1,0:T(8,128)(2,1)S(1)} %get-tuple-element.67), channel_id=1, source_target_pairs={{0,3},{1,2},{2,1},{3,0},{4,7},{5,6},{6,5},{7,4},{8,11},{9,10},{10,... | collective-permute-start | bytes 55304 | tf_op jit(solution)/shard_map/ppermute | solution.py:155
  36.1 0.4 collective-permute-start.19
  36.5 2.4 %collective-permute-start.18 = (bf16[72,128]{1,0:T(8,128)(2,1)S(1)}, bf16[72,128]{1,0:T(8,128)(2,1)S(1)}, u32[]{:S(2)}, u32[]{:S(2)}) collective-permute-start(bf16[72,128]{1,0:T(8,128)(2,1)S(1)} %get-tuple-element.65), channel_id=1, source_target_pairs={{0,1},{1,0},{2,3},{3,2},{4,5},{5,4},{6,7},{7,6},{8,9},{9,8},{10,11... | collective-permute-start | bytes 55304 | tf_op jit(solution)/shard_map/ppermute | solution.py:155
  38.9 0.0 collective-permute-done.13
  38.9 1.1 %collective-permute-done.20 = bf16[72,128]{1,0:T(8,128)(2,1)S(1)} collective-permute-done((bf16[72,128]{1,0:T(8,128)(2,1)S(1)}, bf16[72,128]{1,0:T(8,128)(2,1)S(1)}, u32[]{:S(2)}, u32[]{:S(2)}) %collective-permute-start.20) | collective-permute-done | bytes 18464 | tf_op jit(solution)/shard_map/ppermute | solution.py:155
  40.1 0.9 %collective-permute-done.19 = bf16[72,128]{1,0:T(8,128)(2,1)S(1)} collective-permute-done((bf16[72,128]{1,0:T(8,128)(2,1)S(1)}, bf16[72,128]{1,0:T(8,128)(2,1)S(1)}, u32[]{:S(2)}, u32[]{:S(2)}) %collective-permute-start.19) | collective-permute-done | bytes 18464 | tf_op jit(solution)/shard_map/ppermute | solution.py:155
  41.0 0.0 collective-permute-done.18
  41.0 0.1 collective-permute-start.21
  41.1 0.7 %pad_maximum_fusion.3 = bf16[2,256,256]{2,1,0:T(8,128)(2,1)} fusion(bf16[1,256,256]{2,1,0:T(8,128)(2,1)S(1)} %get-tuple-element.69, bf16[1,256,256]{2,1,0:T(8,128)(2,1)S(1)} %get-tuple-element.68), kind=kLoop, calls=%fused_computation.3 | loop fusion | flops 131072 | bytes 524288 | tf_op jit(solution)/shard_map/stack | solution.py:475
  41.8 0.5 %collective-permute-done.21.refs_1_ = f32[72,128]{1,0:T(8,128)S(1)} collective-permute-done((f32[72,128]{1,0:T(8,128)S(1)}, f32[72,128]{1,0:T(8,128)S(1)}, u32[]{:S(2)}, u32[]{:S(2)}) %collective-permute-start.21) | collective-permute-done | bytes 36896 | tf_op jit(solution)/shard_map/ppermute | solution.py:155
  42.3 0.6 %total.1 = f32[144,128]{1,0:T(8,128)} custom-call(f32[72,128]{1,0:T(8,128)S(1)} %convert_add_fusion.refs_0_, f32[72,128]{1,0:T(8,128)S(1)} %collective-permute-done.21.refs_1_), custom_call_target="tpu_custom_call" | custom-call | tf_op jit(solution)/shard_map/total/pallas_call | solution.py:387
  (17 shorter events, 0.3 us)
Async XLA Ops:
  0.6 17.8 %copy-start = (f32[360,4,256]{2,1,0:T(4,128)S(1)}, f32[360,4,256]{2,1,0:T(4,128)}, u32[]{:S(2)}) copy-start(f32[360,4,256]{2,1,0:T(4,128)} %param.7) | copy-start | bytes 4423684
  0.6 1.6 %collective-permute-start = (bf16[2,18432]{1,0:T(2,128)(2,1)}, bf16[2,18432]{1,0:T(2,128)(2,1)S(1)}, u32[]{:S(2)}, u32[]{:S(2)}) collective-permute-start(bf16[2,18432]{1,0:T(2,128)(2,1)} %param.8), channel_id=1, source_target_pairs={{0,4},{1,5},{2,6},{3,7},{4,0},{5,1},{6,2},{7,3},{8,12},{9,13},{10,... | collective-permute-start | bytes 221192 | tf_op jit(solution)/shard_map/ppermute | solution.py:155
  2.2 15.6 %copy-start.1 = (bf16[1,64,8,256]{3,2,1,0:T(8,128)(2,1)S(1)}, bf16[1,64,8,256]{3,2,1,0:T(8,128)(2,1)}, u32[]{:S(2)}) copy-start(bf16[1,64,8,256]{3,2,1,0:T(8,128)(2,1)} %param.5) | copy-start | bytes 786436
  2.3 16.2 %copy-start.2 = (bf16[1,64,8,256]{3,2,1,0:T(8,128)(2,1)S(1)}, bf16[1,64,8,256]{3,2,1,0:T(8,128)(2,1)}, u32[]{:S(2)}) copy-start(bf16[1,64,8,256]{3,2,1,0:T(8,128)(2,1)} %param.9) | copy-start | bytes 786436
  2.3 3.2 %collective-permute-start.1 = (bf16[2,18432]{1,0:T(2,128)(2,1)S(1)}, bf16[2,18432]{1,0:T(2,128)(2,1)S(1)}, u32[]{:S(2)}, u32[]{:S(2)}) collective-permute-start(bf16[2,18432]{1,0:T(2,128)(2,1)S(1)} %collective-permute-done), channel_id=1, source_target_pairs={{0,4},{1,5},{2,6},{3,7},{4,0},{5,1},{6,2},{7,3},{8,12},{9,13},{10,... | collective-permute-start | bytes 221192 | tf_op jit(solution)/shard_map/ppermute | solution.py:155
  2.7 15.2 %collective-permute-start.9 = (bf16[2,256,256]{2,1,0:T(8,128)(2,1)S(1)}, bf16[2,256,256]{2,1,0:T(8,128)(2,1)S(1)}, u32[]{:S(2)}, u32[]{:S(2)}) collective-permute-start(bf16[2,256,256]{2,1,0:T(8,128)(2,1)S(1)} %give.1), channel_id=1, source_target_pairs={{0,8},{1,9},{2,10},{3,11},{4,12},{5,13},{6,14},{7,15},{8,0},{9,1},... | collective-permute-start | bytes 786440 | tf_op jit(solution)/shard_map/ppermute | solution.py:155
  5.6 5.8 %collective-permute-start.2 = (bf16[2,72,128]{2,1,0:T(8,128)(2,1)S(1)}, bf16[2,72,128]{2,1,0:T(8,128)(2,1)S(1)}, u32[]{:S(2)}, u32[]{:S(2)}) collective-permute-start(bf16[2,72,128]{2,1,0:T(8,128)(2,1)S(1)} %fusion.refs_0_), channel_id=1, source_target_pairs={{0,3},{1,2},{2,1},{3,0},{4,7},{5,6},{6,5},{7,4},{8,11},{9,10},{10,... | collective-permute-start | bytes 110600 | tf_op jit(solution)/shard_map/ppermute | solution.py:155
  9.2 4.9 %collective-permute-start.3 = (bf16[2,72,128]{2,1,0:T(8,128)(2,1)S(1)}, bf16[2,72,128]{2,1,0:T(8,128)(2,1)S(1)}, u32[]{:S(2)}, u32[]{:S(2)}) collective-permute-start(bf16[2,72,128]{2,1,0:T(8,128)(2,1)S(1)} %fusion.refs_0_), channel_id=1, source_target_pairs={{0,2},{1,3},{2,0},{3,1},{4,6},{5,7},{6,4},{7,5},{8,10},{9,11},{10,... | collective-permute-start | bytes 110600 | tf_op jit(solution)/shard_map/ppermute | solution.py:155
  9.2 4.9 %collective-permute-start.4 = (bf16[2,72,128]{2,1,0:T(8,128)(2,1)S(1)}, bf16[2,72,128]{2,1,0:T(8,128)(2,1)S(1)}, u32[]{:S(2)}, u32[]{:S(2)}) collective-permute-start(bf16[2,72,128]{2,1,0:T(8,128)(2,1)S(1)} %fusion.refs_0_), channel_id=1, source_target_pairs={{0,1},{1,0},{2,3},{3,2},{4,5},{5,4},{6,7},{7,6},{8,9},{9,8},{10,11... | collective-permute-start | bytes 110600 | tf_op jit(solution)/shard_map/ppermute | solution.py:155
  14.2 6.8 %collective-permute-start.5 = (bf16[2,256,128]{2,1,0:T(8,128)(2,1)S(1)}, bf16[2,256,128]{2,1,0:T(8,128)(2,1)S(1)}, u32[]{:S(2)}, u32[]{:S(2)}) collective-permute-start(bf16[2,256,128]{2,1,0:T(8,128)(2,1)S(1)} %line.1), channel_id=1, source_target_pairs={{0,24},{1,25},{2,26},{3,27},{4,28},{5,29},{6,30},{7,31},{8,16},{9,... | collective-permute-start | bytes 393224 | tf_op jit(solution)/shard_map/ppermute | solution.py:155
  16.2 5.9 %collective-permute-start.6 = (bf16[2,256,128]{2,1,0:T(8,128)(2,1)S(1)}, bf16[2,256,128]{2,1,0:T(8,128)(2,1)S(1)}, u32[]{:S(2)}, u32[]{:S(2)}) collective-permute-start(bf16[2,256,128]{2,1,0:T(8,128)(2,1)S(1)} %line.1), channel_id=1, source_target_pairs={{0,16},{1,17},{2,18},{3,19},{4,20},{5,21},{6,22},{7,23},{8,24},{9,... | collective-permute-start | bytes 393224 | tf_op jit(solution)/shard_map/ppermute | solution.py:155
  16.7 5.7 %collective-permute-start.7 = (bf16[2,256,128]{2,1,0:T(8,128)(2,1)S(1)}, bf16[2,256,128]{2,1,0:T(8,128)(2,1)S(1)}, u32[]{:S(2)}, u32[]{:S(2)}) collective-permute-start(bf16[2,256,128]{2,1,0:T(8,128)(2,1)S(1)} %line.1), channel_id=1, source_target_pairs={{0,8},{1,9},{2,10},{3,11},{4,12},{5,13},{6,14},{7,15},{8,0},{9,1},... | collective-permute-start | bytes 393224 | tf_op jit(solution)/shard_map/ppermute | solution.py:155
  17.8 4.6 %collective-permute-start.8 = (bf16[256,256]{1,0:T(8,128)(2,1)S(1)}, bf16[256,256]{1,0:T(8,128)(2,1)S(1)}, u32[]{:S(2)}, u32[]{:S(2)}) collective-permute-start(bf16[256,256]{1,0:T(8,128)(2,1)S(1)} %dynamic-slice_bitcast_fusion.1.refs_0_), channel_id=1, source_target_pairs={{0,4},{1,5},{2,6},{3,7},{4,0},{5,1},{6,2},{7,3},{8,12},{9,13},{10,... | collective-permute-start | bytes 393224 | tf_op jit(solution)/shard_map/ppermute | solution.py:155
  17.9 4.5 %collective-permute-start.10 = (bf16[256,256]{1,0:T(8,128)(2,1)S(1)}, bf16[256,256]{1,0:T(8,128)(2,1)S(1)}, u32[]{:S(2)}, u32[]{:S(2)}) collective-permute-start(bf16[256,256]{1,0:T(8,128)(2,1)S(1)} %slice_bitcast_fusion), channel_id=1, source_target_pairs={{0,4},{1,5},{2,6},{3,7},{4,0},{5,1},{6,2},{7,3},{8,12},{9,13},{10,... | collective-permute-start | bytes 393224 | tf_op jit(solution)/shard_map/ppermute | solution.py:155
  22.5 1.6 %collective-permute-start.11 = (bf16[4,256,128]{2,1,0:T(8,128)(2,1)S(1)}, bf16[4,256,128]{2,1,0:T(8,128)(2,1)S(1)}, u32[]{:S(2)}, u32[]{:S(2)}) collective-permute-start(bf16[4,256,128]{2,1,0:T(8,128)(2,1)S(1)} %pad_maximum_fusion.1.refs_4_), channel_id=1, source_target_pairs={{0,4},{1,5},{2,6},{3,7},{4,0},{5,1},{6,2},{7,3},{8,12},{9,13},{10,... | collective-permute-start | bytes 786440 | tf_op jit(solution)/shard_map/ppermute | solution.py:155
  22.7 1.9 %collective-permute-start.12 = (bf16[4,256,128]{2,1,0:T(8,128)(2,1)S(1)}, bf16[4,256,128]{2,1,0:T(8,128)(2,1)S(1)}, u32[]{:S(2)}, u32[]{:S(2)}) collective-permute-start(bf16[4,256,128]{2,1,0:T(8,128)(2,1)S(1)} %pad_maximum_fusion.2.refs_4_), channel_id=1, source_target_pairs={{0,4},{1,5},{2,6},{3,7},{4,0},{5,1},{6,2},{7,3},{8,12},{9,13},{10,... | collective-permute-start | bytes 786440 | tf_op jit(solution)/shard_map/ppermute | solution.py:155
  25.4 1.4 %collective-permute-start.14 = (bf16[512,128]{1,0:T(8,128)(2,1)S(1)}, bf16[512,128]{1,0:T(8,128)(2,1)S(1)}, u32[]{:S(2)}, u32[]{:S(2)}) collective-permute-start(bf16[512,128]{1,0:T(8,128)(2,1)S(1)} %get-tuple-element.59), channel_id=1, source_target_pairs={{0,4},{1,5},{2,6},{3,7},{4,0},{5,1},{6,2},{7,3},{8,12},{9,13},{10,... | collective-permute-start | bytes 393224 | tf_op jit(solution)/shard_map/ppermute | solution.py:155
  25.6 13.3 %collective-permute-start.13 = (bf16[256,256]{1,0:T(8,128)(2,1)S(1)}, bf16[256,256]{1,0:T(8,128)(2,1)S(1)}, u32[]{:S(2)}, u32[]{:S(2)}) collective-permute-start(bf16[256,256]{1,0:T(8,128)(2,1)S(1)} %get-tuple-element.56), channel_id=1, source_target_pairs={{0,8},{1,9},{2,10},{3,11},{4,12},{5,13},{6,14},{7,15},{8,0},{9,1},... | collective-permute-start | bytes 393224 | tf_op jit(solution)/shard_map/ppermute | solution.py:155
  27.4 5.6 %collective-permute-start.15 = (bf16[256,128]{1,0:T(8,128)(2,1)S(1)}, bf16[256,128]{1,0:T(8,128)(2,1)S(1)}, u32[]{:S(2)}, u32[]{:S(2)}) collective-permute-start(bf16[256,128]{1,0:T(8,128)(2,1)S(1)} %get-tuple-element.61), channel_id=1, source_target_pairs={{0,24},{1,25},{2,26},{3,27},{4,28},{5,29},{6,30},{7,31},{8,16},{9,... | collective-permute-start | bytes 196616 | tf_op jit(solution)/shard_map/ppermute | solution.py:155
  29.6 4.3 %collective-permute-start.16 = (bf16[256,128]{1,0:T(8,128)(2,1)S(1)}, bf16[256,128]{1,0:T(8,128)(2,1)S(1)}, u32[]{:S(2)}, u32[]{:S(2)}) collective-permute-start(bf16[256,128]{1,0:T(8,128)(2,1)S(1)} %get-tuple-element.62), channel_id=1, source_target_pairs={{0,16},{1,17},{2,18},{3,19},{4,20},{5,21},{6,22},{7,23},{8,24},{9,... | collective-permute-start | bytes 196616 | tf_op jit(solution)/shard_map/ppermute | solution.py:155
  30.1 4.3 %collective-permute-start.17 = (bf16[256,128]{1,0:T(8,128)(2,1)S(1)}, bf16[256,128]{1,0:T(8,128)(2,1)S(1)}, u32[]{:S(2)}, u32[]{:S(2)}) collective-permute-start(bf16[256,128]{1,0:T(8,128)(2,1)S(1)} %get-tuple-element.63), channel_id=1, source_target_pairs={{0,8},{1,9},{2,10},{3,11},{4,12},{5,13},{6,14},{7,15},{8,0},{9,1},... | collective-permute-start | bytes 196616 | tf_op jit(solution)/shard_map/ppermute | solution.py:155
  34.5 5.6 %collective-permute-start.20 = (bf16[72,128]{1,0:T(8,128)(2,1)S(1)}, bf16[72,128]{1,0:T(8,128)(2,1)S(1)}, u32[]{:S(2)}, u32[]{:S(2)}) collective-permute-start(bf16[72,128]{1,0:T(8,128)(2,1)S(1)} %get-tuple-element.67), channel_id=1, source_target_pairs={{0,3},{1,2},{2,1},{3,0},{4,7},{5,6},{6,5},{7,4},{8,11},{9,10},{10,... | collective-permute-start | bytes 55304 | tf_op jit(solution)/shard_map/ppermute | solution.py:155
  36.1 4.9 %collective-permute-start.19 = (bf16[72,128]{1,0:T(8,128)(2,1)S(1)}, bf16[72,128]{1,0:T(8,128)(2,1)S(1)}, u32[]{:S(2)}, u32[]{:S(2)}) collective-permute-start(bf16[72,128]{1,0:T(8,128)(2,1)S(1)} %get-tuple-element.66), channel_id=1, source_target_pairs={{0,2},{1,3},{2,0},{3,1},{4,6},{5,7},{6,4},{7,5},{8,10},{9,11},{10,... | collective-permute-start | bytes 55304 | tf_op jit(solution)/shard_map/ppermute | solution.py:155
  36.5 4.5 %collective-permute-start.18 = (bf16[72,128]{1,0:T(8,128)(2,1)S(1)}, bf16[72,128]{1,0:T(8,128)(2,1)S(1)}, u32[]{:S(2)}, u32[]{:S(2)}) collective-permute-start(bf16[72,128]{1,0:T(8,128)(2,1)S(1)} %get-tuple-element.65), channel_id=1, source_target_pairs={{0,1},{1,0},{2,3},{3,2},{4,5},{5,4},{6,7},{7,6},{8,9},{9,8},{10,11... | collective-permute-start | bytes 55304 | tf_op jit(solution)/shard_map/ppermute | solution.py:155
  41.0 1.3 %collective-permute-start.21 = (f32[72,128]{1,0:T(8,128)S(1)}, f32[72,128]{1,0:T(8,128)S(1)}, u32[]{:S(2)}, u32[]{:S(2)}) collective-permute-start(f32[72,128]{1,0:T(8,128)S(1)} %convert_add_fusion.refs_0_), channel_id=1, source_target_pairs={{0,4},{1,5},{2,6},{3,7},{4,0},{5,1},{6,2},{7,3},{8,12},{9,13},{10,... | collective-permute-start | bytes 110600 | tf_op jit(solution)/shard_map/ppermute | solution.py:155

commit v5 on v3

--- a/solution.py
+++ b/solution.py
@@ -157,8 +157,8 @@
     )
 
 
-Z_ORDER = (3, 2, 1)
-PLANE_ORDER = ((1, 1), (1, 0), (0, 1))
+FIRST_ROUND = ((1, 2), (0, 2), (1, 0))
+SECOND_ROUND = ((1, 1), (0, 1), (1, 0))
 
 
 def place():
@@ -193,33 +193,34 @@
 
 class Layout:
     def __init__(self, width, shard_rows):
-        self.pieces = used_rows(width, shard_rows)
-        self.start, self.count, self.base, self.first, self.stop = {}, {}, {}, {}, {}
-        for cx, cy, cc, cz, first, count, row in self.pieces:
-            self.start[cx, cy] = min(self.start.get((cx, cy), 3 * width), row)
-            self.count[cx, cy] = self.count.get((cx, cy), 0) + count
-        for cx, cy, cc, cz, first, count, row in self.pieces:
-            self.base[cx, cy, cz, cc] = row - self.start[cx, cy] - first
-            self.first[cx, cy, cz, cc] = first
-            self.stop[cx, cy, cz, cc] = first + count
-        self.low = {
-            key[:3]: stop for key, stop in self.stop.items() if key[3] == 1
-        }
+        self.pieces = {(x, part): [] for x in range(2) for part in range(2)}
+        self.base, self.first, self.stop = {}, {}, {}
+        held = dict.fromkeys(self.pieces, 0)
+        for cx, cy, cc, cz, first, count, row in used_rows(width, shard_rows):
+            group, key = (cx, cz % 2), (cx, cy, cz, cc)
+            assert key not in self.base
+            self.pieces[group].append((held[group], count, row))
+            self.base[key] = held[group] - first
+            self.first[key], self.stop[key] = first, first + count
+            held[group] += count
+        self.rows = max(held.values())
+        self.low = {key[:3]: stop for key, stop in self.stop.items() if key[3] == 1}
         for key, first in self.first.items():
             assert key[3] == 1 or self.low.get(key[:3], 0) <= first
-        self.column_rows = max(self.count.values())
-        assert all(start + self.column_rows <= 3 * width for start in self.start.values())
-        assert len(self.base) == len(self.pieces)
-
-
-def line_kernel(layout, own_ref, far0_ref, far1_ref, far2_ref, out_ref, total):
+
+
+def copy_kernel(layout, value_ref, out_ref):
+    out_ref[...] = value_ref[...]
+
+
+def group_kernel(layout, own_ref, far0_ref, far1_ref, far2_ref, out_ref, total):
     x, y, c, z = place()
     rows = own_ref.shape[1]
     total[...] = jnp.zeros_like(total)
     row = lax.broadcasted_iota(jnp.int32, own_ref.shape[1:], 0)
-    for dz, ref in zip((0, *Z_ORDER), (own_ref, far0_ref, far1_ref, far2_ref)):
+    for (dy, dz), ref in zip(((0, 0), *FIRST_ROUND), (own_ref, far0_ref, far1_ref, far2_ref)):
         for core in range(2):
-            here = (x, y, z ^ dz, core)
+            here = (x, y ^ dy, z ^ dz, core)
             first, stop = chosen(layout.first, here, 0), chosen(layout.stop, here, 0)
             base = pl.multiple_of(rows + chosen(layout.base, here, -rows), 8)
             used = (row >= first) & (row < stop)
@@ -229,23 +230,28 @@
     out_ref[...] = total[:, rows : rows + out_ref.shape[1], :].astype(out_ref.dtype)
 
 
-def slot(dx, dy):
+def slot(dx, dz):
     found = 0
-    for number, (to_x, to_y) in enumerate(PLANE_ORDER):
-        found = jnp.where((dx == to_x) & (dy == to_y), number + 1, found)
+    for number, (to_x, to_z) in enumerate(SECOND_ROUND):
+        found = jnp.where((dx == to_x) & (dz == to_z), number + 1, found)
     return found
 
 
-def matrix(layout, own_ref, near_ref):
-    x, y, c, z = place()
-    halves = []
-    for ref in (own_ref, near_ref):
-        parts = [
-            ref[slot(cx ^ x, cy ^ y)][: layout.count[cx, cy]]
-            for cx, cy in sorted(layout.start, key=layout.start.get)
-        ]
-        halves.append(jnp.concatenate(parts, axis=0))
-    own, near = halves
+def order_kernel(layout, own_ref, far0_ref, far1_ref, far2_ref, a_ref, b_ref, held, total):
+    x, y, c, z = place()
+    for number, ref in enumerate((own_ref, far0_ref, far1_ref, far2_ref)):
+        held[number] = ref[...].astype(jnp.float32)
+    for (cx, part), pieces in layout.pieces.items():
+        number = slot(cx ^ x, part ^ (z % 2))
+        for start, count, row in pieces:
+            total[:, row : row + count, :] = held[number, :, start : start + count, :]
+    a_ref[...] = total[0].astype(a_ref.dtype)
+    b_ref[...] = total[1].astype(b_ref.dtype)
+
+
+def matrix(own_ref, near_ref):
+    c = place()[2]
+    own, near = own_ref[...], near_ref[...]
     return jnp.concatenate([jnp.where(c == 0, own, near), jnp.where(c == 0, near, own)], axis=1)
 
 
@@ -255,7 +261,7 @@
 
 def first_kernel(
     layout, mine_ref, other_ref, near0_ref, near1_ref, own_w, near_w, film_ref,
-    field_ref, pre_ref, hidden_ref,
+    field_ref, slope_ref, hidden_ref,
 ):
     x, y, c, z = place()
     half, width = mine_ref.shape
@@ -272,51 +278,51 @@
     above = jnp.concatenate([field_ref[c], field_ref[c + 2]], axis=0)
     mid = jnp.concatenate([lo, hi], axis=0)
     below = jnp.concatenate([field_ref[c + 2], field_ref[c + 4]], axis=0)
-    weight = matrix(layout, own_w, near_w)
+    weight = matrix(own_w, near_w)
     conv = dot(above, weight[:width]) + dot(mid, weight[width : 2 * width])
     conv = conv + dot(below, weight[2 * width :])
     pre = conv * (1.0 + film_ref[0:1, :]) + film_ref[1:2, :]
-    pre_ref[...] = pre
-    hidden_ref[...] = (mid.astype(jnp.float32) + pre * jax.nn.sigmoid(pre)).astype(hidden_ref.dtype)
+    sig = jax.nn.sigmoid(pre)
+    lift = pre * sig
+    hidden_ref[...] = (mid.astype(jnp.float32) + lift).astype(hidden_ref.dtype)
+    slope_ref[...] = (1.0 + film_ref[0:1, :]) * (sig + lift * (1.0 - sig))
 
 
 def second_kernel(
-    layout, pre_ref, hidden_ref, mine_ct, other_ref, own_w, near_w, film_ref,
+    layout, slope_ref, hidden_ref, mine_ct, other_ref, own_w, near_w, film_ref,
     out_keep, out_send, grad_keep, grad_send,
 ):
     x, y, c, z = place()
     half, width = mine_ct.shape
     f32, bf16 = jnp.float32, jnp.bfloat16
     lane = width // 2
-    mult_a = 1.0 + film_ref[0:1, :]
     mult_b = 1.0 + film_ref[2:3, :]
-    weight = matrix(layout, own_w, near_w)
+    weight = matrix(own_w, near_w)
     up, centre, down = weight[:width], weight[width : 2 * width], weight[2 * width :]
     hidden = hidden_ref[...]
     across = jnp.concatenate([dot(hidden[half:], down), dot(hidden[:half], up)], axis=0)
     pre_b = (dot(hidden, centre) + across) * mult_b + film_ref[3:4, :]
     sig_b = jax.nn.sigmoid(pre_b)
-    result = (hidden.astype(f32) + pre_b * sig_b).astype(bf16)
+    lift_b = pre_b * sig_b
+    result = (hidden.astype(f32) + lift_b).astype(bf16)
     out_keep[...] = jnp.where(y == 0, result[:half], result[half:])
     out_send[...] = jnp.where(y == 0, result[half:], result[:half])
     mine, other = mine_ct[...], other_ref[1]
     lo, hi = jnp.where(y == 0, mine, other), jnp.where(y == 0, other, mine)
     upstream = jnp.concatenate([lo, hi], axis=0).astype(f32)
-    grad_b = (upstream * mult_b * sig_b * (1.0 + pre_b * (1.0 - sig_b))).astype(bf16)
+    grad_b = (upstream * (mult_b * (sig_b + lift_b * (1.0 - sig_b)))).astype(bf16)
     turned = ((1,), (1,))
     back = jnp.concatenate(
         [dot(grad_b[half:], up, turned), dot(grad_b[:half], down, turned)], axis=0
     )
     back = upstream + dot(grad_b, centre, turned) + back
-    pre_a = pre_ref[...]
-    sig_a = jax.nn.sigmoid(pre_a)
-    grad_a = (back * mult_a * sig_a * (1.0 + pre_a * (1.0 - sig_a))).astype(bf16)
+    grad_a = (back * slope_ref[...]).astype(bf16)
     grad_keep[...] = jnp.where(c == 0, grad_a[:, :lane], grad_a[:, lane:])
     grad_send[...] = jnp.where(c == 0, grad_a[:, lane:], grad_a[:, :lane])
 
 
 def term_kernel(
-    layout, scale, field_ref, keep_ref, near_ref, own_ref, far0_ref, far1_ref, far2_ref, total
+    layout, scale, field_ref, keep_ref, near_ref, own_ref, far0_ref, far1_ref, far2_ref, total, groups
 ):
     x, y, c, z = place()
     half, width = field_ref.shape[1:]
@@ -324,14 +330,19 @@
     even, odd = jnp.where(c == 0, keep, near), jnp.where(c == 0, near, keep)
     grad = jnp.concatenate([even[:half], odd[:half], even[half:], odd[half:]], axis=0)
     field = jnp.concatenate([field_ref[tile] for tile in range(1, 5)], axis=0)
-    over = ((0,), (0,))
-    total[:width, :] = dot(field[: 3 * half], grad[half:], over) * scale
-    total[width : 2 * width, :] = dot(field, grad, over) * scale
-    total[2 * width :, :] = dot(field[half:], grad[: 3 * half], over) * scale
-    rows = own_ref.shape[0]
-    for (dx, dy), ref in zip(((0, 0), *PLANE_ORDER), (own_ref, far0_ref, far1_ref, far2_ref)):
-        start = pl.multiple_of(chosen(layout.start, (x ^ dx, y ^ dy), 0), 8)
-        ref[...] = total[pl.ds(start, rows), :].astype(ref.dtype)
+    none = jnp.zeros_like(grad[:half])
+    below = jnp.concatenate([grad[half:], none], axis=0)
+    above = jnp.concatenate([none, grad[: 3 * half]], axis=0)
+    sums = dot(field, jnp.concatenate([below, grad, above], axis=1), ((0,), (0,))) * scale
+    lane = width // 2
+    for number in range(3):
+        total[number * width : (number + 1) * width, :] = sums[:, number * lane : (number + 1) * lane]
+    for number, pieces in enumerate(layout.pieces.values()):
+        for start, count, row in pieces:
+            groups[number, start : start + count, :] = total[row : row + count, :]
+    for (dx, dz), ref in zip(((0, 0), *SECOND_ROUND), (own_ref, far0_ref, far1_ref, far2_ref)):
+        number = 2 * (x ^ dx) + (z ^ dz) % 2
+        ref[...] = groups[number].astype(ref.dtype)
 
 
 def chip_kernel(layout, own_ref, far0_ref, far1_ref, far2_ref, out0, out1, out2, out3, total):
@@ -342,18 +353,19 @@
     value = own_ref[...]
     for ref in (far0_ref, far1_ref, far2_ref):
         value = value + ref[...].astype(f32)
-    row = lax.broadcasted_iota(jnp.int32, value.shape, 0)
     edge = jnp.zeros((piece_rows, lane), f32)
     total[0:piece_rows, :] = edge
-    held = row < chosen(layout.count, (x, y), 0)
-    total[piece_rows : piece_rows + rows, :] = jnp.where(held, value, 0.0)
+    total[piece_rows : piece_rows + rows, :] = value
     total[piece_rows + rows :, :] = edge
-    for dz, ref in zip((0, *Z_ORDER), (out0, out1, out2, out3)):
-        ends = []
+    row = lax.broadcasted_iota(jnp.int32, out0.shape, 0)
+    for (dy, dz), ref in zip(((0, 0), *FIRST_ROUND), (out0, out1, out2, out3)):
+        piece = edge
         for core in range(2):
-            base = piece_rows + chosen(layout.base, (x, y, z ^ dz, core), -piece_rows)
-            ends.append(total[pl.ds(pl.multiple_of(base, 8), piece_rows), :])
-        ref[...] = (ends[0] + ends[1]).astype(ref.dtype)
+            here = (x, y ^ dy, z ^ dz, core)
+            base = piece_rows + chosen(layout.base, here, -piece_rows)
+            used = (row >= chosen(layout.first, here, 0)) & (row < chosen(layout.stop, here, 0))
+            piece = jnp.where(used, total[pl.ds(pl.multiple_of(base, 8), piece_rows), :], piece)
+        ref[...] = piece.astype(ref.dtype)
 
 
 def last_kernel(layout, own_ref, other_ref, out_ref):
@@ -377,7 +389,7 @@
     bf16, f32 = jnp.bfloat16, jnp.float32
     shape = jax.ShapeDtypeStruct
 
-    def call(name, body, out_shape, scratch, *operands):
+    def call(name, body, out_shape, scratch, *operands, cost=0):
         vmem = pl.BlockSpec(memory_space=pltpu.VMEM)
         several = isinstance(out_shape, tuple)
         return pl.pallas_call(
@@ -387,42 +399,54 @@
             out_specs=(vmem,) * len(out_shape) if several else vmem,
             scratch_shapes=scratch,
             compiler_params=pltpu.CompilerParams(vmem_limit_bytes=16 * 1024 * 1024),
+            cost_estimate=pl.CostEstimate(flops=cost * 10**9, bytes_accessed=0, transcendentals=0) if cost else None,
             name=name,
         )(*operands)
 
     shard = flat_weights.reshape(2, shard_rows, width)
     left, right = shard[:, :, :lane], shard[:, :, lane:]
-    near = moved(jnp.where(c == 0, right, left), dc=1)
+    near = moved(flat_weights, dc=1).reshape(shard.shape)
+    near = jnp.where(c == 0, near[:, :, :lane], near[:, :, lane:])
     row = lax.broadcasted_iota(jnp.int32, near.shape, 1)
     from_one = row < chosen(layout.low, (x, y, z), 0)
     piece = jnp.where(from_one == (c == 1), jnp.where(c == 0, left, right), near)
 
     halves_x, halves_ct = (array.reshape(2, half, width) for array in (inputs, cotangent))
     pick = lambda halves, number: lax.dynamic_index_in_dim(halves, number, 0, keepdims=False)
-    other = moved(jnp.stack([pick(halves_x, 1 - y), pick(halves_ct, 1 - y)]), dy=1)
-    line = [piece, *(moved(piece, dz=dz) for dz in Z_ORDER)]
+    piece, halves_x, halves_ct = lax.optimization_barrier((piece, halves_x, halves_ct))
+    give = jnp.stack([pick(halves_x, 1 - y), pick(halves_ct, 1 - y)])
+    give = call("give", copy_kernel, shape(give.shape, bf16), [], give, cost=3)
+    other = moved(give, dy=1)
+    line = [piece, *(moved(piece, dy=dy, dz=dz) for dy, dz in FIRST_ROUND)]
     *line, halves_x, halves_ct, film = lax.optimization_barrier(
         (*line, halves_x, halves_ct, film)
     )
     mine_x, mine_ct = pick(halves_x, y), pick(halves_ct, y)
     film_row = lax.dynamic_index_in_dim(film, lead_ids[0], 0, keepdims=False)
     near_x0 = moved(mine_x, dc=1)
-    line = call(
-        "line",
-        line_kernel,
-        shape((2, layout.column_rows, lane), bf16),
-        [pltpu.VMEM((2, layout.column_rows + 2 * shard_rows, lane), f32)],
+    group = call(
+        "group",
+        group_kernel,
+        shape((2, layout.rows, lane), bf16),
+        [pltpu.VMEM((2, layout.rows + 2 * shard_rows, lane), f32)],
         *line,
+        cost=6,
     )
     near_x1 = moved(other[0], dc=1)
-    plane = [line, *(moved(line, dx=dx, dy=dy) for dx, dy in PLANE_ORDER)]
-    *plane, near_x0, near_x1, mine_x, mine_ct, film_row = lax.optimization_barrier(
-        (*plane, near_x0, near_x1, mine_x, mine_ct, film_row)
-    )
-    own_a, own_b = (jnp.stack([column[k] for column in plane]) for k in range(2))
+    groups = [group, *(moved(group, dx=dx, dz=dz) for dx, dz in SECOND_ROUND)]
+    *groups, near_x0, near_x1, mine_x, mine_ct, film_row = lax.optimization_barrier(
+        (*groups, near_x0, near_x1, mine_x, mine_ct, film_row)
+    )
+    own_a, own_b = call(
+        "order",
+        order_kernel,
+        (shape((3 * width, lane), bf16),) * 2,
+        [pltpu.VMEM((4, 2, layout.rows, lane), f32), pltpu.VMEM((2, 3 * width, lane), f32)],
+        *groups,
+    )
     near_a, near_b = moved(own_a, dc=1), moved(own_b, dc=1)
 
-    field, pre_a, hidden = call(
+    field, slope_a, hidden = call(
         "block_one",
         first_kernel,
         (shape((6, half, width), bf16), shape((2 * half, width), f32), shape((2 * half, width), bf16)),
@@ -434,29 +458,29 @@
         second_kernel,
         (shape((half, width), bf16),) * 2 + (shape((2 * half, lane), bf16),) * 2,
         [],
-        *(pre_a, hidden, mine_ct, other, own_b, near_b, film_row),
+        *(slope_a, hidden, mine_ct, other, own_b, near_b, film_row),
     )
 
     scale = 1.0 / math.sqrt(lax.axis_size(AXES) * rows * columns)
-    column = call(
+    terms = call(
         "terms",
         lambda layout, *refs: term_kernel(layout, scale, *refs),
-        (shape((layout.column_rows, lane), f32),) + (shape((layout.column_rows, lane), bf16),) * 3,
-        [pltpu.VMEM((3 * width, lane), f32)],
+        (shape((layout.rows, lane), f32),) + (shape((layout.rows, lane), bf16),) * 3,
+        [pltpu.VMEM((3 * width, lane), f32), pltpu.VMEM((4, layout.rows, lane), f32)],
         *(field, grad_keep, moved(grad_send, dc=1)),
     )
     other_out = moved(out_send, dy=1)
-    column = [column[0], *(moved(term, dx=dx, dy=dy) for term, (dx, dy) in zip(column[1:], PLANE_ORDER))]
+    terms = [terms[0], *(moved(term, dx=dx, dz=dz) for term, (dx, dz) in zip(terms[1:], SECOND_ROUND))]
     chip = call(
         "chips",
         chip_kernel,
         (shape((shard_rows, lane), f32),) + (shape((shard_rows, lane), bf16),) * 3,
-        [pltpu.VMEM((layout.column_rows + 2 * shard_rows, lane), f32)],
-        *column,
+        [pltpu.VMEM((layout.rows + 2 * shard_rows, lane), f32)],
+        *terms,
     )
     lane_sum = chip[0]
-    for term, dz in reversed(list(zip(chip[1:], Z_ORDER))):
-        lane_sum = lane_sum + moved(term, dz=dz).astype(f32)
+    for term, (dy, dz) in zip(chip[1:], FIRST_ROUND):
+        lane_sum = lane_sum + moved(term, dy=dy, dz=dz).astype(f32)
 
     first = jnp.where(y == 0, out_keep, other_out)
     second = jnp.where(y == 0, other_out, out_keep)

time: 43.5 us -> 41.4 us (0.952)
  waiting for transfers between devices: 14.7 us -> 13.3 us
  starting transfers between devices: 21.3 us -> 20.8 us
    ppermute x21, waiting for transfers between devices: 14.7 us -> 13.3 us  [moved(): lax.ppermute(value, AXES, pairs(lambda x, y, c, z: (x ^ dx, y ^ dy, c ^ d...]
    ppermute x21, starting transfers between devices: 21.3 us -> 20.8 us  [moved(): lax.ppermute(value, AXES, pairs(lambda x, y, c, z: (x ^ dx, y ^ dy, c ^ d...]
    unnamed x7 -> x8, local copies, waits for them, and re-layouts: 1.05 us -> 0.93 us
    pallas_call x6 -> x8, Pallas kernels: 2.71 us -> 2.7 us  [call(): pl.pallas_call(lambda *refs: body(layout, *refs), out_shape=out_shape, in...]
  transfers between devices with their start and end apart: 21 -> 21, of which waited for: 13 -> 12; matrix products, arithmetic and copies ran while one was open for 4% -> 7% of each run, Pallas kernels for 3% -> 3%
where the time goes in v5:
time: 41.4 us; the launch traced here: 41.2 us
  starting transfers between devices  20.8 us (50%)
  waiting for transfers between devices  13.3 us (32%)
  Pallas kernels  2.7 us (7%)
  local copies, waits for them, and re-layouts  1.96 us (5%)
  between operations  1.55 us (4%)
  other arithmetic  0.88 us (2%)
    ppermute x21, starting transfers between devices, moved(): lax.ppermute(value, AXES, pairs(lambda x, y, c, z: (x ^ dx, y ^ dy, c ^ d...  20.8 us
    ppermute x21, waiting for transfers between devices, moved(): lax.ppermute(value, AXES, pairs(lambda x, y, c, z: (x ^ dx, y ^ dy, c ^ d...  13.3 us
    pallas_call x8, Pallas kernels, call(): pl.pallas_call(lambda *refs: body(layout, *refs), out_shape=out_shape, in...  2.7 us
    dynamic_slice x1, local copies, waits for them, and re-layouts, row_shards(): lax.dynamic_index_in_dim(halves, number, 0, keepdims=False)  0.98 us
    unnamed x8, local copies, waits for them, and re-layouts  0.93 us
  transfers between devices with their start and end apart: 21, of which 12 were waited for; matrix products, arithmetic and copies ran while one was open for 7% of the time, Pallas kernels for 3%

profile of v5, /device:TPU:0, one launch (start us, length us, event | category | flops | bytes accessed | tf_op | source)
XLA Modules:
  0.0 41.2 jit_solution(15152347963209232485)
XLA Ops:
  0.6 0.0 copy-start
  0.6 0.5 %collective-permute-start = (bf16[2,18432]{1,0:T(2,128)(2,1)}, bf16[2,18432]{1,0:T(2,128)(2,1)S(1)}, u32[]{:S(2)}, u32[]{:S(2)}) collective-permute-start(bf16[2,18432]{1,0:T(2,128)(2,1)} %param.8), channel_id=1, source_target_pairs={{0,4},{1,5},{2,6},{3,7},{4,0},{5,1},{6,2},{7,3},{8,12},{9,13},{10,... | collective-permute-start | bytes 221192 | tf_op jit(solution)/shard_map/ppermute | solution.py:155
  1.2 0.9 %copy.12 = bf16[1,2,72,256]{3,2,1,0:T(8,128)(2,1)S(1)} copy(bf16[1,2,72,256]{3,1,2,0:T(2,128)(2,1)} %bitcast.35) | data formatting | bytes 147456
  2.8 0.0 collective-permute-done
  2.8 0.1 fusion.refs_0_
  2.9 4.8 %collective-permute-start.1 = (bf16[2,72,128]{2,1,0:T(8,128)(2,1)S(1)}, bf16[2,72,128]{2,1,0:T(8,128)(2,1)S(1)}, u32[]{:S(2)}, u32[]{:S(2)}) collective-permute-start(bf16[2,72,128]{2,1,0:T(8,128)(2,1)S(1)} %fusion.refs_0_), channel_id=1, source_target_pairs={{0,10},{1,11},{2,8},{3,9},{4,14},{5,15},{6,12},{7,13},{8,2},{9,3},... | collective-permute-start | bytes 110600 | tf_op jit(solution)/shard_map/ppermute | solution.py:155
  7.7 0.3 collective-permute-start.2
  8.0 0.3 collective-permute-start.3
  8.3 1.0 %constant_dynamic-slice_fusion = (bf16[1,256,256]{2,1,0:T(8,128)(2,1)S(1)}, bf16[1,256,256]{2,1,0:T(8,128)(2,1)S(1)}) fusion(bf16[2,256,256]{2,1,0:T(8,128)(2,1)} %bitcast.32, s32[]{:T(128)S(6)} %select_n.90, bf16[2,256,256]{2,1,0:T(8,128)(2,1)} %bitcast.30), kind=kLoop, calls=%fused_computation.15 | loop fusion | bytes 524292 | tf_op jit(solution)/shard_map/jit(dynamic_index_in_dim)/dynamic_slice | solution.py:415
  9.4 0.0 copy-start.1
  9.4 0.0 copy-start.2
  9.4 1.8 %collective-permute-start.8 = (bf16[2,256,256]{2,1,0:T(8,128)(2,1)S(1)}, bf16[2,256,256]{2,1,0:T(8,128)(2,1)S(1)}, u32[]{:S(2)}, u32[]{:S(2)}) collective-permute-start(bf16[2,256,256]{2,1,0:T(8,128)(2,1)S(1)} %give.1), channel_id=1, source_target_pairs={{0,8},{1,9},{2,10},{3,11},{4,12},{5,13},{6,14},{7,15},{8,0},{9,1},... | collective-permute-start | bytes 786440 | tf_op jit(solution)/shard_map/ppermute | solution.py:155
  11.2 0.0 collective-permute-done.1.refs_1_
  11.2 1.7 %collective-permute-done.2.refs_2_ = bf16[2,72,128]{2,1,0:T(8,128)(2,1)S(1)} collective-permute-done((bf16[2,72,128]{2,1,0:T(8,128)(2,1)S(1)}, bf16[2,72,128]{2,1,0:T(8,128)(2,1)S(1)}, u32[]{:S(2)}, u32[]{:S(2)}) %collective-permute-start.2) | collective-permute-done | bytes 36896 | tf_op jit(solution)/shard_map/ppermute | solution.py:155
  12.9 0.0 collective-permute-done.3.refs_3_
  12.9 0.1 group.1.refs_0_
  13.1 2.2 %collective-permute-start.4 = (bf16[2,200,128]{2,1,0:T(8,128)(2,1)S(1)}, bf16[2,200,128]{2,1,0:T(8,128)(2,1)S(1)}, u32[]{:S(2)}, u32[]{:S(2)}) collective-permute-start(bf16[2,200,128]{2,1,0:T(8,128)(2,1)S(1)} %group.1.refs_0_), channel_id=1, source_target_pairs={{0,17},{1,16},{2,19},{3,18},{4,21},{5,20},{6,23},{7,22},{8,25},{9,... | collective-permute-start | bytes 307208 | tf_op jit(solution)/shard_map/ppermute | solution.py:155
  15.2 0.8 %collective-permute-start.5 = (bf16[2,200,128]{2,1,0:T(8,128)(2,1)S(1)}, bf16[2,200,128]{2,1,0:T(8,128)(2,1)S(1)}, u32[]{:S(2)}, u32[]{:S(2)}) collective-permute-start(bf16[2,200,128]{2,1,0:T(8,128)(2,1)S(1)} %group.1.refs_0_), channel_id=1, source_target_pairs={{0,1},{1,0},{2,3},{3,2},{4,5},{5,4},{6,7},{7,6},{8,9},{9,8},{10,11... | collective-permute-start | bytes 307208 | tf_op jit(solution)/shard_map/ppermute | solution.py:155
  16.1 0.5 %collective-permute-start.6 = (bf16[2,200,128]{2,1,0:T(8,128)(2,1)S(1)}, bf16[2,200,128]{2,1,0:T(8,128)(2,1)S(1)}, u32[]{:S(2)}, u32[]{:S(2)}) collective-permute-start(bf16[2,200,128]{2,1,0:T(8,128)(2,1)S(1)} %group.1.refs_0_), channel_id=1, source_target_pairs={{0,16},{1,17},{2,18},{3,19},{4,20},{5,21},{6,22},{7,23},{8,24},{9,... | collective-permute-start | bytes 307208 | tf_op jit(solution)/shard_map/ppermute | solution.py:155
  16.6 0.0 copy-done.1
  16.6 0.1 collective-permute-start.7
  16.7 0.9 %collective-permute-done.8.refs_1_.refs_3_ = bf16[2,256,256]{2,1,0:T(8,128)(2,1)S(1)} collective-permute-done((bf16[2,256,256]{2,1,0:T(8,128)(2,1)S(1)}, bf16[2,256,256]{2,1,0:T(8,128)(2,1)S(1)}, u32[]{:S(2)}, u32[]{:S(2)}) %collective-permute-start.8) | collective-permute-done | bytes 262176 | tf_op jit(solution)/shard_map/ppermute | solution.py:155
  17.6 0.1 collective-permute-start.9
  17.7 0.0 copy-done.2
  17.7 0.0 copy-done
  17.7 1.1 %collective-permute-done.4.refs_1_ = bf16[2,200,128]{2,1,0:T(8,128)(2,1)S(1)} collective-permute-done((bf16[2,200,128]{2,1,0:T(8,128)(2,1)S(1)}, bf16[2,200,128]{2,1,0:T(8,128)(2,1)S(1)}, u32[]{:S(2)}, u32[]{:S(2)}) %collective-permute-start.4) | collective-permute-done | bytes 102432 | tf_op jit(solution)/shard_map/ppermute | solution.py:155
  18.8 1.1 %collective-permute-done.5.refs_2_ = bf16[2,200,128]{2,1,0:T(8,128)(2,1)S(1)} collective-permute-done((bf16[2,200,128]{2,1,0:T(8,128)(2,1)S(1)}, bf16[2,200,128]{2,1,0:T(8,128)(2,1)S(1)}, u32[]{:S(2)}, u32[]{:S(2)}) %collective-permute-start.5) | collective-permute-done | bytes 102432 | tf_op jit(solution)/shard_map/ppermute | solution.py:155
  19.9 0.8 %collective-permute-done.6.refs_3_ = bf16[2,200,128]{2,1,0:T(8,128)(2,1)S(1)} collective-permute-done((bf16[2,200,128]{2,1,0:T(8,128)(2,1)S(1)}, bf16[2,200,128]{2,1,0:T(8,128)(2,1)S(1)}, u32[]{:S(2)}, u32[]{:S(2)}) %collective-permute-start.6) | collective-permute-done | bytes 102432 | tf_op jit(solution)/shard_map/ppermute | solution.py:155
  20.7 0.0 collective-permute-done.7.refs_2_
  20.7 0.0 collective-permute-done.9.refs_3_
  20.7 0.1 order.1
  20.9 0.1 collective-permute-start.10
  20.9 0.5 %collective-permute-start.11 = (bf16[768,128]{1,0:T(8,128)(2,1)S(1)}, bf16[768,128]{1,0:T(8,128)(2,1)S(1)}, u32[]{:S(2)}, u32[]{:S(2)}) collective-permute-start(bf16[768,128]{1,0:T(8,128)(2,1)S(1)} %get-tuple-element.60.refs_4_), channel_id=1, source_target_pairs={{0,4},{1,5},{2,6},{3,7},{4,0},{5,1},{6,2},{7,3},{8,12},{9,13},{10,... | collective-permute-start | bytes 589832 | tf_op jit(solution)/shard_map/ppermute | solution.py:155
  21.4 0.9 %collective-permute-done.10.refs_5_ = bf16[768,128]{1,0:T(8,128)(2,1)S(1)} collective-permute-done((bf16[768,128]{1,0:T(8,128)(2,1)S(1)}, bf16[768,128]{1,0:T(8,128)(2,1)S(1)}, u32[]{:S(2)}, u32[]{:S(2)}) %collective-permute-start.10) | collective-permute-done | bytes 196640 | tf_op jit(solution)/shard_map/ppermute | solution.py:155
  22.4 0.5 %block_one.1 = (bf16[6,256,256]{2,1,0:T(8,128)(2,1)S(1)}, f32[512,256]{1,0:T(8,128)S(1)}, bf16[512,256]{1,0:T(8,128)(2,1)S(1)}) custom-call(bf16[256,256]{1,0:T(8,128)(2,1)S(1)} %dynamic-slice_bitcast_fusion.1.refs_0_, bf16[2,256,256]{2,1,0:T(8,128)(2,1)S(1)} %collective-permute-done.8.refs_1_.refs_3_, bf16[256,256]{1,0:T(8,128)(2,1)S(1)} %collective-permute-done.7.refs_2_, ...), custom_call_target="tpu_custom_call" | custom-call | tf_op jit(solution)/shard_map/block_one/pallas_call | solution.py:395
  22.9 0.0 collective-permute-done.11.refs_5_
  22.9 0.7 %block_two.1 = (bf16[256,256]{1,0:T(8,128)(2,1)S(1)}, bf16[256,256]{1,0:T(8,128)(2,1)S(1)}, bf16[512,128]{1,0:T(8,128)(2,1)S(1)}, bf16[512,128]{1,0:T(8,128)(2,1)S(1)}) custom-call(f32[512,256]{1,0:T(8,128)S(1)} %get-tuple-element.57.refs_0_, bf16[512,256]{1,0:T(8,128)(2,1)S(1)} %get-tuple-element.58.refs_1_, ...), custom_call_target="tpu_custom_call" | custom-call | tf_op jit(solution)/shard_map/block_two/pallas_call | solution.py:395
  23.6 0.2 collective-permute-start.13
  23.8 0.5 %collective-permute-start.12 = (bf16[256,256]{1,0:T(8,128)(2,1)S(1)}, bf16[256,256]{1,0:T(8,128)(2,1)S(1)}, u32[]{:S(2)}, u32[]{:S(2)}) collective-permute-start(bf16[256,256]{1,0:T(8,128)(2,1)S(1)} %get-tuple-element.62), channel_id=1, source_target_pairs={{0,8},{1,9},{2,10},{3,11},{4,12},{5,13},{6,14},{7,15},{8,0},{9,1},... | collective-permute-start | bytes 393224 | tf_op jit(solution)/shard_map/ppermute | solution.py:155
  24.3 0.7 %collective-permute-done.13.refs_2_ = bf16[512,128]{1,0:T(8,128)(2,1)S(1)} collective-permute-done((bf16[512,128]{1,0:T(8,128)(2,1)S(1)}, bf16[512,128]{1,0:T(8,128)(2,1)S(1)}, u32[]{:S(2)}, u32[]{:S(2)}) %collective-permute-start.13) | collective-permute-done | bytes 131104 | tf_op jit(solution)/shard_map/ppermute | solution.py:155
  25.0 0.5 %terms.1 = (f32[200,128]{1,0:T(8,128)S(1)}, bf16[200,128]{1,0:T(8,128)(2,1)S(1)}, bf16[200,128]{1,0:T(8,128)(2,1)S(1)}, bf16[200,128]{1,0:T(8,128)(2,1)S(1)}) custom-call(bf16[6,256,256]{2,1,0:T(8,128)(2,1)S(1)} %get-tuple-element.63.refs_0_, bf16[512,128]{1,0:T(8,128)(2,1)S(1)} %get-tuple-element.64.refs_1_, ...), custom_call_target="tpu_custom_call" | custom-call | tf_op jit(solution)/shard_map/terms/pallas_call | solution.py:395
  25.5 1.5 %collective-permute-start.14 = (bf16[200,128]{1,0:T(8,128)(2,1)S(1)}, bf16[200,128]{1,0:T(8,128)(2,1)S(1)}, u32[]{:S(2)}, u32[]{:S(2)}) collective-permute-start(bf16[200,128]{1,0:T(8,128)(2,1)S(1)} %get-tuple-element.67), channel_id=1, source_target_pairs={{0,17},{1,16},{2,19},{3,18},{4,21},{5,20},{6,23},{7,22},{8,25},{9,... | collective-permute-start | bytes 153608 | tf_op jit(solution)/shard_map/ppermute | solution.py:155
  27.0 0.6 %collective-permute-start.15 = (bf16[200,128]{1,0:T(8,128)(2,1)S(1)}, bf16[200,128]{1,0:T(8,128)(2,1)S(1)}, u32[]{:S(2)}, u32[]{:S(2)}) collective-permute-start(bf16[200,128]{1,0:T(8,128)(2,1)S(1)} %get-tuple-element.68), channel_id=1, source_target_pairs={{0,1},{1,0},{2,3},{3,2},{4,5},{5,4},{6,7},{7,6},{8,9},{9,8},{10,11... | collective-permute-start | bytes 153608 | tf_op jit(solution)/shard_map/ppermute | solution.py:155
  27.6 1.4 %collective-permute-start.16 = (bf16[200,128]{1,0:T(8,128)(2,1)S(1)}, bf16[200,128]{1,0:T(8,128)(2,1)S(1)}, u32[]{:S(2)}, u32[]{:S(2)}) collective-permute-start(bf16[200,128]{1,0:T(8,128)(2,1)S(1)} %get-tuple-element.69), channel_id=1, source_target_pairs={{0,16},{1,17},{2,18},{3,19},{4,20},{5,21},{6,22},{7,23},{8,24},{9,... | collective-permute-start | bytes 153608 | tf_op jit(solution)/shard_map/ppermute | solution.py:155
  29.1 2.0 %collective-permute-done.14.refs_1_ = bf16[200,128]{1,0:T(8,128)(2,1)S(1)} collective-permute-done((bf16[200,128]{1,0:T(8,128)(2,1)S(1)}, bf16[200,128]{1,0:T(8,128)(2,1)S(1)}, u32[]{:S(2)}, u32[]{:S(2)}) %collective-permute-start.14) | collective-permute-done | bytes 51232 | tf_op jit(solution)/shard_map/ppermute | solution.py:155
  31.0 0.0 collective-permute-done.15.refs_2_
  31.1 0.6 %collective-permute-done.16.refs_3_ = bf16[200,128]{1,0:T(8,128)(2,1)S(1)} collective-permute-done((bf16[200,128]{1,0:T(8,128)(2,1)S(1)}, bf16[200,128]{1,0:T(8,128)(2,1)S(1)}, u32[]{:S(2)}, u32[]{:S(2)}) %collective-permute-start.16) | collective-permute-done | bytes 51232 | tf_op jit(solution)/shard_map/ppermute | solution.py:155
  31.7 0.1 chips.1
  31.8 2.8 %collective-permute-start.17 = (bf16[72,128]{1,0:T(8,128)(2,1)S(1)}, bf16[72,128]{1,0:T(8,128)(2,1)S(1)}, u32[]{:S(2)}, u32[]{:S(2)}) collective-permute-start(bf16[72,128]{1,0:T(8,128)(2,1)S(1)} %get-tuple-element.71), channel_id=1, source_target_pairs={{0,10},{1,11},{2,8},{3,9},{4,14},{5,15},{6,12},{7,13},{8,2},{9,3},... | collective-permute-start | bytes 55304 | tf_op jit(solution)/shard_map/ppermute | solution.py:155
  34.6 0.5 %collective-permute-start.18 = (bf16[72,128]{1,0:T(8,128)(2,1)S(1)}, bf16[72,128]{1,0:T(8,128)(2,1)S(1)}, u32[]{:S(2)}, u32[]{:S(2)}) collective-permute-start(bf16[72,128]{1,0:T(8,128)(2,1)S(1)} %get-tuple-element.72), channel_id=1, source_target_pairs={{0,2},{1,3},{2,0},{3,1},{4,6},{5,7},{6,4},{7,5},{8,10},{9,11},{10,... | collective-permute-start | bytes 55304 | tf_op jit(solution)/shard_map/ppermute | solution.py:155
  35.1 1.2 %collective-permute-start.19 = (bf16[72,128]{1,0:T(8,128)(2,1)S(1)}, bf16[72,128]{1,0:T(8,128)(2,1)S(1)}, u32[]{:S(2)}, u32[]{:S(2)}) collective-permute-start(bf16[72,128]{1,0:T(8,128)(2,1)S(1)} %get-tuple-element.73), channel_id=1, source_target_pairs={{0,8},{1,9},{2,10},{3,11},{4,12},{5,13},{6,14},{7,15},{8,0},{9,1},... | collective-permute-start | bytes 55304 | tf_op jit(solution)/shard_map/ppermute | solution.py:155
  36.3 0.0 collective-permute-done.12
  36.3 1.3 %collective-permute-done.17 = bf16[72,128]{1,0:T(8,128)(2,1)S(1)} collective-permute-done((bf16[72,128]{1,0:T(8,128)(2,1)S(1)}, bf16[72,128]{1,0:T(8,128)(2,1)S(1)}, u32[]{:S(2)}, u32[]{:S(2)}) %collective-permute-start.17) | collective-permute-done | bytes 18464 | tf_op jit(solution)/shard_map/ppermute | solution.py:155
  37.6 1.6 %collective-permute-done.18 = bf16[72,128]{1,0:T(8,128)(2,1)S(1)} collective-permute-done((bf16[72,128]{1,0:T(8,128)(2,1)S(1)}, bf16[72,128]{1,0:T(8,128)(2,1)S(1)}, u32[]{:S(2)}, u32[]{:S(2)}) %collective-permute-start.18) | collective-permute-done | bytes 18464 | tf_op jit(solution)/shard_map/ppermute | solution.py:155
  39.2 0.0 collective-permute-done.19
  39.3 0.1 collective-permute-start.20
  39.3 0.7 %pad_maximum_fusion.1 = bf16[2,256,256]{2,1,0:T(8,128)(2,1)} fusion(bf16[1,256,256]{2,1,0:T(8,128)(2,1)S(1)} %get-tuple-element.75, bf16[1,256,256]{2,1,0:T(8,128)(2,1)S(1)} %get-tuple-element.74), kind=kLoop, calls=%fused_computation.1 | loop fusion | flops 131072 | bytes 524288 | tf_op jit(solution)/shard_map/stack | solution.py:487
  40.1 0.5 %collective-permute-done.20.refs_1_ = f32[72,128]{1,0:T(8,128)S(1)} collective-permute-done((f32[72,128]{1,0:T(8,128)S(1)}, f32[72,128]{1,0:T(8,128)S(1)}, u32[]{:S(2)}, u32[]{:S(2)}) %collective-permute-start.20) | collective-permute-done | bytes 36896 | tf_op jit(solution)/shard_map/ppermute | solution.py:155
  40.5 0.6 %total.1 = f32[144,128]{1,0:T(8,128)} custom-call(f32[72,128]{1,0:T(8,128)S(1)} %convert_add_fusion.refs_0_, f32[72,128]{1,0:T(8,128)S(1)} %collective-permute-done.20.refs_1_), custom_call_target="tpu_custom_call" | custom-call | tf_op jit(solution)/shard_map/total/pallas_call | solution.py:395
  (10 shorter events, 0.1 us)
Async XLA Ops:
  0.6 17.1 %copy-start = (f32[360,4,256]{2,1,0:T(4,128)S(1)}, f32[360,4,256]{2,1,0:T(4,128)}, u32[]{:S(2)}) copy-start(f32[360,4,256]{2,1,0:T(4,128)} %param.7) | copy-start | bytes 4423684
  0.6 2.1 %collective-permute-start = (bf16[2,18432]{1,0:T(2,128)(2,1)}, bf16[2,18432]{1,0:T(2,128)(2,1)S(1)}, u32[]{:S(2)}, u32[]{:S(2)}) collective-permute-start(bf16[2,18432]{1,0:T(2,128)(2,1)} %param.8), channel_id=1, source_target_pairs={{0,4},{1,5},{2,6},{3,7},{4,0},{5,1},{6,2},{7,3},{8,12},{9,13},{10,... | collective-permute-start | bytes 221192 | tf_op jit(solution)/shard_map/ppermute | solution.py:155
  2.9 8.3 %collective-permute-start.1 = (bf16[2,72,128]{2,1,0:T(8,128)(2,1)S(1)}, bf16[2,72,128]{2,1,0:T(8,128)(2,1)S(1)}, u32[]{:S(2)}, u32[]{:S(2)}) collective-permute-start(bf16[2,72,128]{2,1,0:T(8,128)(2,1)S(1)} %fusion.refs_0_), channel_id=1, source_target_pairs={{0,10},{1,11},{2,8},{3,9},{4,14},{5,15},{6,12},{7,13},{8,2},{9,3},... | collective-permute-start | bytes 110600 | tf_op jit(solution)/shard_map/ppermute | solution.py:155
  7.7 5.3 %collective-permute-start.2 = (bf16[2,72,128]{2,1,0:T(8,128)(2,1)S(1)}, bf16[2,72,128]{2,1,0:T(8,128)(2,1)S(1)}, u32[]{:S(2)}, u32[]{:S(2)}) collective-permute-start(bf16[2,72,128]{2,1,0:T(8,128)(2,1)S(1)} %fusion.refs_0_), channel_id=1, source_target_pairs={{0,2},{1,3},{2,0},{3,1},{4,6},{5,7},{6,4},{7,5},{8,10},{9,11},{10,... | collective-permute-start | bytes 110600 | tf_op jit(solution)/shard_map/ppermute | solution.py:155
  8.0 4.9 %collective-permute-start.3 = (bf16[2,72,128]{2,1,0:T(8,128)(2,1)S(1)}, bf16[2,72,128]{2,1,0:T(8,128)(2,1)S(1)}, u32[]{:S(2)}, u32[]{:S(2)}) collective-permute-start(bf16[2,72,128]{2,1,0:T(8,128)(2,1)S(1)} %fusion.refs_0_), channel_id=1, source_target_pairs={{0,8},{1,9},{2,10},{3,11},{4,12},{5,13},{6,14},{7,15},{8,0},{9,1},... | collective-permute-start | bytes 110600 | tf_op jit(solution)/shard_map/ppermute | solution.py:155
  9.4 7.3 %copy-start.1 = (bf16[1,64,8,256]{3,2,1,0:T(8,128)(2,1)S(1)}, bf16[1,64,8,256]{3,2,1,0:T(8,128)(2,1)}, u32[]{:S(2)}) copy-start(bf16[1,64,8,256]{3,2,1,0:T(8,128)(2,1)} %param.5) | copy-start | bytes 786436
  9.4 8.3 %copy-start.2 = (bf16[1,64,8,256]{3,2,1,0:T(8,128)(2,1)S(1)}, bf16[1,64,8,256]{3,2,1,0:T(8,128)(2,1)}, u32[]{:S(2)}) copy-start(bf16[1,64,8,256]{3,2,1,0:T(8,128)(2,1)} %param.9) | copy-start | bytes 786436
  9.4 8.2 %collective-permute-start.8 = (bf16[2,256,256]{2,1,0:T(8,128)(2,1)S(1)}, bf16[2,256,256]{2,1,0:T(8,128)(2,1)S(1)}, u32[]{:S(2)}, u32[]{:S(2)}) collective-permute-start(bf16[2,256,256]{2,1,0:T(8,128)(2,1)S(1)} %give.1), channel_id=1, source_target_pairs={{0,8},{1,9},{2,10},{3,11},{4,12},{5,13},{6,14},{7,15},{8,0},{9,1},... | collective-permute-start | bytes 786440 | tf_op jit(solution)/shard_map/ppermute | solution.py:155
  13.1 5.8 %collective-permute-start.4 = (bf16[2,200,128]{2,1,0:T(8,128)(2,1)S(1)}, bf16[2,200,128]{2,1,0:T(8,128)(2,1)S(1)}, u32[]{:S(2)}, u32[]{:S(2)}) collective-permute-start(bf16[2,200,128]{2,1,0:T(8,128)(2,1)S(1)} %group.1.refs_0_), channel_id=1, source_target_pairs={{0,17},{1,16},{2,19},{3,18},{4,21},{5,20},{6,23},{7,22},{8,25},{9,... | collective-permute-start | bytes 307208 | tf_op jit(solution)/shard_map/ppermute | solution.py:155
  15.2 4.7 %collective-permute-start.5 = (bf16[2,200,128]{2,1,0:T(8,128)(2,1)S(1)}, bf16[2,200,128]{2,1,0:T(8,128)(2,1)S(1)}, u32[]{:S(2)}, u32[]{:S(2)}) collective-permute-start(bf16[2,200,128]{2,1,0:T(8,128)(2,1)S(1)} %group.1.refs_0_), channel_id=1, source_target_pairs={{0,1},{1,0},{2,3},{3,2},{4,5},{5,4},{6,7},{7,6},{8,9},{9,8},{10,11... | collective-permute-start | bytes 307208 | tf_op jit(solution)/shard_map/ppermute | solution.py:155
  16.1 4.7 %collective-permute-start.6 = (bf16[2,200,128]{2,1,0:T(8,128)(2,1)S(1)}, bf16[2,200,128]{2,1,0:T(8,128)(2,1)S(1)}, u32[]{:S(2)}, u32[]{:S(2)}) collective-permute-start(bf16[2,200,128]{2,1,0:T(8,128)(2,1)S(1)} %group.1.refs_0_), channel_id=1, source_target_pairs={{0,16},{1,17},{2,18},{3,19},{4,20},{5,21},{6,22},{7,23},{8,24},{9,... | collective-permute-start | bytes 307208 | tf_op jit(solution)/shard_map/ppermute | solution.py:155
  16.6 4.1 %collective-permute-start.7 = (bf16[256,256]{1,0:T(8,128)(2,1)S(1)}, bf16[256,256]{1,0:T(8,128)(2,1)S(1)}, u32[]{:S(2)}, u32[]{:S(2)}) collective-permute-start(bf16[256,256]{1,0:T(8,128)(2,1)S(1)} %dynamic-slice_bitcast_fusion.1.refs_0_), channel_id=1, source_target_pairs={{0,4},{1,5},{2,6},{3,7},{4,0},{5,1},{6,2},{7,3},{8,12},{9,13},{10,... | collective-permute-start | bytes 393224 | tf_op jit(solution)/shard_map/ppermute | solution.py:155
  17.6 3.2 %collective-permute-start.9 = (bf16[256,256]{1,0:T(8,128)(2,1)S(1)}, bf16[256,256]{1,0:T(8,128)(2,1)S(1)}, u32[]{:S(2)}, u32[]{:S(2)}) collective-permute-start(bf16[256,256]{1,0:T(8,128)(2,1)S(1)} %slice_bitcast_fusion), channel_id=1, source_target_pairs={{0,4},{1,5},{2,6},{3,7},{4,0},{5,1},{6,2},{7,3},{8,12},{9,13},{10,... | collective-permute-start | bytes 393224 | tf_op jit(solution)/shard_map/ppermute | solution.py:155
  20.9 1.5 %collective-permute-start.10 = (bf16[768,128]{1,0:T(8,128)(2,1)S(1)}, bf16[768,128]{1,0:T(8,128)(2,1)S(1)}, u32[]{:S(2)}, u32[]{:S(2)}) collective-permute-start(bf16[768,128]{1,0:T(8,128)(2,1)S(1)} %get-tuple-element.55.refs_4_), channel_id=1, source_target_pairs={{0,4},{1,5},{2,6},{3,7},{4,0},{5,1},{6,2},{7,3},{8,12},{9,13},{10,... | collective-permute-start | bytes 589832 | tf_op jit(solution)/shard_map/ppermute | solution.py:155
  20.9 1.9 %collective-permute-start.11 = (bf16[768,128]{1,0:T(8,128)(2,1)S(1)}, bf16[768,128]{1,0:T(8,128)(2,1)S(1)}, u32[]{:S(2)}, u32[]{:S(2)}) collective-permute-start(bf16[768,128]{1,0:T(8,128)(2,1)S(1)} %get-tuple-element.60.refs_4_), channel_id=1, source_target_pairs={{0,4},{1,5},{2,6},{3,7},{4,0},{5,1},{6,2},{7,3},{8,12},{9,13},{10,... | collective-permute-start | bytes 589832 | tf_op jit(solution)/shard_map/ppermute | solution.py:155
  23.6 1.4 %collective-permute-start.13 = (bf16[512,128]{1,0:T(8,128)(2,1)S(1)}, bf16[512,128]{1,0:T(8,128)(2,1)S(1)}, u32[]{:S(2)}, u32[]{:S(2)}) collective-permute-start(bf16[512,128]{1,0:T(8,128)(2,1)S(1)} %get-tuple-element.65), channel_id=1, source_target_pairs={{0,4},{1,5},{2,6},{3,7},{4,0},{5,1},{6,2},{7,3},{8,12},{9,13},{10,... | collective-permute-start | bytes 393224 | tf_op jit(solution)/shard_map/ppermute | solution.py:155
  23.8 12.5 %collective-permute-start.12 = (bf16[256,256]{1,0:T(8,128)(2,1)S(1)}, bf16[256,256]{1,0:T(8,128)(2,1)S(1)}, u32[]{:S(2)}, u32[]{:S(2)}) collective-permute-start(bf16[256,256]{1,0:T(8,128)(2,1)S(1)} %get-tuple-element.62), channel_id=1, source_target_pairs={{0,8},{1,9},{2,10},{3,11},{4,12},{5,13},{6,14},{7,15},{8,0},{9,1},... | collective-permute-start | bytes 393224 | tf_op jit(solution)/shard_map/ppermute | solution.py:155
  25.5 5.5 %collective-permute-start.14 = (bf16[200,128]{1,0:T(8,128)(2,1)S(1)}, bf16[200,128]{1,0:T(8,128)(2,1)S(1)}, u32[]{:S(2)}, u32[]{:S(2)}) collective-permute-start(bf16[200,128]{1,0:T(8,128)(2,1)S(1)} %get-tuple-element.67), channel_id=1, source_target_pairs={{0,17},{1,16},{2,19},{3,18},{4,21},{5,20},{6,23},{7,22},{8,25},{9,... | collective-permute-start | bytes 153608 | tf_op jit(solution)/shard_map/ppermute | solution.py:155
  27.0 4.1 %collective-permute-start.15 = (bf16[200,128]{1,0:T(8,128)(2,1)S(1)}, bf16[200,128]{1,0:T(8,128)(2,1)S(1)}, u32[]{:S(2)}, u32[]{:S(2)}) collective-permute-start(bf16[200,128]{1,0:T(8,128)(2,1)S(1)} %get-tuple-element.68), channel_id=1, source_target_pairs={{0,1},{1,0},{2,3},{3,2},{4,5},{5,4},{6,7},{7,6},{8,9},{9,8},{10,11... | collective-permute-start | bytes 153608 | tf_op jit(solution)/shard_map/ppermute | solution.py:155
  27.6 4.1 %collective-permute-start.16 = (bf16[200,128]{1,0:T(8,128)(2,1)S(1)}, bf16[200,128]{1,0:T(8,128)(2,1)S(1)}, u32[]{:S(2)}, u32[]{:S(2)}) collective-permute-start(bf16[200,128]{1,0:T(8,128)(2,1)S(1)} %get-tuple-element.69), channel_id=1, source_target_pairs={{0,16},{1,17},{2,18},{3,19},{4,20},{5,21},{6,22},{7,23},{8,24},{9,... | collective-permute-start | bytes 153608 | tf_op jit(solution)/shard_map/ppermute | solution.py:155
  31.8 5.8 %collective-permute-start.17 = (bf16[72,128]{1,0:T(8,128)(2,1)S(1)}, bf16[72,128]{1,0:T(8,128)(2,1)S(1)}, u32[]{:S(2)}, u32[]{:S(2)}) collective-permute-start(bf16[72,128]{1,0:T(8,128)(2,1)S(1)} %get-tuple-element.71), channel_id=1, source_target_pairs={{0,10},{1,11},{2,8},{3,9},{4,14},{5,15},{6,12},{7,13},{8,2},{9,3},... | collective-permute-start | bytes 55304 | tf_op jit(solution)/shard_map/ppermute | solution.py:155
  34.6 4.7 %collective-permute-start.18 = (bf16[72,128]{1,0:T(8,128)(2,1)S(1)}, bf16[72,128]{1,0:T(8,128)(2,1)S(1)}, u32[]{:S(2)}, u32[]{:S(2)}) collective-permute-start(bf16[72,128]{1,0:T(8,128)(2,1)S(1)} %get-tuple-element.72), channel_id=1, source_target_pairs={{0,2},{1,3},{2,0},{3,1},{4,6},{5,7},{6,4},{7,5},{8,10},{9,11},{10,... | collective-permute-start | bytes 55304 | tf_op jit(solution)/shard_map/ppermute | solution.py:155
  35.1 4.2 %collective-permute-start.19 = (bf16[72,128]{1,0:T(8,128)(2,1)S(1)}, bf16[72,128]{1,0:T(8,128)(2,1)S(1)}, u32[]{:S(2)}, u32[]{:S(2)}) collective-permute-start(bf16[72,128]{1,0:T(8,128)(2,1)S(1)} %get-tuple-element.73), channel_id=1, source_target_pairs={{0,8},{1,9},{2,10},{3,11},{4,12},{5,13},{6,14},{7,15},{8,0},{9,1},... | collective-permute-start | bytes 55304 | tf_op jit(solution)/shard_map/ppermute | solution.py:155
  39.3 1.3 %collective-permute-start.20 = (f32[72,128]{1,0:T(8,128)S(1)}, f32[72,128]{1,0:T(8,128)S(1)}, u32[]{:S(2)}, u32[]{:S(2)}) collective-permute-start(f32[72,128]{1,0:T(8,128)S(1)} %convert_add_fusion.refs_0_), channel_id=1, source_target_pairs={{0,4},{1,5},{2,6},{3,7},{4,0},{5,1},{6,2},{7,3},{8,12},{9,13},{10,... | collective-permute-start | bytes 110600 | tf_op jit(solution)/shard_map/ppermute | solution.py:155

commit v6 on v5

--- a/solution.py
+++ b/solution.py
@@ -211,6 +211,17 @@
 
 def copy_kernel(layout, value_ref, out_ref):
     out_ref[...] = value_ref[...]
+
+
+def piece_kernel(layout, own_ref, near_ref, out_ref):
+    x, y, c, z = place()
+    lane = out_ref.shape[2]
+    own, near = own_ref[...], near_ref[...]
+    own = jnp.where(c == 0, own[:, :, :lane], own[:, :, lane:])
+    near = jnp.where(c == 0, near[:, :, :lane], near[:, :, lane:])
+    row = lax.broadcasted_iota(jnp.int32, out_ref.shape, 1)
+    own_rows = (row < chosen(layout.low, (x, y, z), 0)) == (c == 1)
+    out_ref[...] = jnp.where(own_rows, own, near)
 
 
 def group_kernel(layout, own_ref, far0_ref, far1_ref, far2_ref, out_ref, total):
@@ -404,12 +415,8 @@
         )(*operands)
 
     shard = flat_weights.reshape(2, shard_rows, width)
-    left, right = shard[:, :, :lane], shard[:, :, lane:]
     near = moved(flat_weights, dc=1).reshape(shard.shape)
-    near = jnp.where(c == 0, near[:, :, :lane], near[:, :, lane:])
-    row = lax.broadcasted_iota(jnp.int32, near.shape, 1)
-    from_one = row < chosen(layout.low, (x, y, z), 0)
-    piece = jnp.where(from_one == (c == 1), jnp.where(c == 0, left, right), near)
+    piece = call("piece", piece_kernel, shape((2, shard_rows, lane), bf16), [], shard, near)
 
     halves_x, halves_ct = (array.reshape(2, half, width) for array in (inputs, cotangent))
     pick = lambda halves, number: lax.dynamic_index_in_dim(halves, number, 0, keepdims=False)

time: 41.4 us -> 41.3 us (level)
    pallas_call x8 -> x9, Pallas kernels: 2.7 us -> 2.74 us  [call(): pl.pallas_call(lambda *refs: body(layout, *refs), out_shape=out_shape, in...]
where the time goes in v6:
time: 41.3 us; the launch traced here: 41.1 us
  starting transfers between devices  20.8 us (50%)
  waiting for transfers between devices  13.3 us (32%)
  Pallas kernels  2.74 us (7%)
  local copies, waits for them, and re-layouts  1.96 us (5%)
  between operations  1.51 us (4%)
  other arithmetic  0.79 us (2%)
    ppermute x21, starting transfers between devices, moved(): lax.ppermute(value, AXES, pairs(lambda x, y, c, z: (x ^ dx, y ^ dy, c ^ d...  20.8 us
    ppermute x21, waiting for transfers between devices, moved(): lax.ppermute(value, AXES, pairs(lambda x, y, c, z: (x ^ dx, y ^ dy, c ^ d...  13.3 us
    pallas_call x9, Pallas kernels, call(): pl.pallas_call(lambda *refs: body(layout, *refs), out_shape=out_shape, in...  2.74 us
    dynamic_slice x1, local copies, waits for them, and re-layouts, row_shards(): lax.dynamic_index_in_dim(halves, number, 0, keepdims=False)  0.98 us
    unnamed x8, local copies, waits for them, and re-layouts  0.93 us
  transfers between devices with their start and end apart: 21, of which 12 were waited for; matrix products, arithmetic and copies ran while one was open for 7% of the time, Pallas kernels for 3%

profile of v6, /device:TPU:0, one launch (start us, length us, event | category | flops | bytes accessed | tf_op | source)
XLA Modules:
  0.0 41.1 jit_solution(14230661446734838252)
XLA Ops:
  0.6 0.0 copy-start
  0.6 0.5 %collective-permute-start = (bf16[2,18432]{1,0:T(2,128)(2,1)}, bf16[2,18432]{1,0:T(2,128)(2,1)S(1)}, u32[]{:S(2)}, u32[]{:S(2)}) collective-permute-start(bf16[2,18432]{1,0:T(2,128)(2,1)} %param.8), channel_id=1, source_target_pairs={{0,4},{1,5},{2,6},{3,7},{4,0},{5,1},{6,2},{7,3},{8,12},{9,13},{10,... | collective-permute-start | bytes 221192 | tf_op jit(solution)/shard_map/ppermute | solution.py:155
  1.2 0.9 %copy.12 = bf16[1,2,72,256]{3,2,1,0:T(8,128)(2,1)S(1)} copy(bf16[1,2,72,256]{3,1,2,0:T(2,128)(2,1)} %bitcast.35) | data formatting | bytes 147456
  2.7 0.0 collective-permute-done
  2.8 4.8 %collective-permute-start.1 = (bf16[2,72,128]{2,1,0:T(8,128)(2,1)S(1)}, bf16[2,72,128]{2,1,0:T(8,128)(2,1)S(1)}, u32[]{:S(2)}, u32[]{:S(2)}) collective-permute-start(bf16[2,72,128]{2,1,0:T(8,128)(2,1)S(1)} %piece.1.refs_0_), channel_id=1, source_target_pairs={{0,10},{1,11},{2,8},{3,9},{4,14},{5,15},{6,12},{7,13},{8,2},{9,3},... | collective-permute-start | bytes 110600 | tf_op jit(solution)/shard_map/ppermute | solution.py:155
  7.6 0.3 collective-permute-start.2
  7.9 0.3 collective-permute-start.3
  8.2 1.0 %constant_dynamic-slice_fusion = (bf16[1,256,256]{2,1,0:T(8,128)(2,1)S(1)}, bf16[1,256,256]{2,1,0:T(8,128)(2,1)S(1)}) fusion(bf16[2,256,256]{2,1,0:T(8,128)(2,1)} %bitcast.32, s32[]{:T(128)S(6)} %select_n.33, bf16[2,256,256]{2,1,0:T(8,128)(2,1)} %bitcast.30), kind=kLoop, calls=%fused_computation.11 | loop fusion | bytes 524292 | tf_op jit(solution)/shard_map/jit(dynamic_index_in_dim)/dynamic_slice | solution.py:422
  9.3 0.0 copy-start.1
  9.3 0.0 copy-start.2
  9.3 1.8 %collective-permute-start.8 = (bf16[2,256,256]{2,1,0:T(8,128)(2,1)S(1)}, bf16[2,256,256]{2,1,0:T(8,128)(2,1)S(1)}, u32[]{:S(2)}, u32[]{:S(2)}) collective-permute-start(bf16[2,256,256]{2,1,0:T(8,128)(2,1)S(1)} %give.1), channel_id=1, source_target_pairs={{0,8},{1,9},{2,10},{3,11},{4,12},{5,13},{6,14},{7,15},{8,0},{9,1},... | collective-permute-start | bytes 786440 | tf_op jit(solution)/shard_map/ppermute | solution.py:155
  11.1 0.0 collective-permute-done.1.refs_1_
  11.1 1.7 %collective-permute-done.2.refs_2_ = bf16[2,72,128]{2,1,0:T(8,128)(2,1)S(1)} collective-permute-done((bf16[2,72,128]{2,1,0:T(8,128)(2,1)S(1)}, bf16[2,72,128]{2,1,0:T(8,128)(2,1)S(1)}, u32[]{:S(2)}, u32[]{:S(2)}) %collective-permute-start.2) | collective-permute-done | bytes 36896 | tf_op jit(solution)/shard_map/ppermute | solution.py:155
  12.8 0.0 collective-permute-done.3.refs_3_
  12.8 0.1 group.1.refs_0_
  13.0 2.2 %collective-permute-start.4 = (bf16[2,200,128]{2,1,0:T(8,128)(2,1)S(1)}, bf16[2,200,128]{2,1,0:T(8,128)(2,1)S(1)}, u32[]{:S(2)}, u32[]{:S(2)}) collective-permute-start(bf16[2,200,128]{2,1,0:T(8,128)(2,1)S(1)} %group.1.refs_0_), channel_id=1, source_target_pairs={{0,17},{1,16},{2,19},{3,18},{4,21},{5,20},{6,23},{7,22},{8,25},{9,... | collective-permute-start | bytes 307208 | tf_op jit(solution)/shard_map/ppermute | solution.py:155
  15.1 0.8 %collective-permute-start.5 = (bf16[2,200,128]{2,1,0:T(8,128)(2,1)S(1)}, bf16[2,200,128]{2,1,0:T(8,128)(2,1)S(1)}, u32[]{:S(2)}, u32[]{:S(2)}) collective-permute-start(bf16[2,200,128]{2,1,0:T(8,128)(2,1)S(1)} %group.1.refs_0_), channel_id=1, source_target_pairs={{0,1},{1,0},{2,3},{3,2},{4,5},{5,4},{6,7},{7,6},{8,9},{9,8},{10,11... | collective-permute-start | bytes 307208 | tf_op jit(solution)/shard_map/ppermute | solution.py:155
  16.0 0.5 %collective-permute-start.6 = (bf16[2,200,128]{2,1,0:T(8,128)(2,1)S(1)}, bf16[2,200,128]{2,1,0:T(8,128)(2,1)S(1)}, u32[]{:S(2)}, u32[]{:S(2)}) collective-permute-start(bf16[2,200,128]{2,1,0:T(8,128)(2,1)S(1)} %group.1.refs_0_), channel_id=1, source_target_pairs={{0,16},{1,17},{2,18},{3,19},{4,20},{5,21},{6,22},{7,23},{8,24},{9,... | collective-permute-start | bytes 307208 | tf_op jit(solution)/shard_map/ppermute | solution.py:155
  16.5 0.0 copy-done.1
  16.5 0.1 collective-permute-start.7
  16.6 0.9 %collective-permute-done.8.refs_1_.refs_3_ = bf16[2,256,256]{2,1,0:T(8,128)(2,1)S(1)} collective-permute-done((bf16[2,256,256]{2,1,0:T(8,128)(2,1)S(1)}, bf16[2,256,256]{2,1,0:T(8,128)(2,1)S(1)}, u32[]{:S(2)}, u32[]{:S(2)}) %collective-permute-start.8) | collective-permute-done | bytes 262176 | tf_op jit(solution)/shard_map/ppermute | solution.py:155
  17.5 0.1 collective-permute-start.9
  17.6 0.0 copy-done.2
  17.6 0.0 copy-done
  17.6 1.1 %collective-permute-done.4.refs_1_ = bf16[2,200,128]{2,1,0:T(8,128)(2,1)S(1)} collective-permute-done((bf16[2,200,128]{2,1,0:T(8,128)(2,1)S(1)}, bf16[2,200,128]{2,1,0:T(8,128)(2,1)S(1)}, u32[]{:S(2)}, u32[]{:S(2)}) %collective-permute-start.4) | collective-permute-done | bytes 102432 | tf_op jit(solution)/shard_map/ppermute | solution.py:155
  18.7 1.1 %collective-permute-done.5.refs_2_ = bf16[2,200,128]{2,1,0:T(8,128)(2,1)S(1)} collective-permute-done((bf16[2,200,128]{2,1,0:T(8,128)(2,1)S(1)}, bf16[2,200,128]{2,1,0:T(8,128)(2,1)S(1)}, u32[]{:S(2)}, u32[]{:S(2)}) %collective-permute-start.5) | collective-permute-done | bytes 102432 | tf_op jit(solution)/shard_map/ppermute | solution.py:155
  19.8 0.8 %collective-permute-done.6.refs_3_ = bf16[2,200,128]{2,1,0:T(8,128)(2,1)S(1)} collective-permute-done((bf16[2,200,128]{2,1,0:T(8,128)(2,1)S(1)}, bf16[2,200,128]{2,1,0:T(8,128)(2,1)S(1)}, u32[]{:S(2)}, u32[]{:S(2)}) %collective-permute-start.6) | collective-permute-done | bytes 102432 | tf_op jit(solution)/shard_map/ppermute | solution.py:155
  20.6 0.0 collective-permute-done.7.refs_2_
  20.6 0.0 collective-permute-done.9.refs_3_
  20.6 0.1 order.1
  20.8 0.1 collective-permute-start.10
  20.8 0.5 %collective-permute-start.11 = (bf16[768,128]{1,0:T(8,128)(2,1)S(1)}, bf16[768,128]{1,0:T(8,128)(2,1)S(1)}, u32[]{:S(2)}, u32[]{:S(2)}) collective-permute-start(bf16[768,128]{1,0:T(8,128)(2,1)S(1)} %get-tuple-element.60.refs_4_), channel_id=1, source_target_pairs={{0,4},{1,5},{2,6},{3,7},{4,0},{5,1},{6,2},{7,3},{8,12},{9,13},{10,... | collective-permute-start | bytes 589832 | tf_op jit(solution)/shard_map/ppermute | solution.py:155
  21.3 0.9 %collective-permute-done.10.refs_5_ = bf16[768,128]{1,0:T(8,128)(2,1)S(1)} collective-permute-done((bf16[768,128]{1,0:T(8,128)(2,1)S(1)}, bf16[768,128]{1,0:T(8,128)(2,1)S(1)}, u32[]{:S(2)}, u32[]{:S(2)}) %collective-permute-start.10) | collective-permute-done | bytes 196640 | tf_op jit(solution)/shard_map/ppermute | solution.py:155
  22.3 0.5 %block_one.1 = (bf16[6,256,256]{2,1,0:T(8,128)(2,1)S(1)}, f32[512,256]{1,0:T(8,128)S(1)}, bf16[512,256]{1,0:T(8,128)(2,1)S(1)}) custom-call(bf16[256,256]{1,0:T(8,128)(2,1)S(1)} %dynamic-slice_bitcast_fusion.1.refs_0_, bf16[2,256,256]{2,1,0:T(8,128)(2,1)S(1)} %collective-permute-done.8.refs_1_.refs_3_, bf16[256,256]{1,0:T(8,128)(2,1)S(1)} %collective-permute-done.7.refs_2_, ...), custom_call_target="tpu_custom_call" | custom-call | tf_op jit(solution)/shard_map/block_one/pallas_call | solution.py:406
  22.8 0.0 collective-permute-done.11.refs_5_
  22.8 0.7 %block_two.1 = (bf16[256,256]{1,0:T(8,128)(2,1)S(1)}, bf16[256,256]{1,0:T(8,128)(2,1)S(1)}, bf16[512,128]{1,0:T(8,128)(2,1)S(1)}, bf16[512,128]{1,0:T(8,128)(2,1)S(1)}) custom-call(f32[512,256]{1,0:T(8,128)S(1)} %get-tuple-element.57.refs_0_, bf16[512,256]{1,0:T(8,128)(2,1)S(1)} %get-tuple-element.58.refs_1_, ...), custom_call_target="tpu_custom_call" | custom-call | tf_op jit(solution)/shard_map/block_two/pallas_call | solution.py:406
  23.5 0.2 collective-permute-start.13
  23.7 0.5 %collective-permute-start.12 = (bf16[256,256]{1,0:T(8,128)(2,1)S(1)}, bf16[256,256]{1,0:T(8,128)(2,1)S(1)}, u32[]{:S(2)}, u32[]{:S(2)}) collective-permute-start(bf16[256,256]{1,0:T(8,128)(2,1)S(1)} %get-tuple-element.62), channel_id=1, source_target_pairs={{0,8},{1,9},{2,10},{3,11},{4,12},{5,13},{6,14},{7,15},{8,0},{9,1},... | collective-permute-start | bytes 393224 | tf_op jit(solution)/shard_map/ppermute | solution.py:155
  24.2 0.7 %collective-permute-done.13.refs_2_ = bf16[512,128]{1,0:T(8,128)(2,1)S(1)} collective-permute-done((bf16[512,128]{1,0:T(8,128)(2,1)S(1)}, bf16[512,128]{1,0:T(8,128)(2,1)S(1)}, u32[]{:S(2)}, u32[]{:S(2)}) %collective-permute-start.13) | collective-permute-done | bytes 131104 | tf_op jit(solution)/shard_map/ppermute | solution.py:155
  24.9 0.5 %terms.1 = (f32[200,128]{1,0:T(8,128)S(1)}, bf16[200,128]{1,0:T(8,128)(2,1)S(1)}, bf16[200,128]{1,0:T(8,128)(2,1)S(1)}, bf16[200,128]{1,0:T(8,128)(2,1)S(1)}) custom-call(bf16[6,256,256]{2,1,0:T(8,128)(2,1)S(1)} %get-tuple-element.63.refs_0_, bf16[512,128]{1,0:T(8,128)(2,1)S(1)} %get-tuple-element.64.refs_1_, ...), custom_call_target="tpu_custom_call" | custom-call | tf_op jit(solution)/shard_map/terms/pallas_call | solution.py:406
  25.4 1.5 %collective-permute-start.14 = (bf16[200,128]{1,0:T(8,128)(2,1)S(1)}, bf16[200,128]{1,0:T(8,128)(2,1)S(1)}, u32[]{:S(2)}, u32[]{:S(2)}) collective-permute-start(bf16[200,128]{1,0:T(8,128)(2,1)S(1)} %get-tuple-element.67), channel_id=1, source_target_pairs={{0,17},{1,16},{2,19},{3,18},{4,21},{5,20},{6,23},{7,22},{8,25},{9,... | collective-permute-start | bytes 153608 | tf_op jit(solution)/shard_map/ppermute | solution.py:155
  26.9 0.6 %collective-permute-start.15 = (bf16[200,128]{1,0:T(8,128)(2,1)S(1)}, bf16[200,128]{1,0:T(8,128)(2,1)S(1)}, u32[]{:S(2)}, u32[]{:S(2)}) collective-permute-start(bf16[200,128]{1,0:T(8,128)(2,1)S(1)} %get-tuple-element.68), channel_id=1, source_target_pairs={{0,1},{1,0},{2,3},{3,2},{4,5},{5,4},{6,7},{7,6},{8,9},{9,8},{10,11... | collective-permute-start | bytes 153608 | tf_op jit(solution)/shard_map/ppermute | solution.py:155
  27.5 1.4 %collective-permute-start.16 = (bf16[200,128]{1,0:T(8,128)(2,1)S(1)}, bf16[200,128]{1,0:T(8,128)(2,1)S(1)}, u32[]{:S(2)}, u32[]{:S(2)}) collective-permute-start(bf16[200,128]{1,0:T(8,128)(2,1)S(1)} %get-tuple-element.69), channel_id=1, source_target_pairs={{0,16},{1,17},{2,18},{3,19},{4,20},{5,21},{6,22},{7,23},{8,24},{9,... | collective-permute-start | bytes 153608 | tf_op jit(solution)/shard_map/ppermute | solution.py:155
  29.0 2.0 %collective-permute-done.14.refs_1_ = bf16[200,128]{1,0:T(8,128)(2,1)S(1)} collective-permute-done((bf16[200,128]{1,0:T(8,128)(2,1)S(1)}, bf16[200,128]{1,0:T(8,128)(2,1)S(1)}, u32[]{:S(2)}, u32[]{:S(2)}) %collective-permute-start.14) | collective-permute-done | bytes 51232 | tf_op jit(solution)/shard_map/ppermute | solution.py:155
  30.9 0.0 collective-permute-done.15.refs_2_
  31.0 0.6 %collective-permute-done.16.refs_3_ = bf16[200,128]{1,0:T(8,128)(2,1)S(1)} collective-permute-done((bf16[200,128]{1,0:T(8,128)(2,1)S(1)}, bf16[200,128]{1,0:T(8,128)(2,1)S(1)}, u32[]{:S(2)}, u32[]{:S(2)}) %collective-permute-start.16) | collective-permute-done | bytes 51232 | tf_op jit(solution)/shard_map/ppermute | solution.py:155
  31.6 0.1 chips.1
  31.7 2.8 %collective-permute-start.17 = (bf16[72,128]{1,0:T(8,128)(2,1)S(1)}, bf16[72,128]{1,0:T(8,128)(2,1)S(1)}, u32[]{:S(2)}, u32[]{:S(2)}) collective-permute-start(bf16[72,128]{1,0:T(8,128)(2,1)S(1)} %get-tuple-element.71), channel_id=1, source_target_pairs={{0,10},{1,11},{2,8},{3,9},{4,14},{5,15},{6,12},{7,13},{8,2},{9,3},... | collective-permute-start | bytes 55304 | tf_op jit(solution)/shard_map/ppermute | solution.py:155
  34.5 0.5 %collective-permute-start.18 = (bf16[72,128]{1,0:T(8,128)(2,1)S(1)}, bf16[72,128]{1,0:T(8,128)(2,1)S(1)}, u32[]{:S(2)}, u32[]{:S(2)}) collective-permute-start(bf16[72,128]{1,0:T(8,128)(2,1)S(1)} %get-tuple-element.72), channel_id=1, source_target_pairs={{0,2},{1,3},{2,0},{3,1},{4,6},{5,7},{6,4},{7,5},{8,10},{9,11},{10,... | collective-permute-start | bytes 55304 | tf_op jit(solution)/shard_map/ppermute | solution.py:155
  35.0 1.2 %collective-permute-start.19 = (bf16[72,128]{1,0:T(8,128)(2,1)S(1)}, bf16[72,128]{1,0:T(8,128)(2,1)S(1)}, u32[]{:S(2)}, u32[]{:S(2)}) collective-permute-start(bf16[72,128]{1,0:T(8,128)(2,1)S(1)} %get-tuple-element.73), channel_id=1, source_target_pairs={{0,8},{1,9},{2,10},{3,11},{4,12},{5,13},{6,14},{7,15},{8,0},{9,1},... | collective-permute-start | bytes 55304 | tf_op jit(solution)/shard_map/ppermute | solution.py:155
  36.2 0.0 collective-permute-done.12
  36.2 1.3 %collective-permute-done.17 = bf16[72,128]{1,0:T(8,128)(2,1)S(1)} collective-permute-done((bf16[72,128]{1,0:T(8,128)(2,1)S(1)}, bf16[72,128]{1,0:T(8,128)(2,1)S(1)}, u32[]{:S(2)}, u32[]{:S(2)}) %collective-permute-start.17) | collective-permute-done | bytes 18464 | tf_op jit(solution)/shard_map/ppermute | solution.py:155
  37.5 1.6 %collective-permute-done.18 = bf16[72,128]{1,0:T(8,128)(2,1)S(1)} collective-permute-done((bf16[72,128]{1,0:T(8,128)(2,1)S(1)}, bf16[72,128]{1,0:T(8,128)(2,1)S(1)}, u32[]{:S(2)}, u32[]{:S(2)}) %collective-permute-start.18) | collective-permute-done | bytes 18464 | tf_op jit(solution)/shard_map/ppermute | solution.py:155
  39.2 0.0 collective-permute-done.19
  39.2 0.1 collective-permute-start.20
  39.3 0.7 %pad_maximum_fusion.1 = bf16[2,256,256]{2,1,0:T(8,128)(2,1)} fusion(bf16[1,256,256]{2,1,0:T(8,128)(2,1)S(1)} %get-tuple-element.75, bf16[1,256,256]{2,1,0:T(8,128)(2,1)S(1)} %get-tuple-element.74), kind=kLoop, calls=%fused_computation.1 | loop fusion | flops 131072 | bytes 524288 | tf_op jit(solution)/shard_map/stack | solution.py:494
  40.0 0.5 %collective-permute-done.20.refs_1_ = f32[72,128]{1,0:T(8,128)S(1)} collective-permute-done((f32[72,128]{1,0:T(8,128)S(1)}, f32[72,128]{1,0:T(8,128)S(1)}, u32[]{:S(2)}, u32[]{:S(2)}) %collective-permute-start.20) | collective-permute-done | bytes 36896 | tf_op jit(solution)/shard_map/ppermute | solution.py:155
  40.5 0.6 %total.1 = f32[144,128]{1,0:T(8,128)} custom-call(f32[72,128]{1,0:T(8,128)S(1)} %convert_add_fusion.refs_0_, f32[72,128]{1,0:T(8,128)S(1)} %collective-permute-done.20.refs_1_), custom_call_target="tpu_custom_call" | custom-call | tf_op jit(solution)/shard_map/total/pallas_call | solution.py:406
  (10 shorter events, 0.2 us)
Async XLA Ops:
  0.6 17.0 %copy-start = (f32[360,4,256]{2,1,0:T(4,128)S(1)}, f32[360,4,256]{2,1,0:T(4,128)}, u32[]{:S(2)}) copy-start(f32[360,4,256]{2,1,0:T(4,128)} %param.7) | copy-start | bytes 4423684
  0.6 2.1 %collective-permute-start = (bf16[2,18432]{1,0:T(2,128)(2,1)}, bf16[2,18432]{1,0:T(2,128)(2,1)S(1)}, u32[]{:S(2)}, u32[]{:S(2)}) collective-permute-start(bf16[2,18432]{1,0:T(2,128)(2,1)} %param.8), channel_id=1, source_target_pairs={{0,4},{1,5},{2,6},{3,7},{4,0},{5,1},{6,2},{7,3},{8,12},{9,13},{10,... | collective-permute-start | bytes 221192 | tf_op jit(solution)/shard_map/ppermute | solution.py:155
  2.8 8.3 %collective-permute-start.1 = (bf16[2,72,128]{2,1,0:T(8,128)(2,1)S(1)}, bf16[2,72,128]{2,1,0:T(8,128)(2,1)S(1)}, u32[]{:S(2)}, u32[]{:S(2)}) collective-permute-start(bf16[2,72,128]{2,1,0:T(8,128)(2,1)S(1)} %piece.1.refs_0_), channel_id=1, source_target_pairs={{0,10},{1,11},{2,8},{3,9},{4,14},{5,15},{6,12},{7,13},{8,2},{9,3},... | collective-permute-start | bytes 110600 | tf_op jit(solution)/shard_map/ppermute | solution.py:155
  7.6 5.3 %collective-permute-start.2 = (bf16[2,72,128]{2,1,0:T(8,128)(2,1)S(1)}, bf16[2,72,128]{2,1,0:T(8,128)(2,1)S(1)}, u32[]{:S(2)}, u32[]{:S(2)}) collective-permute-start(bf16[2,72,128]{2,1,0:T(8,128)(2,1)S(1)} %piece.1.refs_0_), channel_id=1, source_target_pairs={{0,2},{1,3},{2,0},{3,1},{4,6},{5,7},{6,4},{7,5},{8,10},{9,11},{10,... | collective-permute-start | bytes 110600 | tf_op jit(solution)/shard_map/ppermute | solution.py:155
  7.9 4.9 %collective-permute-start.3 = (bf16[2,72,128]{2,1,0:T(8,128)(2,1)S(1)}, bf16[2,72,128]{2,1,0:T(8,128)(2,1)S(1)}, u32[]{:S(2)}, u32[]{:S(2)}) collective-permute-start(bf16[2,72,128]{2,1,0:T(8,128)(2,1)S(1)} %piece.1.refs_0_), channel_id=1, source_target_pairs={{0,8},{1,9},{2,10},{3,11},{4,12},{5,13},{6,14},{7,15},{8,0},{9,1},... | collective-permute-start | bytes 110600 | tf_op jit(solution)/shard_map/ppermute | solution.py:155
  9.3 7.3 %copy-start.1 = (bf16[1,64,8,256]{3,2,1,0:T(8,128)(2,1)S(1)}, bf16[1,64,8,256]{3,2,1,0:T(8,128)(2,1)}, u32[]{:S(2)}) copy-start(bf16[1,64,8,256]{3,2,1,0:T(8,128)(2,1)} %param.5) | copy-start | bytes 786436
  9.3 8.3 %copy-start.2 = (bf16[1,64,8,256]{3,2,1,0:T(8,128)(2,1)S(1)}, bf16[1,64,8,256]{3,2,1,0:T(8,128)(2,1)}, u32[]{:S(2)}) copy-start(bf16[1,64,8,256]{3,2,1,0:T(8,128)(2,1)} %param.9) | copy-start | bytes 786436
  9.3 8.2 %collective-permute-start.8 = (bf16[2,256,256]{2,1,0:T(8,128)(2,1)S(1)}, bf16[2,256,256]{2,1,0:T(8,128)(2,1)S(1)}, u32[]{:S(2)}, u32[]{:S(2)}) collective-permute-start(bf16[2,256,256]{2,1,0:T(8,128)(2,1)S(1)} %give.1), channel_id=1, source_target_pairs={{0,8},{1,9},{2,10},{3,11},{4,12},{5,13},{6,14},{7,15},{8,0},{9,1},... | collective-permute-start | bytes 786440 | tf_op jit(solution)/shard_map/ppermute | solution.py:155
  13.0 5.8 %collective-permute-start.4 = (bf16[2,200,128]{2,1,0:T(8,128)(2,1)S(1)}, bf16[2,200,128]{2,1,0:T(8,128)(2,1)S(1)}, u32[]{:S(2)}, u32[]{:S(2)}) collective-permute-start(bf16[2,200,128]{2,1,0:T(8,128)(2,1)S(1)} %group.1.refs_0_), channel_id=1, source_target_pairs={{0,17},{1,16},{2,19},{3,18},{4,21},{5,20},{6,23},{7,22},{8,25},{9,... | collective-permute-start | bytes 307208 | tf_op jit(solution)/shard_map/ppermute | solution.py:155
  15.1 4.7 %collective-permute-start.5 = (bf16[2,200,128]{2,1,0:T(8,128)(2,1)S(1)}, bf16[2,200,128]{2,1,0:T(8,128)(2,1)S(1)}, u32[]{:S(2)}, u32[]{:S(2)}) collective-permute-start(bf16[2,200,128]{2,1,0:T(8,128)(2,1)S(1)} %group.1.refs_0_), channel_id=1, source_target_pairs={{0,1},{1,0},{2,3},{3,2},{4,5},{5,4},{6,7},{7,6},{8,9},{9,8},{10,11... | collective-permute-start | bytes 307208 | tf_op jit(solution)/shard_map/ppermute | solution.py:155
  16.0 4.7 %collective-permute-start.6 = (bf16[2,200,128]{2,1,0:T(8,128)(2,1)S(1)}, bf16[2,200,128]{2,1,0:T(8,128)(2,1)S(1)}, u32[]{:S(2)}, u32[]{:S(2)}) collective-permute-start(bf16[2,200,128]{2,1,0:T(8,128)(2,1)S(1)} %group.1.refs_0_), channel_id=1, source_target_pairs={{0,16},{1,17},{2,18},{3,19},{4,20},{5,21},{6,22},{7,23},{8,24},{9,... | collective-permute-start | bytes 307208 | tf_op jit(solution)/shard_map/ppermute | solution.py:155
  16.5 4.1 %collective-permute-start.7 = (bf16[256,256]{1,0:T(8,128)(2,1)S(1)}, bf16[256,256]{1,0:T(8,128)(2,1)S(1)}, u32[]{:S(2)}, u32[]{:S(2)}) collective-permute-start(bf16[256,256]{1,0:T(8,128)(2,1)S(1)} %dynamic-slice_bitcast_fusion.1.refs_0_), channel_id=1, source_target_pairs={{0,4},{1,5},{2,6},{3,7},{4,0},{5,1},{6,2},{7,3},{8,12},{9,13},{10,... | collective-permute-start | bytes 393224 | tf_op jit(solution)/shard_map/ppermute | solution.py:155
  17.5 3.2 %collective-permute-start.9 = (bf16[256,256]{1,0:T(8,128)(2,1)S(1)}, bf16[256,256]{1,0:T(8,128)(2,1)S(1)}, u32[]{:S(2)}, u32[]{:S(2)}) collective-permute-start(bf16[256,256]{1,0:T(8,128)(2,1)S(1)} %slice_bitcast_fusion), channel_id=1, source_target_pairs={{0,4},{1,5},{2,6},{3,7},{4,0},{5,1},{6,2},{7,3},{8,12},{9,13},{10,... | collective-permute-start | bytes 393224 | tf_op jit(solution)/shard_map/ppermute | solution.py:155
  20.8 1.5 %collective-permute-start.10 = (bf16[768,128]{1,0:T(8,128)(2,1)S(1)}, bf16[768,128]{1,0:T(8,128)(2,1)S(1)}, u32[]{:S(2)}, u32[]{:S(2)}) collective-permute-start(bf16[768,128]{1,0:T(8,128)(2,1)S(1)} %get-tuple-element.55.refs_4_), channel_id=1, source_target_pairs={{0,4},{1,5},{2,6},{3,7},{4,0},{5,1},{6,2},{7,3},{8,12},{9,13},{10,... | collective-permute-start | bytes 589832 | tf_op jit(solution)/shard_map/ppermute | solution.py:155
  20.8 1.9 %collective-permute-start.11 = (bf16[768,128]{1,0:T(8,128)(2,1)S(1)}, bf16[768,128]{1,0:T(8,128)(2,1)S(1)}, u32[]{:S(2)}, u32[]{:S(2)}) collective-permute-start(bf16[768,128]{1,0:T(8,128)(2,1)S(1)} %get-tuple-element.60.refs_4_), channel_id=1, source_target_pairs={{0,4},{1,5},{2,6},{3,7},{4,0},{5,1},{6,2},{7,3},{8,12},{9,13},{10,... | collective-permute-start | bytes 589832 | tf_op jit(solution)/shard_map/ppermute | solution.py:155
  23.5 1.4 %collective-permute-start.13 = (bf16[512,128]{1,0:T(8,128)(2,1)S(1)}, bf16[512,128]{1,0:T(8,128)(2,1)S(1)}, u32[]{:S(2)}, u32[]{:S(2)}) collective-permute-start(bf16[512,128]{1,0:T(8,128)(2,1)S(1)} %get-tuple-element.65), channel_id=1, source_target_pairs={{0,4},{1,5},{2,6},{3,7},{4,0},{5,1},{6,2},{7,3},{8,12},{9,13},{10,... | collective-permute-start | bytes 393224 | tf_op jit(solution)/shard_map/ppermute | solution.py:155
  23.7 12.5 %collective-permute-start.12 = (bf16[256,256]{1,0:T(8,128)(2,1)S(1)}, bf16[256,256]{1,0:T(8,128)(2,1)S(1)}, u32[]{:S(2)}, u32[]{:S(2)}) collective-permute-start(bf16[256,256]{1,0:T(8,128)(2,1)S(1)} %get-tuple-element.62), channel_id=1, source_target_pairs={{0,8},{1,9},{2,10},{3,11},{4,12},{5,13},{6,14},{7,15},{8,0},{9,1},... | collective-permute-start | bytes 393224 | tf_op jit(solution)/shard_map/ppermute | solution.py:155
  25.4 5.5 %collective-permute-start.14 = (bf16[200,128]{1,0:T(8,128)(2,1)S(1)}, bf16[200,128]{1,0:T(8,128)(2,1)S(1)}, u32[]{:S(2)}, u32[]{:S(2)}) collective-permute-start(bf16[200,128]{1,0:T(8,128)(2,1)S(1)} %get-tuple-element.67), channel_id=1, source_target_pairs={{0,17},{1,16},{2,19},{3,18},{4,21},{5,20},{6,23},{7,22},{8,25},{9,... | collective-permute-start | bytes 153608 | tf_op jit(solution)/shard_map/ppermute | solution.py:155
  26.9 4.1 %collective-permute-start.15 = (bf16[200,128]{1,0:T(8,128)(2,1)S(1)}, bf16[200,128]{1,0:T(8,128)(2,1)S(1)}, u32[]{:S(2)}, u32[]{:S(2)}) collective-permute-start(bf16[200,128]{1,0:T(8,128)(2,1)S(1)} %get-tuple-element.68), channel_id=1, source_target_pairs={{0,1},{1,0},{2,3},{3,2},{4,5},{5,4},{6,7},{7,6},{8,9},{9,8},{10,11... | collective-permute-start | bytes 153608 | tf_op jit(solution)/shard_map/ppermute | solution.py:155
  27.5 4.1 %collective-permute-start.16 = (bf16[200,128]{1,0:T(8,128)(2,1)S(1)}, bf16[200,128]{1,0:T(8,128)(2,1)S(1)}, u32[]{:S(2)}, u32[]{:S(2)}) collective-permute-start(bf16[200,128]{1,0:T(8,128)(2,1)S(1)} %get-tuple-element.69), channel_id=1, source_target_pairs={{0,16},{1,17},{2,18},{3,19},{4,20},{5,21},{6,22},{7,23},{8,24},{9,... | collective-permute-start | bytes 153608 | tf_op jit(solution)/shard_map/ppermute | solution.py:155
  31.7 5.8 %collective-permute-start.17 = (bf16[72,128]{1,0:T(8,128)(2,1)S(1)}, bf16[72,128]{1,0:T(8,128)(2,1)S(1)}, u32[]{:S(2)}, u32[]{:S(2)}) collective-permute-start(bf16[72,128]{1,0:T(8,128)(2,1)S(1)} %get-tuple-element.71), channel_id=1, source_target_pairs={{0,10},{1,11},{2,8},{3,9},{4,14},{5,15},{6,12},{7,13},{8,2},{9,3},... | collective-permute-start | bytes 55304 | tf_op jit(solution)/shard_map/ppermute | solution.py:155
  34.5 4.7 %collective-permute-start.18 = (bf16[72,128]{1,0:T(8,128)(2,1)S(1)}, bf16[72,128]{1,0:T(8,128)(2,1)S(1)}, u32[]{:S(2)}, u32[]{:S(2)}) collective-permute-start(bf16[72,128]{1,0:T(8,128)(2,1)S(1)} %get-tuple-element.72), channel_id=1, source_target_pairs={{0,2},{1,3},{2,0},{3,1},{4,6},{5,7},{6,4},{7,5},{8,10},{9,11},{10,... | collective-permute-start | bytes 55304 | tf_op jit(solution)/shard_map/ppermute | solution.py:155
  35.0 4.2 %collective-permute-start.19 = (bf16[72,128]{1,0:T(8,128)(2,1)S(1)}, bf16[72,128]{1,0:T(8,128)(2,1)S(1)}, u32[]{:S(2)}, u32[]{:S(2)}) collective-permute-start(bf16[72,128]{1,0:T(8,128)(2,1)S(1)} %get-tuple-element.73), channel_id=1, source_target_pairs={{0,8},{1,9},{2,10},{3,11},{4,12},{5,13},{6,14},{7,15},{8,0},{9,1},... | collective-permute-start | bytes 55304 | tf_op jit(solution)/shard_map/ppermute | solution.py:155
  39.2 1.3 %collective-permute-start.20 = (f32[72,128]{1,0:T(8,128)S(1)}, f32[72,128]{1,0:T(8,128)S(1)}, u32[]{:S(2)}, u32[]{:S(2)}) collective-permute-start(f32[72,128]{1,0:T(8,128)S(1)} %convert_add_fusion.refs_0_), channel_id=1, source_target_pairs={{0,4},{1,5},{2,6},{3,7},{4,0},{5,1},{6,2},{7,3},{8,12},{9,13},{10,... | collective-permute-start | bytes 110600 | tf_op jit(solution)/shard_map/ppermute | solution.py:155

commit v7 on v6

--- a/solution.py
+++ b/solution.py
@@ -409,12 +409,13 @@
             in_specs=[vmem] * len(operands),
             out_specs=(vmem,) * len(out_shape) if several else vmem,
             scratch_shapes=scratch,
-            compiler_params=pltpu.CompilerParams(vmem_limit_bytes=16 * 1024 * 1024),
+            compiler_params=pltpu.CompilerParams(vmem_limit_bytes=32 * 1024 * 1024),
             cost_estimate=pl.CostEstimate(flops=cost * 10**9, bytes_accessed=0, transcendentals=0) if cost else None,
             name=name,
         )(*operands)
 
-    shard = flat_weights.reshape(2, shard_rows, width)
+    held = call("hold", copy_kernel, shape(flat_weights.shape, bf16), [], flat_weights)
+    shard = held.reshape(2, shard_rows, width)
     near = moved(flat_weights, dc=1).reshape(shard.shape)
     piece = call("piece", piece_kernel, shape((2, shard_rows, lane), bf16), [], shard, near)
 

time: 41.3 us -> 41.3 us (level)
    pallas_call x9 -> x10, Pallas kernels: 2.74 us -> 2.75 us  [call(): pl.pallas_call(lambda *refs: body(layout, *refs), out_shape=out_shape, in...]
    unnamed x8 -> x10, local copies, waits for them, and re-layouts: 0.93 us -> 0.93 us
  transfers between devices with their start and end apart: 21 -> 21, of which waited for: 12 -> 12; matrix products, arithmetic and copies ran while one was open for 7% -> 4% of each run, Pallas kernels for 3% -> 3%
where the time goes in v7:
time: 41.3 us; the launch traced here: 41.1 us
  starting transfers between devices  20.8 us (50%)
  waiting for transfers between devices  13.3 us (32%)
  Pallas kernels  2.75 us (7%)
  local copies, waits for them, and re-layouts  1.96 us (5%)
  between operations  1.51 us (4%)
  other arithmetic  0.79 us (2%)
    ppermute x21, starting transfers between devices, moved(): lax.ppermute(value, AXES, pairs(lambda x, y, c, z: (x ^ dx, y ^ dy, c ^ d...  20.8 us
    ppermute x21, waiting for transfers between devices, moved(): lax.ppermute(value, AXES, pairs(lambda x, y, c, z: (x ^ dx, y ^ dy, c ^ d...  13.3 us
    pallas_call x10, Pallas kernels, call(): pl.pallas_call(lambda *refs: body(layout, *refs), out_shape=out_shape, in...  2.75 us
    dynamic_slice x1, local copies, waits for them, and re-layouts, row_shards(): lax.dynamic_index_in_dim(halves, number, 0, keepdims=False)  0.98 us
    unnamed x10, local copies, waits for them, and re-layouts  0.93 us
  transfers between devices with their start and end apart: 21, of which 12 were waited for; matrix products, arithmetic and copies ran while one was open for 4% of the time, Pallas kernels for 3%

profile of v7, /device:TPU:0, one launch (start us, length us, event | category | flops | bytes accessed | tf_op | source)
XLA Modules:
  0.0 41.1 jit_solution(1284413698732690050)
XLA Ops:
  0.6 0.0 copy-start
  0.6 0.5 %collective-permute-start = (bf16[2,18432]{1,0:T(2,128)(2,1)}, bf16[2,18432]{1,0:T(2,128)(2,1)S(1)}, u32[]{:S(2)}, u32[]{:S(2)}) collective-permute-start(bf16[2,18432]{1,0:T(2,128)(2,1)} %refs_0_.1), channel_id=1, source_target_pairs={{0,4},{1,5},{2,6},{3,7},{4,0},{5,1},{6,2},{7,3},{8,12},{9,13},{10,... | collective-permute-start | bytes 221192 | tf_op jit(solution)/shard_map/ppermute | solution.py:155
  1.2 0.0 copy-start.1
  1.2 0.9 %copy-done.1 = bf16[2,18432]{1,0:T(2,128)(2,1)S(1)} copy-done((bf16[2,18432]{1,0:T(2,128)(2,1)S(1)}, bf16[2,18432]{1,0:T(2,128)(2,1)}, u32[]{:S(2)}) %copy-start.1) | copy-done | bytes 73752
  2.7 0.0 collective-permute-done
  2.8 4.8 %collective-permute-start.1 = (bf16[2,72,128]{2,1,0:T(8,128)(2,1)S(1)}, bf16[2,72,128]{2,1,0:T(8,128)(2,1)S(1)}, u32[]{:S(2)}, u32[]{:S(2)}) collective-permute-start(bf16[2,72,128]{2,1,0:T(8,128)(2,1)S(1)} %piece.1.refs_0_), channel_id=1, source_target_pairs={{0,10},{1,11},{2,8},{3,9},{4,14},{5,15},{6,12},{7,13},{8,2},{9,3},... | collective-permute-start | bytes 110600 | tf_op jit(solution)/shard_map/ppermute | solution.py:155
  7.6 0.3 collective-permute-start.2
  7.9 0.3 collective-permute-start.3
  8.2 1.0 %constant_dynamic-slice_fusion = (bf16[1,256,256]{2,1,0:T(8,128)(2,1)S(1)}, bf16[1,256,256]{2,1,0:T(8,128)(2,1)S(1)}) fusion(bf16[2,256,256]{2,1,0:T(8,128)(2,1)} %bitcast.33, s32[]{:T(128)S(6)} %select_n.33, bf16[2,256,256]{2,1,0:T(8,128)(2,1)} %bitcast.31), kind=kLoop, calls=%fused_computation.11 | loop fusion | bytes 524292 | tf_op jit(solution)/shard_map/jit(dynamic_index_in_dim)/dynamic_slice | solution.py:423
  9.3 0.0 copy-start.2
  9.3 0.0 copy-start.3
  9.3 1.8 %collective-permute-start.8 = (bf16[2,256,256]{2,1,0:T(8,128)(2,1)S(1)}, bf16[2,256,256]{2,1,0:T(8,128)(2,1)S(1)}, u32[]{:S(2)}, u32[]{:S(2)}) collective-permute-start(bf16[2,256,256]{2,1,0:T(8,128)(2,1)S(1)} %give.1), channel_id=1, source_target_pairs={{0,8},{1,9},{2,10},{3,11},{4,12},{5,13},{6,14},{7,15},{8,0},{9,1},... | collective-permute-start | bytes 786440 | tf_op jit(solution)/shard_map/ppermute | solution.py:155
  11.1 0.0 collective-permute-done.1.refs_1_
  11.1 1.7 %collective-permute-done.2.refs_2_ = bf16[2,72,128]{2,1,0:T(8,128)(2,1)S(1)} collective-permute-done((bf16[2,72,128]{2,1,0:T(8,128)(2,1)S(1)}, bf16[2,72,128]{2,1,0:T(8,128)(2,1)S(1)}, u32[]{:S(2)}, u32[]{:S(2)}) %collective-permute-start.2) | collective-permute-done | bytes 36896 | tf_op jit(solution)/shard_map/ppermute | solution.py:155
  12.8 0.0 collective-permute-done.3.refs_3_
  12.8 0.1 group.1.refs_0_
  13.0 2.2 %collective-permute-start.4 = (bf16[2,200,128]{2,1,0:T(8,128)(2,1)S(1)}, bf16[2,200,128]{2,1,0:T(8,128)(2,1)S(1)}, u32[]{:S(2)}, u32[]{:S(2)}) collective-permute-start(bf16[2,200,128]{2,1,0:T(8,128)(2,1)S(1)} %group.1.refs_0_), channel_id=1, source_target_pairs={{0,17},{1,16},{2,19},{3,18},{4,21},{5,20},{6,23},{7,22},{8,25},{9,... | collective-permute-start | bytes 307208 | tf_op jit(solution)/shard_map/ppermute | solution.py:155
  15.1 0.8 %collective-permute-start.5 = (bf16[2,200,128]{2,1,0:T(8,128)(2,1)S(1)}, bf16[2,200,128]{2,1,0:T(8,128)(2,1)S(1)}, u32[]{:S(2)}, u32[]{:S(2)}) collective-permute-start(bf16[2,200,128]{2,1,0:T(8,128)(2,1)S(1)} %group.1.refs_0_), channel_id=1, source_target_pairs={{0,1},{1,0},{2,3},{3,2},{4,5},{5,4},{6,7},{7,6},{8,9},{9,8},{10,11... | collective-permute-start | bytes 307208 | tf_op jit(solution)/shard_map/ppermute | solution.py:155
  16.0 0.5 %collective-permute-start.6 = (bf16[2,200,128]{2,1,0:T(8,128)(2,1)S(1)}, bf16[2,200,128]{2,1,0:T(8,128)(2,1)S(1)}, u32[]{:S(2)}, u32[]{:S(2)}) collective-permute-start(bf16[2,200,128]{2,1,0:T(8,128)(2,1)S(1)} %group.1.refs_0_), channel_id=1, source_target_pairs={{0,16},{1,17},{2,18},{3,19},{4,20},{5,21},{6,22},{7,23},{8,24},{9,... | collective-permute-start | bytes 307208 | tf_op jit(solution)/shard_map/ppermute | solution.py:155
  16.5 0.0 copy-done.2
  16.5 0.1 collective-permute-start.7
  16.6 0.9 %collective-permute-done.8.refs_1_.refs_3_ = bf16[2,256,256]{2,1,0:T(8,128)(2,1)S(1)} collective-permute-done((bf16[2,256,256]{2,1,0:T(8,128)(2,1)S(1)}, bf16[2,256,256]{2,1,0:T(8,128)(2,1)S(1)}, u32[]{:S(2)}, u32[]{:S(2)}) %collective-permute-start.8) | collective-permute-done | bytes 262176 | tf_op jit(solution)/shard_map/ppermute | solution.py:155
  17.5 0.1 collective-permute-start.9
  17.6 0.0 copy-done.3
  17.6 0.0 copy-done
  17.6 1.1 %collective-permute-done.4.refs_1_ = bf16[2,200,128]{2,1,0:T(8,128)(2,1)S(1)} collective-permute-done((bf16[2,200,128]{2,1,0:T(8,128)(2,1)S(1)}, bf16[2,200,128]{2,1,0:T(8,128)(2,1)S(1)}, u32[]{:S(2)}, u32[]{:S(2)}) %collective-permute-start.4) | collective-permute-done | bytes 102432 | tf_op jit(solution)/shard_map/ppermute | solution.py:155
  18.8 1.1 %collective-permute-done.5.refs_2_ = bf16[2,200,128]{2,1,0:T(8,128)(2,1)S(1)} collective-permute-done((bf16[2,200,128]{2,1,0:T(8,128)(2,1)S(1)}, bf16[2,200,128]{2,1,0:T(8,128)(2,1)S(1)}, u32[]{:S(2)}, u32[]{:S(2)}) %collective-permute-start.5) | collective-permute-done | bytes 102432 | tf_op jit(solution)/shard_map/ppermute | solution.py:155
  19.8 0.8 %collective-permute-done.6.refs_3_ = bf16[2,200,128]{2,1,0:T(8,128)(2,1)S(1)} collective-permute-done((bf16[2,200,128]{2,1,0:T(8,128)(2,1)S(1)}, bf16[2,200,128]{2,1,0:T(8,128)(2,1)S(1)}, u32[]{:S(2)}, u32[]{:S(2)}) %collective-permute-start.6) | collective-permute-done | bytes 102432 | tf_op jit(solution)/shard_map/ppermute | solution.py:155
  20.6 0.0 collective-permute-done.7.refs_2_
  20.7 0.0 collective-permute-done.9.refs_3_
  20.7 0.1 order.1
  20.8 0.1 collective-permute-start.10
  20.8 0.5 %collective-permute-start.11 = (bf16[768,128]{1,0:T(8,128)(2,1)S(1)}, bf16[768,128]{1,0:T(8,128)(2,1)S(1)}, u32[]{:S(2)}, u32[]{:S(2)}) collective-permute-start(bf16[768,128]{1,0:T(8,128)(2,1)S(1)} %get-tuple-element.60.refs_4_), channel_id=1, source_target_pairs={{0,4},{1,5},{2,6},{3,7},{4,0},{5,1},{6,2},{7,3},{8,12},{9,13},{10,... | collective-permute-start | bytes 589832 | tf_op jit(solution)/shard_map/ppermute | solution.py:155
  21.3 0.9 %collective-permute-done.10.refs_5_ = bf16[768,128]{1,0:T(8,128)(2,1)S(1)} collective-permute-done((bf16[768,128]{1,0:T(8,128)(2,1)S(1)}, bf16[768,128]{1,0:T(8,128)(2,1)S(1)}, u32[]{:S(2)}, u32[]{:S(2)}) %collective-permute-start.10) | collective-permute-done | bytes 196640 | tf_op jit(solution)/shard_map/ppermute | solution.py:155
  22.3 0.5 %block_one.1 = (bf16[6,256,256]{2,1,0:T(8,128)(2,1)S(1)}, f32[512,256]{1,0:T(8,128)S(1)}, bf16[512,256]{1,0:T(8,128)(2,1)S(1)}) custom-call(bf16[256,256]{1,0:T(8,128)(2,1)S(1)} %dynamic-slice_bitcast_fusion.1.refs_0_, bf16[2,256,256]{2,1,0:T(8,128)(2,1)S(1)} %collective-permute-done.8.refs_1_.refs_3_, bf16[256,256]{1,0:T(8,128)(2,1)S(1)} %collective-permute-done.7.refs_2_, ...), custom_call_target="tpu_custom_call" | custom-call | tf_op jit(solution)/shard_map/block_one/pallas_call | solution.py:406
  22.8 0.0 collective-permute-done.11.refs_5_
  22.8 0.7 %block_two.1 = (bf16[256,256]{1,0:T(8,128)(2,1)S(1)}, bf16[256,256]{1,0:T(8,128)(2,1)S(1)}, bf16[512,128]{1,0:T(8,128)(2,1)S(1)}, bf16[512,128]{1,0:T(8,128)(2,1)S(1)}) custom-call(f32[512,256]{1,0:T(8,128)S(1)} %get-tuple-element.57.refs_0_, bf16[512,256]{1,0:T(8,128)(2,1)S(1)} %get-tuple-element.58.refs_1_, ...), custom_call_target="tpu_custom_call" | custom-call | tf_op jit(solution)/shard_map/block_two/pallas_call | solution.py:406
  23.5 0.2 collective-permute-start.13
  23.7 0.5 %collective-permute-start.12 = (bf16[256,256]{1,0:T(8,128)(2,1)S(1)}, bf16[256,256]{1,0:T(8,128)(2,1)S(1)}, u32[]{:S(2)}, u32[]{:S(2)}) collective-permute-start(bf16[256,256]{1,0:T(8,128)(2,1)S(1)} %get-tuple-element.62), channel_id=1, source_target_pairs={{0,8},{1,9},{2,10},{3,11},{4,12},{5,13},{6,14},{7,15},{8,0},{9,1},... | collective-permute-start | bytes 393224 | tf_op jit(solution)/shard_map/ppermute | solution.py:155
  24.2 0.7 %collective-permute-done.13.refs_2_ = bf16[512,128]{1,0:T(8,128)(2,1)S(1)} collective-permute-done((bf16[512,128]{1,0:T(8,128)(2,1)S(1)}, bf16[512,128]{1,0:T(8,128)(2,1)S(1)}, u32[]{:S(2)}, u32[]{:S(2)}) %collective-permute-start.13) | collective-permute-done | bytes 131104 | tf_op jit(solution)/shard_map/ppermute | solution.py:155
  24.9 0.5 %terms.1 = (f32[200,128]{1,0:T(8,128)S(1)}, bf16[200,128]{1,0:T(8,128)(2,1)S(1)}, bf16[200,128]{1,0:T(8,128)(2,1)S(1)}, bf16[200,128]{1,0:T(8,128)(2,1)S(1)}) custom-call(bf16[6,256,256]{2,1,0:T(8,128)(2,1)S(1)} %get-tuple-element.63.refs_0_, bf16[512,128]{1,0:T(8,128)(2,1)S(1)} %get-tuple-element.64.refs_1_, ...), custom_call_target="tpu_custom_call" | custom-call | tf_op jit(solution)/shard_map/terms/pallas_call | solution.py:406
  25.4 1.5 %collective-permute-start.14 = (bf16[200,128]{1,0:T(8,128)(2,1)S(1)}, bf16[200,128]{1,0:T(8,128)(2,1)S(1)}, u32[]{:S(2)}, u32[]{:S(2)}) collective-permute-start(bf16[200,128]{1,0:T(8,128)(2,1)S(1)} %get-tuple-element.67), channel_id=1, source_target_pairs={{0,17},{1,16},{2,19},{3,18},{4,21},{5,20},{6,23},{7,22},{8,25},{9,... | collective-permute-start | bytes 153608 | tf_op jit(solution)/shard_map/ppermute | solution.py:155
  26.9 0.6 %collective-permute-start.15 = (bf16[200,128]{1,0:T(8,128)(2,1)S(1)}, bf16[200,128]{1,0:T(8,128)(2,1)S(1)}, u32[]{:S(2)}, u32[]{:S(2)}) collective-permute-start(bf16[200,128]{1,0:T(8,128)(2,1)S(1)} %get-tuple-element.68), channel_id=1, source_target_pairs={{0,1},{1,0},{2,3},{3,2},{4,5},{5,4},{6,7},{7,6},{8,9},{9,8},{10,11... | collective-permute-start | bytes 153608 | tf_op jit(solution)/shard_map/ppermute | solution.py:155
  27.5 1.4 %collective-permute-start.16 = (bf16[200,128]{1,0:T(8,128)(2,1)S(1)}, bf16[200,128]{1,0:T(8,128)(2,1)S(1)}, u32[]{:S(2)}, u32[]{:S(2)}) collective-permute-start(bf16[200,128]{1,0:T(8,128)(2,1)S(1)} %get-tuple-element.69), channel_id=1, source_target_pairs={{0,16},{1,17},{2,18},{3,19},{4,20},{5,21},{6,22},{7,23},{8,24},{9,... | collective-permute-start | bytes 153608 | tf_op jit(solution)/shard_map/ppermute | solution.py:155
  29.0 2.0 %collective-permute-done.14.refs_1_ = bf16[200,128]{1,0:T(8,128)(2,1)S(1)} collective-permute-done((bf16[200,128]{1,0:T(8,128)(2,1)S(1)}, bf16[200,128]{1,0:T(8,128)(2,1)S(1)}, u32[]{:S(2)}, u32[]{:S(2)}) %collective-permute-start.14) | collective-permute-done | bytes 51232 | tf_op jit(solution)/shard_map/ppermute | solution.py:155
  31.0 0.0 collective-permute-done.15.refs_2_
  31.0 0.6 %collective-permute-done.16.refs_3_ = bf16[200,128]{1,0:T(8,128)(2,1)S(1)} collective-permute-done((bf16[200,128]{1,0:T(8,128)(2,1)S(1)}, bf16[200,128]{1,0:T(8,128)(2,1)S(1)}, u32[]{:S(2)}, u32[]{:S(2)}) %collective-permute-start.16) | collective-permute-done | bytes 51232 | tf_op jit(solution)/shard_map/ppermute | solution.py:155
  31.6 0.1 chips.1
  31.8 2.8 %collective-permute-start.17 = (bf16[72,128]{1,0:T(8,128)(2,1)S(1)}, bf16[72,128]{1,0:T(8,128)(2,1)S(1)}, u32[]{:S(2)}, u32[]{:S(2)}) collective-permute-start(bf16[72,128]{1,0:T(8,128)(2,1)S(1)} %get-tuple-element.71), channel_id=1, source_target_pairs={{0,10},{1,11},{2,8},{3,9},{4,14},{5,15},{6,12},{7,13},{8,2},{9,3},... | collective-permute-start | bytes 55304 | tf_op jit(solution)/shard_map/ppermute | solution.py:155
  34.5 0.5 %collective-permute-start.18 = (bf16[72,128]{1,0:T(8,128)(2,1)S(1)}, bf16[72,128]{1,0:T(8,128)(2,1)S(1)}, u32[]{:S(2)}, u32[]{:S(2)}) collective-permute-start(bf16[72,128]{1,0:T(8,128)(2,1)S(1)} %get-tuple-element.72), channel_id=1, source_target_pairs={{0,2},{1,3},{2,0},{3,1},{4,6},{5,7},{6,4},{7,5},{8,10},{9,11},{10,... | collective-permute-start | bytes 55304 | tf_op jit(solution)/shard_map/ppermute | solution.py:155
  35.0 1.2 %collective-permute-start.19 = (bf16[72,128]{1,0:T(8,128)(2,1)S(1)}, bf16[72,128]{1,0:T(8,128)(2,1)S(1)}, u32[]{:S(2)}, u32[]{:S(2)}) collective-permute-start(bf16[72,128]{1,0:T(8,128)(2,1)S(1)} %get-tuple-element.73), channel_id=1, source_target_pairs={{0,8},{1,9},{2,10},{3,11},{4,12},{5,13},{6,14},{7,15},{8,0},{9,1},... | collective-permute-start | bytes 55304 | tf_op jit(solution)/shard_map/ppermute | solution.py:155
  36.2 0.0 collective-permute-done.12
  36.2 1.3 %collective-permute-done.17 = bf16[72,128]{1,0:T(8,128)(2,1)S(1)} collective-permute-done((bf16[72,128]{1,0:T(8,128)(2,1)S(1)}, bf16[72,128]{1,0:T(8,128)(2,1)S(1)}, u32[]{:S(2)}, u32[]{:S(2)}) %collective-permute-start.17) | collective-permute-done | bytes 18464 | tf_op jit(solution)/shard_map/ppermute | solution.py:155
  37.5 1.6 %collective-permute-done.18 = bf16[72,128]{1,0:T(8,128)(2,1)S(1)} collective-permute-done((bf16[72,128]{1,0:T(8,128)(2,1)S(1)}, bf16[72,128]{1,0:T(8,128)(2,1)S(1)}, u32[]{:S(2)}, u32[]{:S(2)}) %collective-permute-start.18) | collective-permute-done | bytes 18464 | tf_op jit(solution)/shard_map/ppermute | solution.py:155
  39.2 0.0 collective-permute-done.19
  39.2 0.1 collective-permute-start.20
  39.3 0.7 %pad_maximum_fusion.1 = bf16[2,256,256]{2,1,0:T(8,128)(2,1)} fusion(bf16[1,256,256]{2,1,0:T(8,128)(2,1)S(1)} %get-tuple-element.75, bf16[1,256,256]{2,1,0:T(8,128)(2,1)S(1)} %get-tuple-element.74), kind=kLoop, calls=%fused_computation.1 | loop fusion | flops 131072 | bytes 524288 | tf_op jit(solution)/shard_map/stack | solution.py:495
  40.0 0.5 %collective-permute-done.20.refs_1_ = f32[72,128]{1,0:T(8,128)S(1)} collective-permute-done((f32[72,128]{1,0:T(8,128)S(1)}, f32[72,128]{1,0:T(8,128)S(1)}, u32[]{:S(2)}, u32[]{:S(2)}) %collective-permute-start.20) | collective-permute-done | bytes 36896 | tf_op jit(solution)/shard_map/ppermute | solution.py:155
  40.5 0.6 %total.1 = f32[144,128]{1,0:T(8,128)} custom-call(f32[72,128]{1,0:T(8,128)S(1)} %convert_add_fusion.refs_0_, f32[72,128]{1,0:T(8,128)S(1)} %collective-permute-done.20.refs_1_), custom_call_target="tpu_custom_call" | custom-call | tf_op jit(solution)/shard_map/total/pallas_call | solution.py:406
  (12 shorter events, 0.2 us)
Async XLA Ops:
  0.6 17.0 %copy-start = (f32[360,4,256]{2,1,0:T(4,128)S(1)}, f32[360,4,256]{2,1,0:T(4,128)}, u32[]{:S(2)}) copy-start(f32[360,4,256]{2,1,0:T(4,128)} %param.7) | copy-start | bytes 4423684
  0.6 2.1 %collective-permute-start = (bf16[2,18432]{1,0:T(2,128)(2,1)}, bf16[2,18432]{1,0:T(2,128)(2,1)S(1)}, u32[]{:S(2)}, u32[]{:S(2)}) collective-permute-start(bf16[2,18432]{1,0:T(2,128)(2,1)} %refs_0_.1), channel_id=1, source_target_pairs={{0,4},{1,5},{2,6},{3,7},{4,0},{5,1},{6,2},{7,3},{8,12},{9,13},{10,... | collective-permute-start | bytes 221192 | tf_op jit(solution)/shard_map/ppermute | solution.py:155
  1.2 0.9 %copy-start.1 = (bf16[2,18432]{1,0:T(2,128)(2,1)S(1)}, bf16[2,18432]{1,0:T(2,128)(2,1)}, u32[]{:S(2)}) copy-start(bf16[2,18432]{1,0:T(2,128)(2,1)} %refs_0_.1) | copy-start | bytes 221188
  2.8 8.3 %collective-permute-start.1 = (bf16[2,72,128]{2,1,0:T(8,128)(2,1)S(1)}, bf16[2,72,128]{2,1,0:T(8,128)(2,1)S(1)}, u32[]{:S(2)}, u32[]{:S(2)}) collective-permute-start(bf16[2,72,128]{2,1,0:T(8,128)(2,1)S(1)} %piece.1.refs_0_), channel_id=1, source_target_pairs={{0,10},{1,11},{2,8},{3,9},{4,14},{5,15},{6,12},{7,13},{8,2},{9,3},... | collective-permute-start | bytes 110600 | tf_op jit(solution)/shard_map/ppermute | solution.py:155
  7.6 5.3 %collective-permute-start.2 = (bf16[2,72,128]{2,1,0:T(8,128)(2,1)S(1)}, bf16[2,72,128]{2,1,0:T(8,128)(2,1)S(1)}, u32[]{:S(2)}, u32[]{:S(2)}) collective-permute-start(bf16[2,72,128]{2,1,0:T(8,128)(2,1)S(1)} %piece.1.refs_0_), channel_id=1, source_target_pairs={{0,2},{1,3},{2,0},{3,1},{4,6},{5,7},{6,4},{7,5},{8,10},{9,11},{10,... | collective-permute-start | bytes 110600 | tf_op jit(solution)/shard_map/ppermute | solution.py:155
  7.9 4.9 %collective-permute-start.3 = (bf16[2,72,128]{2,1,0:T(8,128)(2,1)S(1)}, bf16[2,72,128]{2,1,0:T(8,128)(2,1)S(1)}, u32[]{:S(2)}, u32[]{:S(2)}) collective-permute-start(bf16[2,72,128]{2,1,0:T(8,128)(2,1)S(1)} %piece.1.refs_0_), channel_id=1, source_target_pairs={{0,8},{1,9},{2,10},{3,11},{4,12},{5,13},{6,14},{7,15},{8,0},{9,1},... | collective-permute-start | bytes 110600 | tf_op jit(solution)/shard_map/ppermute | solution.py:155
  9.3 7.3 %copy-start.2 = (bf16[1,64,8,256]{3,2,1,0:T(8,128)(2,1)S(1)}, bf16[1,64,8,256]{3,2,1,0:T(8,128)(2,1)}, u32[]{:S(2)}) copy-start(bf16[1,64,8,256]{3,2,1,0:T(8,128)(2,1)} %param.5) | copy-start | bytes 786436
  9.3 8.3 %copy-start.3 = (bf16[1,64,8,256]{3,2,1,0:T(8,128)(2,1)S(1)}, bf16[1,64,8,256]{3,2,1,0:T(8,128)(2,1)}, u32[]{:S(2)}) copy-start(bf16[1,64,8,256]{3,2,1,0:T(8,128)(2,1)} %param.9) | copy-start | bytes 786436
  9.3 8.2 %collective-permute-start.8 = (bf16[2,256,256]{2,1,0:T(8,128)(2,1)S(1)}, bf16[2,256,256]{2,1,0:T(8,128)(2,1)S(1)}, u32[]{:S(2)}, u32[]{:S(2)}) collective-permute-start(bf16[2,256,256]{2,1,0:T(8,128)(2,1)S(1)} %give.1), channel_id=1, source_target_pairs={{0,8},{1,9},{2,10},{3,11},{4,12},{5,13},{6,14},{7,15},{8,0},{9,1},... | collective-permute-start | bytes 786440 | tf_op jit(solution)/shard_map/ppermute | solution.py:155
  13.0 5.8 %collective-permute-start.4 = (bf16[2,200,128]{2,1,0:T(8,128)(2,1)S(1)}, bf16[2,200,128]{2,1,0:T(8,128)(2,1)S(1)}, u32[]{:S(2)}, u32[]{:S(2)}) collective-permute-start(bf16[2,200,128]{2,1,0:T(8,128)(2,1)S(1)} %group.1.refs_0_), channel_id=1, source_target_pairs={{0,17},{1,16},{2,19},{3,18},{4,21},{5,20},{6,23},{7,22},{8,25},{9,... | collective-permute-start | bytes 307208 | tf_op jit(solution)/shard_map/ppermute | solution.py:155
  15.1 4.7 %collective-permute-start.5 = (bf16[2,200,128]{2,1,0:T(8,128)(2,1)S(1)}, bf16[2,200,128]{2,1,0:T(8,128)(2,1)S(1)}, u32[]{:S(2)}, u32[]{:S(2)}) collective-permute-start(bf16[2,200,128]{2,1,0:T(8,128)(2,1)S(1)} %group.1.refs_0_), channel_id=1, source_target_pairs={{0,1},{1,0},{2,3},{3,2},{4,5},{5,4},{6,7},{7,6},{8,9},{9,8},{10,11... | collective-permute-start | bytes 307208 | tf_op jit(solution)/shard_map/ppermute | solution.py:155
  16.0 4.7 %collective-permute-start.6 = (bf16[2,200,128]{2,1,0:T(8,128)(2,1)S(1)}, bf16[2,200,128]{2,1,0:T(8,128)(2,1)S(1)}, u32[]{:S(2)}, u32[]{:S(2)}) collective-permute-start(bf16[2,200,128]{2,1,0:T(8,128)(2,1)S(1)} %group.1.refs_0_), channel_id=1, source_target_pairs={{0,16},{1,17},{2,18},{3,19},{4,20},{5,21},{6,22},{7,23},{8,24},{9,... | collective-permute-start | bytes 307208 | tf_op jit(solution)/shard_map/ppermute | solution.py:155
  16.5 4.1 %collective-permute-start.7 = (bf16[256,256]{1,0:T(8,128)(2,1)S(1)}, bf16[256,256]{1,0:T(8,128)(2,1)S(1)}, u32[]{:S(2)}, u32[]{:S(2)}) collective-permute-start(bf16[256,256]{1,0:T(8,128)(2,1)S(1)} %dynamic-slice_bitcast_fusion.1.refs_0_), channel_id=1, source_target_pairs={{0,4},{1,5},{2,6},{3,7},{4,0},{5,1},{6,2},{7,3},{8,12},{9,13},{10,... | collective-permute-start | bytes 393224 | tf_op jit(solution)/shard_map/ppermute | solution.py:155
  17.5 3.2 %collective-permute-start.9 = (bf16[256,256]{1,0:T(8,128)(2,1)S(1)}, bf16[256,256]{1,0:T(8,128)(2,1)S(1)}, u32[]{:S(2)}, u32[]{:S(2)}) collective-permute-start(bf16[256,256]{1,0:T(8,128)(2,1)S(1)} %slice_bitcast_fusion), channel_id=1, source_target_pairs={{0,4},{1,5},{2,6},{3,7},{4,0},{5,1},{6,2},{7,3},{8,12},{9,13},{10,... | collective-permute-start | bytes 393224 | tf_op jit(solution)/shard_map/ppermute | solution.py:155
  20.8 1.5 %collective-permute-start.10 = (bf16[768,128]{1,0:T(8,128)(2,1)S(1)}, bf16[768,128]{1,0:T(8,128)(2,1)S(1)}, u32[]{:S(2)}, u32[]{:S(2)}) collective-permute-start(bf16[768,128]{1,0:T(8,128)(2,1)S(1)} %get-tuple-element.55.refs_4_), channel_id=1, source_target_pairs={{0,4},{1,5},{2,6},{3,7},{4,0},{5,1},{6,2},{7,3},{8,12},{9,13},{10,... | collective-permute-start | bytes 589832 | tf_op jit(solution)/shard_map/ppermute | solution.py:155
  20.8 1.9 %collective-permute-start.11 = (bf16[768,128]{1,0:T(8,128)(2,1)S(1)}, bf16[768,128]{1,0:T(8,128)(2,1)S(1)}, u32[]{:S(2)}, u32[]{:S(2)}) collective-permute-start(bf16[768,128]{1,0:T(8,128)(2,1)S(1)} %get-tuple-element.60.refs_4_), channel_id=1, source_target_pairs={{0,4},{1,5},{2,6},{3,7},{4,0},{5,1},{6,2},{7,3},{8,12},{9,13},{10,... | collective-permute-start | bytes 589832 | tf_op jit(solution)/shard_map/ppermute | solution.py:155
  23.5 1.4 %collective-permute-start.13 = (bf16[512,128]{1,0:T(8,128)(2,1)S(1)}, bf16[512,128]{1,0:T(8,128)(2,1)S(1)}, u32[]{:S(2)}, u32[]{:S(2)}) collective-permute-start(bf16[512,128]{1,0:T(8,128)(2,1)S(1)} %get-tuple-element.65), channel_id=1, source_target_pairs={{0,4},{1,5},{2,6},{3,7},{4,0},{5,1},{6,2},{7,3},{8,12},{9,13},{10,... | collective-permute-start | bytes 393224 | tf_op jit(solution)/shard_map/ppermute | solution.py:155
  23.7 12.5 %collective-permute-start.12 = (bf16[256,256]{1,0:T(8,128)(2,1)S(1)}, bf16[256,256]{1,0:T(8,128)(2,1)S(1)}, u32[]{:S(2)}, u32[]{:S(2)}) collective-permute-start(bf16[256,256]{1,0:T(8,128)(2,1)S(1)} %get-tuple-element.62), channel_id=1, source_target_pairs={{0,8},{1,9},{2,10},{3,11},{4,12},{5,13},{6,14},{7,15},{8,0},{9,1},... | collective-permute-start | bytes 393224 | tf_op jit(solution)/shard_map/ppermute | solution.py:155
  25.4 5.5 %collective-permute-start.14 = (bf16[200,128]{1,0:T(8,128)(2,1)S(1)}, bf16[200,128]{1,0:T(8,128)(2,1)S(1)}, u32[]{:S(2)}, u32[]{:S(2)}) collective-permute-start(bf16[200,128]{1,0:T(8,128)(2,1)S(1)} %get-tuple-element.67), channel_id=1, source_target_pairs={{0,17},{1,16},{2,19},{3,18},{4,21},{5,20},{6,23},{7,22},{8,25},{9,... | collective-permute-start | bytes 153608 | tf_op jit(solution)/shard_map/ppermute | solution.py:155
  26.9 4.1 %collective-permute-start.15 = (bf16[200,128]{1,0:T(8,128)(2,1)S(1)}, bf16[200,128]{1,0:T(8,128)(2,1)S(1)}, u32[]{:S(2)}, u32[]{:S(2)}) collective-permute-start(bf16[200,128]{1,0:T(8,128)(2,1)S(1)} %get-tuple-element.68), channel_id=1, source_target_pairs={{0,1},{1,0},{2,3},{3,2},{4,5},{5,4},{6,7},{7,6},{8,9},{9,8},{10,11... | collective-permute-start | bytes 153608 | tf_op jit(solution)/shard_map/ppermute | solution.py:155
  27.5 4.1 %collective-permute-start.16 = (bf16[200,128]{1,0:T(8,128)(2,1)S(1)}, bf16[200,128]{1,0:T(8,128)(2,1)S(1)}, u32[]{:S(2)}, u32[]{:S(2)}) collective-permute-start(bf16[200,128]{1,0:T(8,128)(2,1)S(1)} %get-tuple-element.69), channel_id=1, source_target_pairs={{0,16},{1,17},{2,18},{3,19},{4,20},{5,21},{6,22},{7,23},{8,24},{9,... | collective-permute-start | bytes 153608 | tf_op jit(solution)/shard_map/ppermute | solution.py:155
  31.8 5.8 %collective-permute-start.17 = (bf16[72,128]{1,0:T(8,128)(2,1)S(1)}, bf16[72,128]{1,0:T(8,128)(2,1)S(1)}, u32[]{:S(2)}, u32[]{:S(2)}) collective-permute-start(bf16[72,128]{1,0:T(8,128)(2,1)S(1)} %get-tuple-element.71), channel_id=1, source_target_pairs={{0,10},{1,11},{2,8},{3,9},{4,14},{5,15},{6,12},{7,13},{8,2},{9,3},... | collective-permute-start | bytes 55304 | tf_op jit(solution)/shard_map/ppermute | solution.py:155
  34.5 4.7 %collective-permute-start.18 = (bf16[72,128]{1,0:T(8,128)(2,1)S(1)}, bf16[72,128]{1,0:T(8,128)(2,1)S(1)}, u32[]{:S(2)}, u32[]{:S(2)}) collective-permute-start(bf16[72,128]{1,0:T(8,128)(2,1)S(1)} %get-tuple-element.72), channel_id=1, source_target_pairs={{0,2},{1,3},{2,0},{3,1},{4,6},{5,7},{6,4},{7,5},{8,10},{9,11},{10,... | collective-permute-start | bytes 55304 | tf_op jit(solution)/shard_map/ppermute | solution.py:155
  35.0 4.2 %collective-permute-start.19 = (bf16[72,128]{1,0:T(8,128)(2,1)S(1)}, bf16[72,128]{1,0:T(8,128)(2,1)S(1)}, u32[]{:S(2)}, u32[]{:S(2)}) collective-permute-start(bf16[72,128]{1,0:T(8,128)(2,1)S(1)} %get-tuple-element.73), channel_id=1, source_target_pairs={{0,8},{1,9},{2,10},{3,11},{4,12},{5,13},{6,14},{7,15},{8,0},{9,1},... | collective-permute-start | bytes 55304 | tf_op jit(solution)/shard_map/ppermute | solution.py:155
  39.2 1.3 %collective-permute-start.20 = (f32[72,128]{1,0:T(8,128)S(1)}, f32[72,128]{1,0:T(8,128)S(1)}, u32[]{:S(2)}, u32[]{:S(2)}) collective-permute-start(f32[72,128]{1,0:T(8,128)S(1)} %convert_add_fusion.refs_0_), channel_id=1, source_target_pairs={{0,4},{1,5},{2,6},{3,7},{4,0},{5,1},{6,2},{7,3},{8,12},{9,13},{10,... | collective-permute-start | bytes 110600 | tf_op jit(solution)/shard_map/ppermute | solution.py:155
